TPU v7x, 512 devices: a whole 4x8x8 slice. The times are simulated.
512 devices in a mesh: mem: 16 (over y, core), space: 32 (over z, x).
Axes of the slice: x: 4, y: 8, z: 8, core: 2. Of those that a mesh axis runs over, the one named last changes fastest.
Arguments:
- ensemble: bfloat16 [16, 896, 2048], P('mem', 'space'), may hold values from -4 to 4
- decay_rate: float32 [896, 2048], P('space'), may hold values from 0 to 1, as said below
- innovation: float32 [896, 2048], P('space'), may hold values from -6 to 6
- obs_weight: float32 [896, 2048], P('space'), may hold values from 0.25 to 4
Outputs:
- control: float32 [16, 896, 2048], P('mem', 'space')
- increment: float32 [896, 2048], P('space')
Inputs may be any that keep to these rules, and one draw needn't show every extreme that they name: `decay_rate`: every entry lies strictly between 0 and 1.
All inputs are finite; a program needn't handle non-finite values.
Results may differ from a plain program's by a relative error of at most 0.0003.
Values sent between devices are 32-bit elements; how exact they have to be, the bound alone decides.
No kernel may reach another device: no remote copies, remote signals or barrier semaphores. Data moves between devices by JAX's collectives and lax.ppermute only.
A program may use at most 64 MiB of HBM per device.

v0:
```python
import jax
import jax.numpy as jnp
from jax import lax
from jax.sharding import PartitionSpec as P

ITERS = 2


def carried_in(value, axis, combine, identity, reverse):
    size, place = (lax.axis_size(axis), lax.axis_index(axis))
    everything = jax.tree.map(lambda part: lax.all_gather(part, axis), value)
    start = jax.tree.map(
        lambda part, zero: jnp.broadcast_to(jnp.asarray(zero, part.dtype), part.shape),
        value,
        identity,
    )

    def hop(k, before):
        at = size - 1 - k if reverse else k
        reached = at > place if reverse else at < place
        new = combine(before, jax.tree.map(lambda part: part[at], everything))
        return jax.tree.map(lambda a, b: jnp.where(reached, a, b), new, before)

    return lax.fori_loop(0, size, hop, start)


def combine(earlier, later):
    return (earlier[0] * later[0], later[0] * earlier[1] + later[1])


def advance(values, decay_rate, signal_amplitude):
    products, partial_value = lax.associative_scan(
        combine, (decay_rate[None], signal_amplitude[None] * values), axis=1
    )
    identity = (jnp.ones_like(decay_rate[0]), jnp.zeros_like(partial_value[:, 0]))
    _, entering = carried_in(
        (products[0, -1], partial_value[:, -1]), "space", combine, identity, False
    )
    return partial_value + products * entering[:, None, :]


def retreat(values, decay_rate, signal_amplitude):
    products, partial_value = lax.associative_scan(
        combine, (decay_rate[None], decay_rate[None] * values), axis=1, reverse=True
    )
    identity = (jnp.ones_like(decay_rate[0]), jnp.zeros_like(partial_value[:, 0]))
    _, entering = carried_in(
        (products[0, 0], partial_value[:, 0]), "space", combine, identity, True
    )
    carried = partial_value + products * entering[:, None, :]
    following = jnp.concatenate([carried[:, 1:], entering[:, None, :]], axis=1)
    return signal_amplitude[None] * (values + following)


def hessian(direction, ensemble, decay_rate, signal_amplitude, obs_weight):
    filtered = advance(direction, decay_rate, signal_amplitude)
    summand = jnp.sum(ensemble * filtered, axis=0)
    field_part = lax.psum(summand, "mem")
    weighted = obs_weight * field_part
    return (
        field_part,
        direction + retreat(ensemble * weighted[None], decay_rate, signal_amplitude),
    )


def squares(residual):
    return lax.psum(jnp.sum(residual * residual), ("mem", "space"))


def on_device(ensemble, decay_rate, innovation, obs_weight):
    signal_amplitude = jnp.sqrt((1.0 - decay_rate) * (1.0 + decay_rate))
    rhs = retreat(ensemble * (obs_weight * innovation)[None], decay_rate, signal_amplitude)
    control = jnp.zeros_like(rhs)
    increment = jnp.float32(0.0)
    residual = rhs
    direction = rhs
    norm_now = squares(residual)
    for repeat in range(ITERS):
        field_part, hessian_times_direction = hessian(
            direction, ensemble, decay_rate, signal_amplitude, obs_weight
        )
        step_size = norm_now / lax.psum(
            jnp.sum(direction * hessian_times_direction), ("mem", "space")
        )
        control = control + step_size * direction
        increment = increment + step_size * field_part
        residual = residual - step_size * hessian_times_direction
        if repeat + 1 < ITERS:
            norm_next = squares(residual)
            direction = residual + norm_next / norm_now * direction
            norm_now = norm_next
    return (control, increment)


def solution(mesh):
    in_specs = (P("mem", "space", None), P("space", None), P("space", None), P("space", None))
    out_specs = (P("mem", "space", None), P("space", None))
    return jax.shard_map(
        on_device, mesh=mesh, in_specs=in_specs, out_specs=out_specs, check_vma=False
    )
```

profile of v0, /device:TPU:1, one launch (start us, length us, event | category | flops | bytes accessed | tf_op | source)
XLA Modules:
  0.0 985.3 jit_solution(6393310146459393171)
XLA Ops:
  7.2 5.9 reverse.19
  13.2 1.0 fusion.17
  19.1 43.8 %all_gather.25 = f32[32,1,2048]{2,1,0:T(1,128)S(1)} all-gather(f32[1,1,2048]{2,1,0:T(1,128)S(1)} %slice_add_fusion.16), channel_id=1, replica_groups=mesh['mem'=16,'space'=32] {'space'}, dimensions={0}, use_global_device_ids=true | all-gather | bytes 270336 | tf_op jit(solution)/shard_map/all_gather | solution.py:11
  63.0 36.0 %all-gather = f32[32,1,2048]{2,1,0:T(1,128)S(1)} all-gather(f32[1,1,2048]{2,1,0:T(1,128)S(1)} %slice_add_fusion.17), channel_id=2, replica_groups=mesh['mem'=16,'space'=32] {'space'}, dimensions={0}, use_global_device_ids=true | all-gather | bytes 270336 | tf_op jit(solution)/shard_map/all_gather | solution.py:11
  99.1 1.9 while.76
  105.8 39.1 %all_gather.27 = f32[32,1,2048]{2,1,0:T(1,128)} all-gather(f32[1,1,2048]{2,1,0:T(1,128)S(1)} %slice_add_fusion.12), channel_id=1, replica_groups=mesh['mem'=16,'space'=32] {'space'}, dimensions={0}, use_global_device_ids=true | all-gather | bytes 270336 | tf_op jit(solution)/shard_map/all_gather | solution.py:11
  145.1 35.3 %all-gather.1 = f32[32,1,2048]{2,1,0:T(1,128)S(1)} all-gather(f32[1,1,2048]{2,1,0:T(1,128)S(1)} %slice_add_fusion.13), channel_id=3, replica_groups=mesh['mem'=16,'space'=32] {'space'}, dimensions={0}, use_global_device_ids=true | all-gather | bytes 270336 | tf_op jit(solution)/shard_map/all_gather | solution.py:11
  181.1 28.9 %while.77 = (s32[]{:T(128)}, f32[1,2048]{1,0:T(1,128)S(1)}, s32[]{:T(128)}, f32[32,2048]{1,0:T(8,128)}, f32[32,1,2048]{2,1,0:T(1,128)}, /*index=5*/s32[]{:T(128)}, s32[]{:T(128)}) while((s32[]{:T(128)}, f32[1,2048]{1,0:T(1,128)S(1)}, s32[]{:T(128)}, f32[32,2048]{1,0:T(8,128)}, f32[32,1,2048]{2,1,0:T(1,128)}, /*index=5*/s32[]{:T(128)}, ...), condition=%wide.region_5.6_spmd.clone, body=%wide.region_4.5_spmd.clone.sunk | while | flops 8196 | bytes 32869 | solution.py:24
  182.0 0.9 broadcast_select_fusion.16
  182.9 0.9 broadcast_select_fusion.16
  183.8 0.9 broadcast_select_fusion.16
  184.8 0.9 broadcast_select_fusion.16
  185.7 0.9 broadcast_select_fusion.16
  186.6 0.9 broadcast_select_fusion.16
  187.5 0.9 broadcast_select_fusion.16
  194.7 0.9 broadcast_select_fusion.16
  200.1 0.9 broadcast_select_fusion.16
  210.9 158.9 %all-reduce.60.cloned.1.call-done = f32[28,2048]{1,0:T(8,128)} async-done(((f32[28,2048]{1,0:T(8,128)}), f32[28,2048]{1,0:T(8,128)}) %all-reduce.60.cloned.1.call-update) | async-done | bytes 229392 | tf_op jit(solution)/shard_map/psum | solution.py:58
  369.8 1.0 fusion.18
  376.9 38.1 %all_gather.28 = f32[32,1,2048]{2,1,0:T(1,128)S(1)} all-gather(f32[1,1,2048]{2,1,0:T(1,128)S(1)} %slice_add_fusion.9), channel_id=1, replica_groups=mesh['mem'=16,'space'=32] {'space'}, dimensions={0}, use_global_device_ids=true | all-gather | bytes 270336 | tf_op jit(solution)/shard_map/all_gather | solution.py:11
  415.0 1.9 while.78
  418.7 107.2 %all-reduce.56 = (f32[]{:T(128)}, f32[]{:T(128)}) all-reduce(f32[]{:T(128)} %get-tuple-element.686, f32[]{:T(128)} %get-tuple-element.685), channel_id=1, replica_groups=mesh['mem'=16,'space'=32] {'mem','space'}, use_global_device_ids=true, to_apply=%region_3.4 | all-reduce | flops 2 | bytes 16 | tf_op jit(solution)/shard_map/psum | solution.py:67
  527.9 95.9 %psum.45 = f32[]{:T(128)} all-reduce(f32[]{:T(128)} %multiply_reduce_fusion), channel_id=1, replica_groups=mesh['mem'=16,'space'=32] {'mem','space'}, use_global_device_ids=true, to_apply=%region_12.13 | all-reduce | flops 1 | bytes 8 | tf_op jit(solution)/shard_map/psum | solution.py:67
  626.0 0.9 multiply_add_fusion.4
  631.8 34.9 %all_gather.29 = f32[32,1,2048]{2,1,0:T(1,128)S(1)} all-gather(f32[1,1,2048]{2,1,0:T(1,128)S(1)} %slice_add_fusion.6), channel_id=1, replica_groups=mesh['mem'=16,'space'=32] {'space'}, dimensions={0}, use_global_device_ids=true | all-gather | bytes 270336 | tf_op jit(solution)/shard_map/all_gather | solution.py:11
  666.7 28.4 %while.79 = (s32[]{:T(128)}, f32[1,2048]{1,0:T(1,128)S(1)}, s32[]{:T(128)}, f32[32,2048]{1,0:T(8,128)}, f32[32,1,2048]{2,1,0:T(1,128)S(1)}, /*index=5*/s32[]{:T(128)}, s32[]{:T(128)}) while((s32[]{:T(128)}, f32[1,2048]{1,0:T(1,128)S(1)}, s32[]{:T(128)}, f32[32,2048]{1,0:T(8,128)}, f32[32,1,2048]{2,1,0:T(1,128)S(1)}, ...), condition=%wide.region_14.15_spmd.clone, body=%wide.region_13.14_spmd.clone.sunk | while | flops 8196 | bytes 32869 | solution.py:24
  695.9 123.5 %all-reduce.62.cloned.1.call-done = f32[28,2048]{1,0:T(8,128)} async-done(((f32[28,2048]{1,0:T(8,128)}), f32[28,2048]{1,0:T(8,128)}) %all-reduce.62.cloned.1.call-update) | async-done | bytes 229392 | tf_op jit(solution)/shard_map/psum | solution.py:58
  819.4 1.0 fusion.19
  826.5 38.1 %all_gather.30 = f32[32,1,2048]{2,1,0:T(1,128)S(1)} all-gather(f32[1,1,2048]{2,1,0:T(1,128)S(1)} %slice_add_fusion.3), channel_id=1, replica_groups=mesh['mem'=16,'space'=32] {'space'}, dimensions={0}, use_global_device_ids=true | all-gather | bytes 270336 | tf_op jit(solution)/shard_map/all_gather | solution.py:11
  864.6 1.9 while.80
  868.3 107.1 %psum.47 = f32[]{:T(128)} all-reduce(f32[]{:T(128)} %fusion), channel_id=1, replica_groups=mesh['mem'=16,'space'=32] {'mem','space'}, use_global_device_ids=true, to_apply=%region_19.20 | all-reduce | flops 1 | bytes 8 | tf_op jit(solution)/shard_map/psum | solution.py:82
  976.8 0.9 copy.7
  (461 shorter events, 84.9 us)
Async XLA Ops:
  7.2 6.0 copy-start
  7.2 6.0 copy-start.1
  7.2 362.7 %all-reduce.60.cloned.1.call-start = ((), (), s32[]{:S(2)}) async-start(), calls=%async_computation | async-start | bytes 524288 | tf_op jit(solution)/shard_map/psum | solution.py:58
  15.5 0.6 copy-start.9
  15.6 1.3 copy-start.6
  16.2 0.6 copy-start.19
  101.0 0.9 copy-start.2
  101.0 1.0 copy-start.5
  102.7 1.0 copy-start.17
  102.8 1.7 copy-start.15
  103.7 0.6 copy-start.22
  105.0 0.7 copy-start.24
  210.9 608.6 %all-reduce.62.cloned.1.call-start = ((), (), s32[]{:S(2)}) async-start(), calls=%async_computation.1 | async-start | bytes 524288 | tf_op jit(solution)/shard_map/psum | solution.py:58
  371.9 0.6 copy-start.14
  372.5 0.8 copy-start.10
  373.3 0.8 copy-start.20
  374.1 0.8 copy-start.7
  374.9 0.7 slice-start.2
  416.9 1.0 copy-start.3
  627.0 0.6 copy-start.12
  627.7 0.8 copy-start.18
  628.4 0.8 copy-start.23
  629.2 0.8 copy-start.16
  630.0 0.7 slice-start
  630.8 0.7 copy-start.25
  821.5 0.6 copy-start.13
  822.2 0.8 copy-start.11
  822.9 0.8 copy-start.21
  823.7 0.8 copy-start.8
  824.5 0.7 slice-start.1
  866.6 1.0 copy-start.4
Sparse Core Ops, SparseCore 0:
  211.0 158.8 all-reduce.59
  696.0 123.3 all-reduce.61
where the time goes:
time: 990 us; the launch traced here: 985 us
  blocking collectives  576 us (58%)
  waiting for transfers between devices  282 us (28%)
  other arithmetic  70.1 us (7%)
  local copies, waits for them, and re-layouts  33.4 us (3%)
  between operations  19.8 us (2%)
    psum x2, waiting for transfers between devices, hessian(): field_part = lax.psum(summand, 'mem')  282 us
    all_gather x7, blocking collectives, carried_in(): everything = jax.tree.map(lambda part: lax.all_gather(part, axis), value)  265 us
    psum x2, blocking collectives, squares(): return lax.psum(jnp.sum(residual * residual), ('mem', 'space'))  203 us
    psum x1, blocking collectives, on_device(): lax.psum(jnp.sum(direction * hessian_times_direction), ('mem', 'space'))  107 us
    select_n x160, other arithmetic, hop(): return jax.tree.map(lambda a, b: jnp.where(reached, a, b), new, before)  59.2 us
  transfers between devices with their start and end apart: 2, of which 2 were waited for; matrix products, arithmetic and copies ran while one was open for 0% of the time, Pallas kernels for 0%

commit v1 on v0

v1 whole, which is shorter than its diff:
```python
import jax
import jax.numpy as jnp
from jax import lax
from jax.experimental import pallas as pl
from jax.experimental.pallas import tpu as pltpu
from jax.sharding import PartitionSpec as P

MEMBERS, TILES, COLS, LINES = 16, 32, 28, 4
DEVICES = MEMBERS * TILES
ROWS = 32
LANES = 128
BLOCKS = DEVICES // LANES
VMEM = pl.BlockSpec(memory_space=pltpu.VMEM)


def lane_block(line, block):
    start = line * DEVICES + block * LANES
    return slice(start, start + LANES)


def pack(place, ensemble_ref, decay_ref, innovation_ref, weight_ref, out_ref, rows_ref):
    rows_ref[:COLS, :] = ensemble_ref[0].astype(jnp.float32) * jnp.sqrt(weight_ref[...])
    quarter = lax.rem(place, 8)
    start = pl.multiple_of(8 * jnp.minimum(lax.div(quarter, 2), 2), 8)

    def four(ref):
        eight = ref[pl.ds(start, 8), :]
        inner = jnp.where(lax.rem(quarter, 2) == 0, eight[:4], eight[4:])
        return jnp.where(quarter >= 6, ref[COLS - 4 :, :], inner)

    scaled = jnp.sqrt(four(weight_ref)) * four(innovation_ref)
    rows_ref[COLS:, :] = jnp.where(place < 8, four(decay_ref), scaled)
    for block in range(BLOCKS):
        piece = jnp.concatenate([rows_ref[:, lane_block(line, block)] for line in range(LINES)], axis=0)
        out_ref[block * LANES : (block + 1) * LANES, :] = piece.T


def spread(piece, lane_group):
    turned = [piece] + [pltpu.roll(piece, 32 * k, 1) for k in (1, 2, 3)]
    out = []
    for source in range(4):
        value = turned[(3 - source) % 4]
        for group in (2, 1, 0):
            value = jnp.where(lane_group == group, turned[(group - source) % 4], value)
        out.append(value)
    return out


def own_lines(in_ref, out_ref, rows_ref, fields_ref, state_ref, first_ref, sums_ref):
    for block in range(BLOCKS):
        piece = slice(block * LANES, (block + 1) * LANES)
        rows_ref[piece, :] = in_ref[piece, :].T

    lane = lax.broadcasted_iota(jnp.int32, (8, LANES), 1)
    sub = lax.broadcasted_iota(jnp.int32, (8, LANES), 0)
    tile, lane_group = lane % TILES, lane // TILES
    low = sub < 4

    def column(c):
        value = rows_ref[pl.ds(c, 16, stride=ROWS), :]
        return value[:8], value[8:]

    RATE, SQUARED, AFTER, UPTO, INNOV, Z0, Z1 = range(7)

    def field(kind, c):
        return fields_ref[kind, c]

    for j in range(4):
        for kind, value in zip((RATE, INNOV), column(COLS + j)):
            other = pltpu.roll(value, 4, 0)
            for half, both in enumerate((jnp.where(low, value, other), jnp.where(low, other, value))):
                for source, copied in enumerate(spread(both, lane_group)):
                    c = 16 * half + 4 * source + j
                    if c < COLS:
                        fields_ref[kind, c] = copied

    one = jnp.ones((8, LANES), jnp.float32)
    upto, after = one, one
    for c in range(COLS):
        rate = field(RATE, c)
        fields_ref[SQUARED, c] = (1.0 - rate) * (1.0 + rate)
        upto = upto * rate
        fields_ref[UPTO, c] = upto
        fields_ref[AFTER, COLS - 1 - c] = after
        after = after * field(RATE, COLS - 1 - c)

    steps = (1, 2, 4, 8, 16)
    back, forth = [], []
    to_left, to_right = upto, upto
    for k in steps:
        back.append(jnp.where(tile < TILES - k, to_left, 0.0))
        to_left = back[-1] * pltpu.roll(to_left, LANES - k, 1)
        forth.append(jnp.where(tile >= k, to_right, 0.0))
        to_right = forth[-1] * pltpu.roll(to_right, k, 1)

    def entering(values, backward):
        out = []
        for value in values:
            for k, factor in zip(steps, back if backward else forth):
                value = value + factor * pltpu.roll(value, LANES - k if backward else k, 1)
            if backward:
                out.append(jnp.where(tile < TILES - 1, pltpu.roll(value, LANES - 1, 1), 0.0))
            else:
                out.append(jnp.where(tile >= 1, pltpu.roll(value, 1, 1), 0.0))
        return out

    def apply(source, target, on_state):
        zero = jnp.zeros((8, LANES), jnp.float32)
        carry = [zero, zero]
        for c in reversed(range(COLS)):
            rate, weight = field(RATE, c), field(source, c)
            for i, member in enumerate(column(c)):
                summed = member * weight + carry[i]
                state_ref[c, i] = summed
                carry[i] = rate * summed
        from_right = entering(carry, True)
        state = [zero, zero]
        for c in range(COLS):
            rate, squared, after = field(RATE, c), field(SQUARED, c), field(AFTER, c)
            for i in range(2):
                summed = state_ref[c, i] + after * from_right[i]
                driven = squared * summed
                on_state(c, i, summed, driven)
                state[i] = rate * state[i] + driven
                state_ref[c, i] = state[i]
        from_left = entering(state, False)
        for c in range(COLS):
            upto, members = field(UPTO, c), column(c)
            total = sum(members[i] * (state_ref[c, i] + upto * from_left[i]) for i in range(2))
            total = total + pltpu.roll(total, 4, 0)
            total = total + pltpu.roll(total, 64, 1)
            total = total + pltpu.roll(total, 32, 1)
            fields_ref[target, c] = total
        return from_right

    def whole(value):
        return jnp.sum(jnp.sum(value, axis=0, keepdims=True), axis=1, keepdims=True)

    squares = [jnp.zeros((8, LANES), jnp.float32)] * 2

    def keep(c, i, summed, driven):
        first_ref[c, i] = summed
        squares[i] = squares[i] + summed * driven

    right0 = apply(INNOV, Z0, keep)
    alpha = whole(squares[0] + squares[1])
    beta = jnp.zeros((8, LANES), jnp.float32)
    for c in range(COLS):
        beta = beta + field(Z0, c) * field(Z0, c)
    beta = 0.125 * whole(beta)
    ratio = jnp.where(alpha > 0.0, beta / jnp.where(alpha > 0.0, alpha, 1.0), 0.0)
    ratio = jnp.broadcast_to(ratio, (8, LANES))

    rest = [jnp.zeros((8, LANES), jnp.float32)] * 2

    def orthogonal(c, i, summed, driven):
        part = summed - ratio * first_ref[c, i]
        rest[i] = rest[i] + field(SQUARED, c) * part * part

    right1 = apply(Z0, Z1, orthogonal)
    kappa = whole(rest[0] + rest[1])
    energy = jnp.zeros((8, LANES), jnp.float32)
    cross = energy
    for c in range(COLS):
        part = field(Z1, c) - ratio * field(Z0, c)
        energy = energy + part * part
        cross = cross + part * field(Z0, c)
    energy, cross = 0.125 * whole(energy), 0.125 * whole(cross)

    def put(row, values):
        rows_ref[pl.ds(row, 16, stride=ROWS), :] = jnp.concatenate(values, axis=0)

    line = sub % 4
    scalars = jnp.where(line == 0, alpha, jnp.where(line == 1, beta, jnp.where(line == 2, kappa, energy)))
    others = jnp.where(line == 0, cross, 0.0)
    for c in range(COLS):
        put(c, [field(Z0, c)] * 2)
    put(COLS, right0)
    put(COLS + 1, right1)
    put(COLS + 2, [scalars] * 2)
    put(COLS + 3, [others] * 2)
    for c in range(COLS):
        sums_ref[pl.ds(c, 4, stride=ROWS), :] = field(Z1, c)[:4]
    for r in range(COLS, ROWS):
        sums_ref[pl.ds(r, 4, stride=ROWS), :] = jnp.zeros((4, LANES), jnp.float32)
    second = sums_ref[...].T
    for block in range(BLOCKS):
        first = rows_ref[block * LANES : (block + 1) * LANES, :].T
        out_ref[pl.ds(2 * block * LANES, LANES, stride=2), :] = first
        out_ref[pl.ds(2 * block * LANES + 1, LANES, stride=2), :] = second


def finish(in_ref, ensemble_ref, decay_ref, innovation_ref, weight_ref, control_ref, increment_ref,
           first_ref, second_ref, driven_ref, rate_ref):
    for block in range(BLOCKS):
        for half, ref in enumerate((first_ref, second_ref)):
            piece = in_ref[pl.ds(2 * block * LANES + half, LANES, stride=2), :].T
            for line in range(LINES):
                ref[:, lane_block(line, block)] = piece[line * ROWS : (line + 1) * ROWS]

    def scalar(row, line):
        return first_ref[row : row + 1, line * DEVICES : (line + 1) * DEVICES]

    def whole(value):
        return jnp.sum(value, axis=1, keepdims=True)

    alphas, betas, kappas, energies = (scalar(COLS + 2, line) for line in range(LINES))
    crosses = scalar(COLS + 3, 0)
    alpha, beta = whole(alphas), whole(betas)
    ratio = beta / alpha
    shift = jnp.where(alphas > 0.0, betas / jnp.where(alphas > 0.0, alphas, 1.0), 0.0) - ratio
    kappa = whole(kappas + alphas * shift * shift)
    energy = whole(energies + shift * (2.0 * crosses + shift * betas))
    step = alpha / (alpha + beta)
    curvature = kappa + energy - step * kappa * (kappa / alpha)
    back = jnp.where(curvature > 0.0, step * kappa / jnp.where(curvature > 0.0, curvature, 1.0), 0.0)
    ahead = step + back * (ratio + step * (kappa / alpha))

    root = jnp.sqrt(weight_ref[...])
    z0 = first_ref[:COLS, :]
    increment_ref[...] = (ahead * z0 - back * second_ref[:COLS, :]) / root
    scaled = root * (ahead * (root * innovation_ref[...]) - back * z0)
    driven = ensemble_ref[0].astype(jnp.float32) * scaled
    groups = LINES * DEVICES // LANES
    carry = []
    for g in range(groups):
        part = slice(g * LANES, (g + 1) * LANES)
        driven_ref[pl.ds(g, COLS, stride=groups), :] = driven[:, part]
        rate_ref[pl.ds(g, COLS, stride=groups), :] = decay_ref[:, part]
        carry.append(ahead * first_ref[COLS : COLS + 1, part] - back * first_ref[COLS + 1 : COLS + 2, part])
    carry = jnp.concatenate(carry, axis=0)
    for c in reversed(range(COLS)):
        part = slice(c * groups, (c + 1) * groups)
        rate = rate_ref[part, :]
        summed = driven_ref[part, :] + carry
        carry = rate * summed
        driven_ref[part, :] = jnp.sqrt((1.0 - rate) * (1.0 + rate)) * summed
    for g in range(groups):
        control_ref[0, :, g * LANES : (g + 1) * LANES] = driven_ref[pl.ds(g, COLS, stride=groups), :]


def shape(*dims):
    return jax.ShapeDtypeStruct(dims, jnp.float32)


def scratch(*dims):
    return pltpu.VMEM(dims, jnp.float32)


def call(kernel, out_shape, scratch_shapes, inputs):
    one = not isinstance(out_shape, tuple)
    return pl.pallas_call(
        kernel,
        out_shape=out_shape,
        in_specs=[VMEM] * inputs,
        out_specs=VMEM if one else (VMEM,) * len(out_shape),
        scratch_shapes=scratch_shapes,
        compiler_params=pltpu.CompilerParams(vmem_limit_bytes=32 * 1024 * 1024),
    )


def pack_here(*refs):
    pack(lax.axis_index("mem"), *refs)


def own_call(received):
    return call(
        own_lines,
        shape(2 * DEVICES, LANES),
        [
            scratch(DEVICES, LANES),
            scratch(7, COLS, 8, LANES),
            scratch(COLS, 2, 8, LANES),
            scratch(COLS, 2, 8, LANES),
            scratch(LANES, LANES),
        ],
        1,
    )(received)


def finish_call(received, *args):
    width = LINES * DEVICES
    return call(
        finish,
        (shape(1, COLS, width), shape(COLS, width)),
        [scratch(ROWS, width), scratch(ROWS, width)] + [scratch(COLS * width // LANES, LANES)] * 2,
        5,
    )(received, *args)


def on_device(ensemble, decay_rate, innovation, obs_weight):
    args = (ensemble, decay_rate, innovation, obs_weight)
    axes = ("mem", "space")
    sent = call(pack_here, shape(DEVICES, LANES), [scratch(ROWS, LINES * DEVICES)], 4)(*args)
    received = lax.all_to_all(sent, axes, 0, 0, tiled=True)
    results = own_call(received).reshape(DEVICES, 2, LANES)
    returned = lax.all_to_all(results, axes, 0, 0, tiled=True)
    return finish_call(returned.reshape(2 * DEVICES, LANES), *args)


def solution(mesh):
    in_specs = (P("mem", "space", None), P("space", None), P("space", None), P("space", None))
    out_specs = (P("mem", "space", None), P("space", None))
    return jax.shard_map(
        on_device, mesh=mesh, in_specs=in_specs, out_specs=out_specs, check_vma=False
    )
```

time: 990 us -> 81.2 us (0.08)
  blocking collectives: 576 us -> 70.6 us
  waiting for transfers between devices: 282 us -> 0 us
  other arithmetic: 70.1 us -> 0 us
  local copies, waits for them, and re-layouts: 33.4 us -> 4.7 us
  between operations: 19.8 us -> 0.69 us
    psum x3 -> x0, blocking collectives: 310 us -> none  [the longest x2 203 us: squares(): return lax.psum(jnp.sum(residual * residual), ('mem', 'space'))]
    psum x2 -> x0, waiting for transfers between devices: 282 us -> none  [hessian(): field_part = lax.psum(summand, 'mem')]
    all_gather x7 -> x0, blocking collectives: 265 us -> none  [carried_in(): everything = jax.tree.map(lambda part: lax.all_gather(part, axis), value)]
    all_to_all x0 -> x2, blocking collectives: none -> 70.6 us  [the longest x1 39.3 us: on_device(): received = lax.all_to_all(sent, axes, 0, 0, tiled=True)]
    select_n x160 -> x0, other arithmetic: 59.2 us -> none  [hop(): return jax.tree.map(lambda a, b: jnp.where(reached, a, b), new, before)]
    unnamed x55 -> x16, local copies, waits for them, and re-layouts: 14.5 us -> 3.77 us
  transfers between devices with their start and end apart: 2 -> 0, of which waited for: 2 -> 0; matrix products, arithmetic and copies ran while one was open for 0% -> 0% of each run, Pallas kernels for 0% -> 0%
where the time goes in v1:
time: 81.2 us; the launch traced here: 80.9 us
  blocking collectives  70.6 us (87%)
  Pallas kernels  4.94 us (6%)
  local copies, waits for them, and re-layouts  4.7 us (6%)
    all_to_all x1, blocking collectives, on_device(): received = lax.all_to_all(sent, axes, 0, 0, tiled=True)  39.3 us
    all_to_all x1, blocking collectives, on_device(): returned = lax.all_to_all(results, axes, 0, 0, tiled=True)  31.3 us
    unnamed x16, local copies, waits for them, and re-layouts  3.77 us
    pallas_call x1, Pallas kernels, own_call(): call(own_lines, shape(2 * DEVICES, LANES), [scratch(DEVICES, LANES), scra...  3.32 us

profile of v1, /device:TPU:1, one launch (start us, length us, event | category | flops | bytes accessed | tf_op | source)
XLA Modules:
  0.0 80.9 jit_solution(4080454984164167215)
XLA Ops:
  0.6 0.0 copy-start
  0.6 0.9 %copy-done = f32[28,2048]{1,0:T(8,128)S(1)} copy-done((f32[28,2048]{1,0:T(8,128)S(1)}, f32[28,2048]{1,0:T(8,128)}, u32[]{:S(2)}) %copy-start) | copy-done | bytes 229400
  1.6 0.0 copy-start.2
  1.6 0.9 %copy-done.2 = f32[28,2048]{1,0:T(8,128)S(1)} copy-done((f32[28,2048]{1,0:T(8,128)S(1)}, f32[28,2048]{1,0:T(8,128)}, u32[]{:S(2)}) %copy-start.2) | copy-done | bytes 229400
  2.5 0.0 copy-start.4
  2.5 0.9 %copy-done.4 = f32[28,2048]{1,0:T(8,128)S(1)} copy-done((f32[28,2048]{1,0:T(8,128)S(1)}, f32[28,2048]{1,0:T(8,128)}, u32[]{:S(2)}) %copy-start.4) | copy-done | bytes 229400
  3.5 0.0 copy-start.6
  3.5 0.9 %copy-done.6 = bf16[1,28,2048]{2,1,0:T(8,128)(2,1)S(1)} copy-done((bf16[1,28,2048]{2,1,0:T(8,128)(2,1)S(1)}, bf16[1,28,2048]{2,1,0:T(8,128)(2,1)}, u32[]{:S(2)}) %copy-start.6) | copy-done | bytes 114712
  4.4 0.2 shard_map.59
  4.6 39.3 %all_to_all.16 = f32[512,1,128]{2,1,0:T(1,128)S(1)} all-to-all(f32[512,1,128]{2,1,0:T(1,128)S(1)} %bitcast.9), channel_id=1, replica_groups=mesh['mem'=16,'space'=32] {'mem','space'}, dimensions={0} | all-to-all | bytes 524288 | tf_op jit(solution)/shard_map/all_to_all | solution.py:295
  43.9 3.3 %shard_map.60 = f32[1024,128]{1,0:T(8,128)S(1)} custom-call(f32[512,128]{1,0:T(8,128)S(1)} %bitcast.8), custom_call_target="tpu_custom_call" | custom-call | tf_op jit(solution)/shard_map/pallas_call | solution.py:267
  47.2 0.0 copy-start.1
  47.2 0.0 copy-start.3
  47.2 0.0 copy-start.5
  47.2 0.0 copy-start.7
  47.3 31.3 %all_to_all.17 = f32[512,2,128]{2,1,0:T(2,128)S(1)} all-to-all(f32[512,2,128]{2,1,0:T(2,128)S(1)} %bitcast.6), channel_id=1, replica_groups=mesh['mem'=16,'space'=32] {'mem','space'}, dimensions={0} | all-to-all | bytes 1048576 | tf_op jit(solution)/shard_map/all_to_all | solution.py:297
  78.6 0.0 copy-done.1
  78.6 0.0 copy-done.3
  78.6 0.0 copy-done.5
  78.6 0.0 copy-done.7
  78.6 1.4 %shard_map.61 = (f32[1,28,2048]{2,1,0:T(8,128)S(1)}, f32[28,2048]{1,0:T(8,128)}) custom-call(f32[1024,128]{1,0:T(8,128)S(1)} %bitcast.7, bf16[1,28,2048]{2,1,0:T(8,128)(2,1)S(1)} %copy-done.7, f32[28,2048]{1,0:T(8,128)S(1)} %copy-done.1, f32[28,2048]{1,0:T(8,128)S(1)} %copy-done.3, f32[28,2048]{1,0:T(8,128)S(1)} %copy-done.5), custom_call_target="tpu_custom_call" | custom-call | tf_op jit(solution)/shard_map/pallas_call | solution.py:283
  80.0 0.9 %copy.8 = f32[1,28,2048]{2,0,1:T(1,128)} copy(f32[1,28,2048]{2,1,0:T(8,128)S(1)} %get-tuple-element.4) | data formatting | bytes 458752 | tf_op jit(solution)/shard_map/pallas_call | solution.py:283
Async XLA Ops:
  0.6 1.0 %copy-start = (f32[28,2048]{1,0:T(8,128)S(1)}, f32[28,2048]{1,0:T(8,128)}, u32[]{:S(2)}) copy-start(f32[28,2048]{1,0:T(8,128)} %decay_ref.1) | copy-start | bytes 688132
  1.6 0.9 %copy-start.2 = (f32[28,2048]{1,0:T(8,128)S(1)}, f32[28,2048]{1,0:T(8,128)}, u32[]{:S(2)}) copy-start(f32[28,2048]{1,0:T(8,128)} %innovation_ref.1) | copy-start | bytes 688132
  2.5 0.9 %copy-start.4 = (f32[28,2048]{1,0:T(8,128)S(1)}, f32[28,2048]{1,0:T(8,128)}, u32[]{:S(2)}) copy-start(f32[28,2048]{1,0:T(8,128)} %weight_ref.1) | copy-start | bytes 688132
  3.5 0.9 %copy-start.6 = (bf16[1,28,2048]{2,1,0:T(8,128)(2,1)S(1)}, bf16[1,28,2048]{2,1,0:T(8,128)(2,1)}, u32[]{:S(2)}) copy-start(bf16[1,28,2048]{2,1,0:T(8,128)(2,1)} %ensemble_ref.1) | copy-start | bytes 344068
  47.2 31.4 %copy-start.1 = (f32[28,2048]{1,0:T(8,128)S(1)}, f32[28,2048]{1,0:T(8,128)}, u32[]{:S(2)}) copy-start(f32[28,2048]{1,0:T(8,128)} %decay_ref.1) | copy-start | bytes 688132
  47.2 31.4 %copy-start.3 = (f32[28,2048]{1,0:T(8,128)S(1)}, f32[28,2048]{1,0:T(8,128)}, u32[]{:S(2)}) copy-start(f32[28,2048]{1,0:T(8,128)} %innovation_ref.1) | copy-start | bytes 688132
  47.2 31.3 %copy-start.5 = (f32[28,2048]{1,0:T(8,128)S(1)}, f32[28,2048]{1,0:T(8,128)}, u32[]{:S(2)}) copy-start(f32[28,2048]{1,0:T(8,128)} %weight_ref.1) | copy-start | bytes 688132
  47.2 31.3 %copy-start.7 = (bf16[1,28,2048]{2,1,0:T(8,128)(2,1)S(1)}, bf16[1,28,2048]{2,1,0:T(8,128)(2,1)}, u32[]{:S(2)}) copy-start(bf16[1,28,2048]{2,1,0:T(8,128)(2,1)} %ensemble_ref.1) | copy-start | bytes 344068

commit v2 on v1

--- a/solution.py
+++ b/solution.py
@@ -18,7 +18,16 @@
     return slice(start, start + LANES)
 
 
-def pack(place, ensemble_ref, decay_ref, innovation_ref, weight_ref, out_ref, rows_ref):
+def pack(place, ensemble_hbm, decay_hbm, innovation_hbm, weight_hbm, out_ref,
+         ensemble_ref, decay_ref, innovation_ref, weight_ref, rows_ref, sems):
+    pairs = (
+        (ensemble_hbm, ensemble_ref), (weight_hbm, weight_ref), (decay_hbm, decay_ref), (innovation_hbm, innovation_ref)
+    )
+    copies = [pltpu.make_async_copy(*pair, sems.at[i]) for i, pair in enumerate(pairs)]
+    for copy in copies:
+        copy.start()
+    for copy in copies:
+        copy.wait()
     rows_ref[:COLS, :] = ensemble_ref[0].astype(jnp.float32) * jnp.sqrt(weight_ref[...])
     quarter = lax.rem(place, 8)
     start = pl.multiple_of(8 * jnp.minimum(lax.div(quarter, 2), 2), 8)
@@ -46,7 +55,7 @@
     return out
 
 
-def own_lines(in_ref, out_ref, rows_ref, fields_ref, state_ref, first_ref, sums_ref):
+def own_lines(in_ref, out_ref, rows_ref, fields_ref, state_ref, first_ref):
     for block in range(BLOCKS):
         piece = slice(block * LANES, (block + 1) * LANES)
         rows_ref[piece, :] = in_ref[piece, :].T
@@ -173,33 +182,32 @@
     line = sub % 4
     scalars = jnp.where(line == 0, alpha, jnp.where(line == 1, beta, jnp.where(line == 2, kappa, energy)))
     others = jnp.where(line == 0, cross, 0.0)
+    even = lane_group % 2 == 0
     for c in range(COLS):
-        put(c, [field(Z0, c)] * 2)
+        put(c, [jnp.where(even, field(Z0, c), field(Z1, c))] * 2)
     put(COLS, right0)
     put(COLS + 1, right1)
     put(COLS + 2, [scalars] * 2)
     put(COLS + 3, [others] * 2)
-    for c in range(COLS):
-        sums_ref[pl.ds(c, 4, stride=ROWS), :] = field(Z1, c)[:4]
-    for r in range(COLS, ROWS):
-        sums_ref[pl.ds(r, 4, stride=ROWS), :] = jnp.zeros((4, LANES), jnp.float32)
-    second = sums_ref[...].T
     for block in range(BLOCKS):
-        first = rows_ref[block * LANES : (block + 1) * LANES, :].T
-        out_ref[pl.ds(2 * block * LANES, LANES, stride=2), :] = first
-        out_ref[pl.ds(2 * block * LANES + 1, LANES, stride=2), :] = second
-
-
-def finish(in_ref, ensemble_ref, decay_ref, innovation_ref, weight_ref, control_ref, increment_ref,
-           first_ref, second_ref, driven_ref, rate_ref):
+        piece = slice(block * LANES, (block + 1) * LANES)
+        out_ref[piece, :] = rows_ref[piece, :].T
+
+
+def unpack(in_ref, out_ref):
     for block in range(BLOCKS):
-        for half, ref in enumerate((first_ref, second_ref)):
-            piece = in_ref[pl.ds(2 * block * LANES + half, LANES, stride=2), :].T
-            for line in range(LINES):
-                ref[:, lane_block(line, block)] = piece[line * ROWS : (line + 1) * ROWS]
+        piece = in_ref[block * LANES : (block + 1) * LANES, :].T
+        for line in range(LINES):
+            out_ref[:, lane_block(line, block)] = piece[line * ROWS : (line + 1) * ROWS]
+
+
+def finish(place, own_ref, in_ref, ensemble_ref, decay_ref, innovation_ref, weight_ref, control_ref, increment_ref,
+           other_ref, rate_ref):
+    unpack(in_ref, other_ref)
+    even = lax.rem(place, 2) == 0
 
     def scalar(row, line):
-        return first_ref[row : row + 1, line * DEVICES : (line + 1) * DEVICES]
+        return own_ref[row : row + 1, line * DEVICES : (line + 1) * DEVICES]
 
     def whole(value):
         return jnp.sum(value, axis=1, keepdims=True)
@@ -217,26 +225,25 @@
     ahead = step + back * (ratio + step * (kappa / alpha))
 
     root = jnp.sqrt(weight_ref[...])
-    z0 = first_ref[:COLS, :]
-    increment_ref[...] = (ahead * z0 - back * second_ref[:COLS, :]) / root
+    own, other = own_ref[:COLS, :], other_ref[:COLS, :]
+    z0, z1 = jnp.where(even, own, other), jnp.where(even, other, own)
+    increment_ref[...] = (ahead * z0 - back * z1) / root
     scaled = root * (ahead * (root * innovation_ref[...]) - back * z0)
     driven = ensemble_ref[0].astype(jnp.float32) * scaled
     groups = LINES * DEVICES // LANES
     carry = []
     for g in range(groups):
         part = slice(g * LANES, (g + 1) * LANES)
-        driven_ref[pl.ds(g, COLS, stride=groups), :] = driven[:, part]
+        control_ref[pl.ds(g, COLS, stride=groups), :] = driven[:, part]
         rate_ref[pl.ds(g, COLS, stride=groups), :] = decay_ref[:, part]
-        carry.append(ahead * first_ref[COLS : COLS + 1, part] - back * first_ref[COLS + 1 : COLS + 2, part])
+        carry.append(ahead * own_ref[COLS : COLS + 1, part] - back * own_ref[COLS + 1 : COLS + 2, part])
     carry = jnp.concatenate(carry, axis=0)
     for c in reversed(range(COLS)):
         part = slice(c * groups, (c + 1) * groups)
         rate = rate_ref[part, :]
-        summed = driven_ref[part, :] + carry
+        summed = control_ref[part, :] + carry
         carry = rate * summed
-        driven_ref[part, :] = jnp.sqrt((1.0 - rate) * (1.0 + rate)) * summed
-    for g in range(groups):
-        control_ref[0, :, g * LANES : (g + 1) * LANES] = driven_ref[pl.ds(g, COLS, stride=groups), :]
+        control_ref[part, :] = jnp.sqrt((1.0 - rate) * (1.0 + rate)) * summed
 
 
 def shape(*dims):
@@ -247,55 +254,70 @@
     return pltpu.VMEM(dims, jnp.float32)
 
 
-def call(kernel, out_shape, scratch_shapes, inputs):
+def call(kernel, out_shape, scratch_shapes, in_specs, limit=32 * 1024 * 1024):
     one = not isinstance(out_shape, tuple)
     return pl.pallas_call(
         kernel,
         out_shape=out_shape,
-        in_specs=[VMEM] * inputs,
+        in_specs=in_specs,
         out_specs=VMEM if one else (VMEM,) * len(out_shape),
         scratch_shapes=scratch_shapes,
-        compiler_params=pltpu.CompilerParams(vmem_limit_bytes=32 * 1024 * 1024),
+        compiler_params=pltpu.CompilerParams(vmem_limit_bytes=limit),
     )
 
 
-def pack_here(*refs):
-    pack(lax.axis_index("mem"), *refs)
+WIDTH = LINES * DEVICES
+
+
+def pack_call(place, *args):
+    return call(
+        lambda *refs: pack(place(), *refs),
+        shape(DEVICES, LANES),
+        [pltpu.VMEM((1, COLS, WIDTH), jnp.bfloat16)]
+        + [scratch(COLS, WIDTH)] * 3
+        + [scratch(ROWS, WIDTH), pltpu.SemaphoreType.DMA((4,))],
+        [pl.BlockSpec(memory_space=pltpu.HBM)] * 4,
+        limit=32 * 1024 * 1024,
+    )(*(pltpu.with_memory_space_constraint(a, pltpu.HBM) for a in args))
 
 
 def own_call(received):
     return call(
         own_lines,
-        shape(2 * DEVICES, LANES),
+        shape(DEVICES, LANES),
         [
             scratch(DEVICES, LANES),
             scratch(7, COLS, 8, LANES),
             scratch(COLS, 2, 8, LANES),
             scratch(COLS, 2, 8, LANES),
-            scratch(LANES, LANES),
         ],
-        1,
+        [VMEM],
     )(received)
 
 
-def finish_call(received, *args):
-    width = LINES * DEVICES
+def unpack_call(received):
+    return call(unpack, shape(ROWS, WIDTH), [], [VMEM])(received)
+
+
+def finish_call(place, own, received, *args):
     return call(
-        finish,
-        (shape(1, COLS, width), shape(COLS, width)),
-        [scratch(ROWS, width), scratch(ROWS, width)] + [scratch(COLS * width // LANES, LANES)] * 2,
-        5,
-    )(received, *args)
+        lambda *refs: finish(place(), *refs),
+        (shape(COLS * WIDTH // LANES, LANES), shape(COLS, WIDTH)),
+        [scratch(ROWS, WIDTH), scratch(COLS * WIDTH // LANES, LANES)],
+        [VMEM] * 6,
+    )(own, received, *args)
 
 
 def on_device(ensemble, decay_rate, innovation, obs_weight):
     args = (ensemble, decay_rate, innovation, obs_weight)
     axes = ("mem", "space")
-    sent = call(pack_here, shape(DEVICES, LANES), [scratch(ROWS, LINES * DEVICES)], 4)(*args)
+    place = lambda: lax.axis_index("mem")
+    sent = pack_call(place, *args)
     received = lax.all_to_all(sent, axes, 0, 0, tiled=True)
-    results = own_call(received).reshape(DEVICES, 2, LANES)
-    returned = lax.all_to_all(results, axes, 0, 0, tiled=True)
-    return finish_call(returned.reshape(2 * DEVICES, LANES), *args)
+    returned = lax.all_to_all(own_call(received), axes, 0, 0, tiled=True)
+    other = lax.ppermute(returned, "mem", [(k, k ^ 1) for k in range(MEMBERS)])
+    control, increment = finish_call(place, unpack_call(returned), other, *args)
+    return control.reshape(1, COLS, WIDTH), increment
 
 
 def solution(mesh):

time: 81.2 us -> 75.6 us (0.931)
  blocking collectives: 70.6 us -> 65.4 us
  local copies, waits for them, and re-layouts: 4.7 us -> 0.02 us
  starting transfers between devices: 0 us -> 2.04 us
  waiting for transfers between devices: 0 us -> 1.36 us
  Pallas kernels: 4.94 us -> 5.94 us
    all_to_all x1, blocking collectives: 31.3 us -> 26.1 us  [on_device(): returned = lax.all_to_all(own_call(received), axes, 0, 0, tiled=True)]
    unnamed x16 -> x8, local copies, waits for them, and re-layouts: 3.77 us -> 0.02 us
    ppermute x0 -> x1, starting transfers between devices: none -> 2.04 us  [on_device(): other = lax.ppermute(returned, 'mem', [(k, k ^ 1) for k in range(MEMBERS)])]
    ppermute x0 -> x1, waiting for transfers between devices: none -> 1.36 us  [on_device(): other = lax.ppermute(returned, 'mem', [(k, k ^ 1) for k in range(MEMBERS)])]
    pallas_call x3 -> x4, Pallas kernels: 4.94 us -> 5.94 us  [the longest x1 3.06 us: own_call(): call(own_lines, shape(DEVICES, LANES), [scratch(DEVICES, LANES), scratch(...]
    pallas_call x1 -> x0, local copies, waits for them, and re-layouts: 0.92 us -> none  [finish_call(): call(finish, (shape(1, COLS, width), shape(COLS, width)), [scratch(ROWS,...]
  transfers between devices with their start and end apart: 0 -> 1, of which waited for: 0 -> 1; matrix products, arithmetic and copies ran while one was open for 0% -> 0% of each run, Pallas kernels for 0% -> 0%
where the time goes in v2:
time: 75.6 us; the launch traced here: 75.4 us
  blocking collectives  65.4 us (87%)
  Pallas kernels  5.94 us (8%)
  starting transfers between devices  2.04 us (3%)
  waiting for transfers between devices  1.36 us (2%)
    all_to_all x1, blocking collectives, on_device(): received = lax.all_to_all(sent, axes, 0, 0, tiled=True)  39.3 us
    all_to_all x1, blocking collectives, on_device(): returned = lax.all_to_all(own_call(received), axes, 0, 0, tiled=True)  26.1 us
    pallas_call x1, Pallas kernels, own_call(): call(own_lines, shape(DEVICES, LANES), [scratch(DEVICES, LANES), scratch(...  3.06 us
    ppermute x1, starting transfers between devices, on_device(): other = lax.ppermute(returned, 'mem', [(k, k ^ 1) for k in range(MEMBERS)])  2.04 us
  transfers between devices with their start and end apart: 1, of which 1 were waited for; matrix products, arithmetic and copies ran while one was open for 0% of the time, Pallas kernels for 0%

profile of v2, /device:TPU:1, one launch (start us, length us, event | category | flops | bytes accessed | tf_op | source)
XLA Modules:
  0.0 75.4 jit_solution(11643456697851388768)
XLA Ops:
  0.6 1.4 %shard_map.59 = f32[512,128]{1,0:T(8,128)S(1)} custom-call(bf16[1,28,2048]{2,1,0:T(8,128)(2,1)} %refs_2_.3, f32[28,2048]{1,0:T(8,128)} %refs_3_.3, f32[28,2048]{1,0:T(8,128)} %refs_4_.1, f32[28,2048]{1,0:T(8,128)} %refs_5_.1), custom_call_target="tpu_custom_call" | custom-call | tf_op jit(solution)/shard_map/pallas_call | solution.py:273
  2.1 39.3 %all_to_all.22 = f32[512,1,128]{2,1,0:T(1,128)S(1)} all-to-all(f32[512,1,128]{2,1,0:T(1,128)S(1)} %bitcast.13), channel_id=1, replica_groups=mesh['mem'=16,'space'=32] {'mem','space'}, dimensions={0} | all-to-all | bytes 524288 | tf_op jit(solution)/shard_map/all_to_all | solution.py:316
  41.4 3.1 %shard_map.60 = f32[512,128]{1,0:T(8,128)S(1)} custom-call(f32[512,128]{1,0:T(8,128)S(1)} %bitcast.11), custom_call_target="tpu_custom_call" | custom-call | tf_op jit(solution)/shard_map/pallas_call | solution.py:285
  44.4 0.0 copy-start.2
  44.4 0.0 copy-start.3
  44.5 26.1 %all_to_all.23 = f32[512,1,128]{2,1,0:T(1,128)S(1)} all-to-all(f32[512,1,128]{2,1,0:T(1,128)S(1)} %bitcast.12), channel_id=1, replica_groups=mesh['mem'=16,'space'=32] {'mem','space'}, dimensions={0} | all-to-all | bytes 524288 | tf_op jit(solution)/shard_map/all_to_all | solution.py:317
  70.5 0.0 copy-start
  70.5 0.0 copy-start.1
  70.5 2.0 %collective-permute-start = (f32[512,128]{1,0:T(8,128)S(1)}, f32[512,128]{1,0:T(8,128)S(1)}, u32[]{:S(2)}, u32[]{:S(2)}) collective-permute-start(f32[512,128]{1,0:T(8,128)S(1)} %bitcast.9), channel_id=1, source_target_pairs={{0,32},{32,0},{64,96},{96,64},{128,160},{160,128},{192,224},{224,1... | collective-permute-start | bytes 786440 | tf_op jit(solution)/shard_map/ppermute | solution.py:318
  72.6 0.1 shard_map.61.refs_0_
  72.7 1.4 %collective-permute-done.refs_1_ = f32[512,128]{1,0:T(8,128)S(1)} collective-permute-done((f32[512,128]{1,0:T(8,128)S(1)}, f32[512,128]{1,0:T(8,128)S(1)}, u32[]{:S(2)}, u32[]{:S(2)}) %collective-permute-start) | collective-permute-done | bytes 262176 | tf_op jit(solution)/shard_map/ppermute | solution.py:318
  74.1 0.0 copy-done.2
  74.1 0.0 copy-done.3
  74.1 0.0 copy-done
  74.1 0.0 copy-done.1
  74.1 1.3 %shard_map.62 = (f32[448,128]{1,0:T(8,128)}, f32[28,2048]{1,0:T(8,128)}) custom-call(f32[32,2048]{1,0:T(8,128)S(1)} %shard_map.61.refs_0_, f32[512,128]{1,0:T(8,128)S(1)} %collective-permute-done.refs_1_, bf16[1,28,2048]{2,1,0:T(8,128)(2,1)S(1)} %copy-done.3, f32[28,2048]{1,0:T(8,128)S(1)} %copy-done, f32[28,2048]{1,0:T(8,128)S(1)} %copy-done.1, ...), custom_call_target="tpu_custom_call" | custom-call | tf_op jit(solution)/shard_map/pallas_call | solution.py:303
Async XLA Ops:
  44.4 29.7 %copy-start.2 = (f32[28,2048]{1,0:T(8,128)S(1)}, f32[28,2048]{1,0:T(8,128)}, u32[]{:S(2)}) copy-start(f32[28,2048]{1,0:T(8,128)} %refs_5_.1) | copy-start | bytes 688132
  44.4 29.6 %copy-start.3 = (bf16[1,28,2048]{2,1,0:T(8,128)(2,1)S(1)}, bf16[1,28,2048]{2,1,0:T(8,128)(2,1)}, u32[]{:S(2)}) copy-start(bf16[1,28,2048]{2,1,0:T(8,128)(2,1)} %refs_2_.3) | copy-start | bytes 344068
  70.5 3.6 %copy-start = (f32[28,2048]{1,0:T(8,128)S(1)}, f32[28,2048]{1,0:T(8,128)}, u32[]{:S(2)}) copy-start(f32[28,2048]{1,0:T(8,128)} %refs_3_.3) | copy-start | bytes 688132
  70.5 3.6 %copy-start.1 = (f32[28,2048]{1,0:T(8,128)S(1)}, f32[28,2048]{1,0:T(8,128)}, u32[]{:S(2)}) copy-start(f32[28,2048]{1,0:T(8,128)} %refs_4_.1) | copy-start | bytes 688132
  70.5 3.5 %collective-permute-start = (f32[512,128]{1,0:T(8,128)S(1)}, f32[512,128]{1,0:T(8,128)S(1)}, u32[]{:S(2)}, u32[]{:S(2)}) collective-permute-start(f32[512,128]{1,0:T(8,128)S(1)} %bitcast.9), channel_id=1, source_target_pairs={{0,32},{32,0},{64,96},{96,64},{128,160},{160,128},{192,224},{224,1... | collective-permute-start | bytes 786440 | tf_op jit(solution)/shard_map/ppermute | solution.py:318

commit v3 on v2

v3 whole, which is shorter than its diff:
```python
import jax
import jax.numpy as jnp
from jax import lax
from jax.experimental import pallas as pl
from jax.experimental.pallas import tpu as pltpu
from jax.sharding import PartitionSpec as P

MEMBERS, TILES, COLS, LINES = 16, 32, 28, 4
DEVICES = MEMBERS * TILES
ROWS = 32
LANES = 128
BLOCKS = DEVICES // LANES
GROUPS = LINES * BLOCKS
WIDTH = LINES * DEVICES
NEAR = 8
SCALARS = tuple(line * ROWS + COLS + 2 for line in range(LINES)) + (COLS + 3,)
VMEM = pl.BlockSpec(memory_space=pltpu.VMEM)
HBM = pl.BlockSpec(memory_space=pltpu.HBM)


def lane_block(line, block):
    start = line * DEVICES + block * LANES
    return slice(start, start + LANES)


def pack(place, ensemble_hbm, decay_hbm, innovation_hbm, weight_hbm, out_ref,
         ensemble_ref, decay_ref, innovation_ref, weight_ref, rows_ref, sems):
    pairs = (
        (ensemble_hbm, ensemble_ref), (weight_hbm, weight_ref), (decay_hbm, decay_ref), (innovation_hbm, innovation_ref)
    )
    copies = [pltpu.make_async_copy(*pair, sems.at[i]) for i, pair in enumerate(pairs)]
    for copy in copies:
        copy.start()
    for copy in copies:
        copy.wait()
    rows_ref[:COLS, :] = ensemble_ref[0].astype(jnp.float32) * jnp.sqrt(weight_ref[...])
    quarter = lax.rem(place, 8)
    start = pl.multiple_of(8 * jnp.minimum(lax.div(quarter, 2), 2), 8)

    def four(ref):
        eight = ref[pl.ds(start, 8), :]
        inner = jnp.where(lax.rem(quarter, 2) == 0, eight[:4], eight[4:])
        return jnp.where(quarter >= 6, ref[COLS - 4 :, :], inner)

    scaled = jnp.sqrt(four(weight_ref)) * four(innovation_ref)
    rows_ref[COLS:, :] = jnp.where(place < 8, four(decay_ref), scaled)
    for block in range(BLOCKS):
        piece = jnp.concatenate([rows_ref[:, lane_block(line, block)] for line in range(LINES)], axis=0)
        out_ref[block * LANES : (block + 1) * LANES, :] = piece.T


def spread(piece, lane_group):
    turned = [piece] + [pltpu.roll(piece, 32 * k, 1) for k in (1, 2, 3)]
    out = []
    for source in range(4):
        value = turned[(3 - source) % 4]
        for group in (2, 1, 0):
            value = jnp.where(lane_group == group, turned[(group - source) % 4], value)
        out.append(value)
    return out


def own_lines(in_ref, out_ref, rows_ref, members_ref, fields_ref, state_ref, first_ref):
    for block in range(BLOCKS):
        piece = slice(block * LANES, (block + 1) * LANES)
        rows_ref[piece, :] = in_ref[piece, :].T

    lane = lax.broadcasted_iota(jnp.int32, (8, LANES), 1)
    sub = lax.broadcasted_iota(jnp.int32, (8, LANES), 0)
    tile, lane_group = lane % TILES, lane // TILES
    low = sub < 4
    zero = jnp.zeros((8, LANES), jnp.float32)

    for c in range(COLS):
        value = rows_ref[pl.ds(c, 16, stride=ROWS), :]
        members_ref[c, 0], members_ref[c, 1] = value[:8], value[8:]

    RATE, SQUARED, AFTER, UPTO, INNOV, Z0, Z1 = range(7)

    def field(kind, c):
        return fields_ref[kind, c]

    for j in range(4):
        given = rows_ref[pl.ds(COLS + j, 16, stride=ROWS), :]
        for kind, value in ((RATE, given[:8]), (INNOV, given[8:])):
            other = pltpu.roll(value, 4, 0)
            for half, both in enumerate((jnp.where(low, value, other), jnp.where(low, other, value))):
                for source, copied in enumerate(spread(both, lane_group)):
                    c = 16 * half + 4 * source + j
                    if c < COLS:
                        fields_ref[kind, c] = copied

    upto, after = zero + 1.0, zero + 1.0
    for c in range(COLS):
        rate = field(RATE, c)
        fields_ref[SQUARED, c] = (1.0 - rate) * (1.0 + rate)
        upto = upto * rate
        fields_ref[UPTO, c] = upto
        fields_ref[AFTER, COLS - 1 - c] = after
        after = after * field(RATE, COLS - 1 - c)

    def turn(value, k, backward):
        return pltpu.roll(value, LANES - k if backward else k, 1)

    def inside(k, backward):
        return tile < TILES - k if backward else tile >= k

    def factors(backward):
        near, product = [], zero + 1.0
        for k in range(1, NEAR + 1):
            near.append((k, jnp.where(inside(k, backward), product, 0.0)))
            product = product * turn(upto, k, backward)
        stride = jnp.where(inside(NEAR, backward), product, 0.0)
        far, product = [(NEAR, stride)], stride
        for k in range(2 * NEAR, TILES, NEAR):
            product = stride * turn(product, NEAR, backward)
            far.append((k, jnp.where(inside(k, backward), product, 0.0)))
        return near, far

    chains = {backward: factors(backward) for backward in (True, False)}

    def entering(values, backward):
        near, far = chains[backward]
        out = []
        for value in values:
            value = sum(factor * turn(value, k, backward) for k, factor in near)
            out.append(value + sum(factor * turn(value, k, backward) for k, factor in far))
        return out

    def apply(source, target, on_state, on_field):
        carry = [zero, zero]
        for c in reversed(range(COLS)):
            rate, weight = field(RATE, c), field(source, c)
            for i in range(2):
                summed = members_ref[c, i] * weight + carry[i]
                state_ref[c, i] = summed
                carry[i] = rate * summed
        from_right = entering(carry, True)
        state = [zero, zero]
        for c in range(COLS):
            rate, squared, after = field(RATE, c), field(SQUARED, c), field(AFTER, c)
            for i in range(2):
                summed = state_ref[c, i] + after * from_right[i]
                driven = squared * summed
                on_state(c, i, summed, driven)
                state[i] = rate * state[i] + driven
                state_ref[c, i] = state[i]
        from_left = entering(state, False)
        for c in reversed(range(COLS)):
            upto = field(UPTO, c)
            total = sum(members_ref[c, i] * (state_ref[c, i] + upto * from_left[i]) for i in range(2))
            total = total + pltpu.roll(total, 4, 0)
            total = total + pltpu.roll(total, 64, 1)
            total = total + pltpu.roll(total, 32, 1)
            fields_ref[target, c] = total
            on_field(c, total)
        return from_right

    def whole(value):
        return jnp.sum(jnp.sum(value, axis=0, keepdims=True), axis=1, keepdims=True)

    sums = {name: zero for name in ("alpha", "beta", "kappa", "energy", "cross")}

    def keep(c, i, summed, driven):
        first_ref[c, i] = summed
        sums["alpha"] += summed * driven

    def square(c, total):
        sums["beta"] += total * total

    right0 = apply(INNOV, Z0, keep, square)
    alpha = whole(sums["alpha"])
    beta = 0.125 * whole(sums["beta"])
    ratio = jnp.where(alpha > 0.0, beta / jnp.where(alpha > 0.0, alpha, 1.0), 0.0)
    ratio = jnp.broadcast_to(ratio, (8, LANES))

    def orthogonal(c, i, summed, driven):
        part = summed - ratio * first_ref[c, i]
        sums["kappa"] += field(SQUARED, c) * part * part

    even = lane_group % 2 == 0

    def put(row, values):
        rows_ref[pl.ds(row, 16, stride=ROWS), :] = jnp.concatenate(values, axis=0)

    def compare(c, total):
        part = total - ratio * field(Z0, c)
        sums["energy"] += part * part
        sums["cross"] += part * field(Z0, c)
        put(c, [jnp.where(even, field(Z0, c), total)] * 2)

    put(COLS, right0)
    put(COLS + 1, apply(Z0, Z1, orthogonal, compare))
    scalars = (alpha, beta, whole(sums["kappa"]), 0.125 * whole(sums["energy"]), 0.125 * whole(sums["cross"]))
    row = lax.broadcasted_iota(jnp.int32, (1, LANES), 1)
    last = jnp.zeros((1, LANES), jnp.float32)
    for place, value in zip(SCALARS, scalars):
        last = jnp.where(row == place, value, last)
    last = jnp.broadcast_to(last, (LANES, LANES))
    ours = lax.broadcasted_iota(jnp.int32, (LANES, LANES), 1) % ROWS >= COLS + 2
    for block in range(BLOCKS):
        piece = slice(block * LANES, (block + 1) * LANES)
        out_ref[piece, :] = jnp.where(ours, last, rows_ref[piece, :].T)


def prepare(place, in_ref, ensemble_ref, decay_ref, innovation_ref, weight_ref,
            add_ref, scale_ref, add_control_ref, scale_control_ref, rate_ref, amplitude_ref, carry_ref, own_ref):
    for block in range(BLOCKS):
        piece = in_ref[block * LANES : (block + 1) * LANES, :].T
        for line in range(LINES):
            own_ref[:, lane_block(line, block)] = piece[line * ROWS : (line + 1) * ROWS]

    def scalar(at):
        line, row = at // ROWS, at % ROWS
        return own_ref[row : row + 1, line * DEVICES : (line + 1) * DEVICES]

    def whole(value):
        return jnp.sum(value, axis=1, keepdims=True)

    alphas, betas, kappas, energies, crosses = (scalar(at) for at in SCALARS)
    alpha, beta = whole(alphas), whole(betas)
    ratio = beta / alpha
    shift = jnp.where(alphas > 0.0, betas / jnp.where(alphas > 0.0, alphas, 1.0), 0.0) - ratio
    kappa = whole(kappas + alphas * shift * shift)
    energy = whole(energies + shift * (2.0 * crosses + shift * betas))
    step = alpha / (alpha + beta)
    curvature = kappa + energy - step * kappa * (kappa / alpha)
    back = jnp.where(curvature > 0.0, step * kappa / jnp.where(curvature > 0.0, curvature, 1.0), 0.0)
    ahead = step + back * (ratio + step * (kappa / alpha))

    even = lax.rem(place, 2) == 0
    to_own, to_other = jnp.where(even, ahead, -back), jnp.where(even, -back, ahead)
    z0_own, z0_other = jnp.where(even, -back, 0.0), jnp.where(even, 0.0, -back)
    for g in range(GROUPS):
        part = slice(g * LANES, (g + 1) * LANES)
        rows = pl.ds(g, COLS, stride=GROUPS)
        root = jnp.sqrt(weight_ref[:, part])
        own, inverse = own_ref[:COLS, part], 1.0 / root
        add_ref[:, part] = to_own * inverse * own
        scale_ref[:, part] = to_other * inverse
        factor = ensemble_ref[0, :, part].astype(jnp.float32) * root
        add_control_ref[rows, :] = factor * (ahead * (root * innovation_ref[:, part]) + z0_own * own)
        scale_control_ref[rows, :] = z0_other * factor
        rate = decay_ref[:, part]
        rate_ref[rows, :] = rate
        amplitude_ref[rows, :] = jnp.sqrt((1.0 - rate) * (1.0 + rate))
        carry_ref[g : g + 1, :] = ahead * own_ref[COLS : COLS + 1, part] - back * own_ref[COLS + 1 : COLS + 2, part]


def finish(in_ref, add_ref, scale_ref, add_control_ref, scale_control_ref, rate_ref, amplitude_ref, carry_ref,
           control_hbm, increment_hbm, control_ref, increment_ref, sems):
    for block in range(BLOCKS):
        piece = in_ref[block * LANES : (block + 1) * LANES, :].T
        for line in range(LINES):
            part, other = lane_block(line, block), piece[line * ROWS : line * ROWS + COLS]
            increment_ref[:, part] = add_ref[:, part] + scale_ref[:, part] * other
            control_ref[pl.ds(line * BLOCKS + block, COLS, stride=GROUPS), :] = other
    copies = [pltpu.make_async_copy(increment_ref, increment_hbm, sems.at[0])]
    copies[0].start()
    carry = carry_ref[...]
    for c in reversed(range(COLS)):
        part = slice(c * GROUPS, (c + 1) * GROUPS)
        summed = add_control_ref[part, :] + scale_control_ref[part, :] * control_ref[part, :] + carry
        carry = rate_ref[part, :] * summed
        control_ref[part, :] = amplitude_ref[part, :] * summed
        if c % 7 == 0:
            part = slice(c * GROUPS, (c + 7) * GROUPS)
            copies.append(
                pltpu.make_async_copy(control_ref.at[part, :], control_hbm.at[part, :], sems.at[len(copies)])
            )
            copies[-1].start()
    for copy in copies:
        copy.wait()


def shape(*dims):
    return jax.ShapeDtypeStruct(dims, jnp.float32)


def scratch(*dims):
    return pltpu.VMEM(dims, jnp.float32)


def call(kernel, out_shape, scratch_shapes, in_specs, out_specs):
    return pl.pallas_call(
        kernel,
        out_shape=out_shape,
        in_specs=in_specs,
        out_specs=out_specs,
        scratch_shapes=scratch_shapes,
        compiler_params=pltpu.CompilerParams(vmem_limit_bytes=32 * 1024 * 1024),
    )


def pack_call(place, *args):
    return call(
        lambda *refs: pack(place(), *refs),
        shape(DEVICES, LANES),
        [pltpu.VMEM((1, COLS, WIDTH), jnp.bfloat16)]
        + [scratch(COLS, WIDTH)] * 3
        + [scratch(ROWS, WIDTH), pltpu.SemaphoreType.DMA((4,))],
        [HBM] * 4,
        VMEM,
    )(*(pltpu.with_memory_space_constraint(value, pltpu.HBM) for value in args))


def own_call(received):
    return call(
        own_lines,
        shape(DEVICES, LANES),
        [
            scratch(DEVICES, LANES),
            scratch(COLS, 2, 8, LANES),
            scratch(7, COLS, 8, LANES),
            scratch(COLS, 2, 8, LANES),
            scratch(COLS, 2, 8, LANES),
        ],
        [VMEM],
        VMEM,
    )(received)


def prepare_call(place, returned, *args):
    plain, by_column = shape(COLS, WIDTH), shape(COLS * GROUPS, LANES)
    return call(
        lambda *refs: prepare(place(), *refs),
        (plain, plain, by_column, by_column, by_column, by_column, shape(GROUPS, LANES)),
        [scratch(ROWS, WIDTH)],
        [VMEM] * 5,
        (VMEM,) * 7,
    )(returned, *args)


def finish_call(other, *prepared):
    return call(
        finish,
        (shape(COLS * GROUPS, LANES), shape(COLS, WIDTH)),
        [scratch(COLS * GROUPS, LANES), scratch(COLS, WIDTH), pltpu.SemaphoreType.DMA((5,))],
        [VMEM] * 8,
        (HBM, HBM),
    )(other, *prepared)


def on_device(ensemble, decay_rate, innovation, obs_weight):
    args = (ensemble, decay_rate, innovation, obs_weight)
    axes = ("mem", "space")
    place = lambda: lax.axis_index("mem")
    sent = pack_call(place, *args)
    received = lax.all_to_all(sent, axes, 0, 0, tiled=True)
    returned = lax.all_to_all(own_call(received), axes, 0, 0, tiled=True)
    other = lax.ppermute(returned, "mem", [(k, k ^ 1) for k in range(MEMBERS)])
    control, increment = finish_call(other, *prepare_call(place, returned, *args))
    return control.reshape(1, COLS, WIDTH), increment


def solution(mesh):
    in_specs = (P("mem", "space", None), P("space", None), P("space", None), P("space", None))
    out_specs = (P("mem", "space", None), P("space", None))
    return jax.shard_map(
        on_device, mesh=mesh, in_specs=in_specs, out_specs=out_specs, check_vma=False
    )
```

time: 75.6 us -> 74 us (0.979)
  waiting for transfers between devices: 1.36 us -> 0.6 us
    pallas_call x1, Pallas kernels: 3.06 us -> 1.91 us  [own_call(): call(own_lines, shape(DEVICES, LANES), [scratch(DEVICES, LANES), scratch(...]
    ppermute x1, waiting for transfers between devices: 1.36 us -> 0.6 us  [on_device(): other = lax.ppermute(returned, 'mem', [(k, k ^ 1) for k in range(MEMBERS)])]
  transfers between devices with their start and end apart: 1 -> 1, of which waited for: 1 -> 1; matrix products, arithmetic and copies ran while one was open for 0% -> 0% of each run, Pallas kernels for 0% -> 1%
where the time goes in v3:
time: 74 us; the launch traced here: 73.8 us
  blocking collectives  65.4 us (88%)
  Pallas kernels  5.19 us (7%)
  starting transfers between devices  1.91 us (3%)
    all_to_all x1, blocking collectives, on_device(): received = lax.all_to_all(sent, axes, 0, 0, tiled=True)  39.3 us
    all_to_all x1, blocking collectives, on_device(): returned = lax.all_to_all(own_call(received), axes, 0, 0, tiled=True)  26.1 us
    ppermute x1, starting transfers between devices, on_device(): other = lax.ppermute(returned, 'mem', [(k, k ^ 1) for k in range(MEMBERS)])  1.91 us
    pallas_call x1, Pallas kernels, own_call(): call(own_lines, shape(DEVICES, LANES), [scratch(DEVICES, LANES), scratch(...  1.91 us
  transfers between devices with their start and end apart: 1, of which 1 were waited for; matrix products, arithmetic and copies ran while one was open for 0% of the time, Pallas kernels for 1%

profile of v3, /device:TPU:1, one launch (start us, length us, event | category | flops | bytes accessed | tf_op | source)
XLA Modules:
  0.0 73.8 jit_solution(6542454176107629283)
XLA Ops:
  0.6 1.4 %shard_map.59 = f32[512,128]{1,0:T(8,128)S(1)} custom-call(bf16[1,28,2048]{2,1,0:T(8,128)(2,1)} %refs_1_.3, f32[28,2048]{1,0:T(8,128)} %refs_2_.3, f32[28,2048]{1,0:T(8,128)} %refs_3_.3, f32[28,2048]{1,0:T(8,128)} %refs_4_.1), custom_call_target="tpu_custom_call" | custom-call | tf_op jit(solution)/shard_map/pallas_call | solution.py:296
  2.1 39.3 %all_to_all.22 = f32[512,1,128]{2,1,0:T(1,128)S(1)} all-to-all(f32[512,1,128]{2,1,0:T(1,128)S(1)} %bitcast.13), channel_id=1, replica_groups=mesh['mem'=16,'space'=32] {'mem','space'}, dimensions={0} | all-to-all | bytes 524288 | tf_op jit(solution)/shard_map/all_to_all | solution.py:349
  41.4 0.0 copy-start.2
  41.4 0.0 copy-start.3
  41.4 1.9 %shard_map.60 = f32[512,128]{1,0:T(8,128)S(1)} custom-call(f32[512,128]{1,0:T(8,128)S(1)} %bitcast.9), custom_call_target="tpu_custom_call" | custom-call | tf_op jit(solution)/shard_map/pallas_call | solution.py:308
  43.3 0.0 copy-start
  43.3 0.0 copy-start.1
  43.3 26.1 %all_to_all.23 = f32[512,1,128]{2,1,0:T(1,128)S(1)} all-to-all(f32[512,1,128]{2,1,0:T(1,128)S(1)} %bitcast.10), channel_id=1, replica_groups=mesh['mem'=16,'space'=32] {'mem','space'}, dimensions={0} | all-to-all | bytes 524288 | tf_op jit(solution)/shard_map/all_to_all | solution.py:350
  69.4 1.9 %collective-permute-start = (f32[512,128]{1,0:T(8,128)S(1)}, f32[512,128]{1,0:T(8,128)S(1)}, u32[]{:S(2)}, u32[]{:S(2)}) collective-permute-start(f32[512,128]{1,0:T(8,128)S(1)} %bitcast.11), channel_id=1, source_target_pairs={{0,32},{32,0},{64,96},{96,64},{128,160},{160,128},{192,224},{224,1... | collective-permute-start | bytes 786440 | tf_op jit(solution)/shard_map/ppermute | solution.py:351
  71.3 0.0 copy-done.2
  71.3 0.0 copy-done.3
  71.3 0.0 copy-done
  71.3 0.0 copy-done.1
  71.3 0.8 %shard_map.61 = (f32[28,2048]{1,0:T(8,128)S(1)}, f32[28,2048]{1,0:T(8,128)S(1)}, f32[448,128]{1,0:T(8,128)S(1)}, f32[448,128]{1,0:T(8,128)S(1)}, f32[448,128]{1,...) custom-call(f32[512,128]{1,0:T(8,128)S(1)} %bitcast.12, bf16[1,28,2048]{2,1,0:T(8,128)(2,1)S(1)} %copy-done.3, ...), custom_call_target="tpu_custom_call" | custom-call | tf_op jit(solution)/shard_map/pallas_call | solution.py:325
  72.2 0.6 collective-permute-done.in_ref
  72.8 1.0 %shard_map.62 = (f32[448,128]{1,0:T(8,128)}, f32[28,2048]{1,0:T(8,128)}) custom-call(f32[512,128]{1,0:T(8,128)S(1)} %collective-permute-done.in_ref, f32[28,2048]{1,0:T(8,128)S(1)} %get-tuple-element.11.add_ref, f32[28,2048]{1,0:T(8,128)S(1)} %get-tuple-element.12.scale_ref, f32[448,128]{1,0:T(8,128)S(1)} %get-tuple-element.13.add_control_ref, ...), custom_call_target="tpu_custom_call" | custom-call | tf_op jit(solution)/shard_map/pallas_call | solution.py:335
Async XLA Ops:
  41.4 29.9 %copy-start.2 = (f32[28,2048]{1,0:T(8,128)S(1)}, f32[28,2048]{1,0:T(8,128)}, u32[]{:S(2)}) copy-start(f32[28,2048]{1,0:T(8,128)} %refs_4_.1) | copy-start | bytes 688132
  41.4 29.9 %copy-start.3 = (bf16[1,28,2048]{2,1,0:T(8,128)(2,1)S(1)}, bf16[1,28,2048]{2,1,0:T(8,128)(2,1)}, u32[]{:S(2)}) copy-start(bf16[1,28,2048]{2,1,0:T(8,128)(2,1)} %refs_1_.3) | copy-start | bytes 344068
  43.3 28.0 %copy-start = (f32[28,2048]{1,0:T(8,128)S(1)}, f32[28,2048]{1,0:T(8,128)}, u32[]{:S(2)}) copy-start(f32[28,2048]{1,0:T(8,128)} %refs_2_.3) | copy-start | bytes 688132
  43.3 28.0 %copy-start.1 = (f32[28,2048]{1,0:T(8,128)S(1)}, f32[28,2048]{1,0:T(8,128)}, u32[]{:S(2)}) copy-start(f32[28,2048]{1,0:T(8,128)} %refs_3_.3) | copy-start | bytes 688132
  69.4 3.4 %collective-permute-start = (f32[512,128]{1,0:T(8,128)S(1)}, f32[512,128]{1,0:T(8,128)S(1)}, u32[]{:S(2)}, u32[]{:S(2)}) collective-permute-start(f32[512,128]{1,0:T(8,128)S(1)} %bitcast.11), channel_id=1, source_target_pairs={{0,32},{32,0},{64,96},{96,64},{128,160},{160,128},{192,224},{224,1... | collective-permute-start | bytes 786440 | tf_op jit(solution)/shard_map/ppermute | solution.py:351

commit v4 on v3

--- a/solution.py
+++ b/solution.py
@@ -12,6 +12,7 @@
 BLOCKS = DEVICES // LANES
 GROUPS = LINES * BLOCKS
 WIDTH = LINES * DEVICES
+CHIPS, HALF = DEVICES // 2, WIDTH // 2
 NEAR = 8
 SCALARS = tuple(line * ROWS + COLS + 2 for line in range(LINES)) + (COLS + 3,)
 VMEM = pl.BlockSpec(memory_space=pltpu.VMEM)
@@ -19,7 +20,7 @@
 
 
 def lane_block(line, block):
-    start = line * DEVICES + block * LANES
+    start = (block // 2) * HALF + line * CHIPS + (block % 2) * LANES
     return slice(start, start + LANES)
 
 
@@ -178,8 +179,6 @@
         part = summed - ratio * first_ref[c, i]
         sums["kappa"] += field(SQUARED, c) * part * part
 
-    even = lane_group % 2 == 0
-
     def put(row, values):
         rows_ref[pl.ds(row, 16, stride=ROWS), :] = jnp.concatenate(values, axis=0)
 
@@ -187,7 +186,7 @@
         part = total - ratio * field(Z0, c)
         sums["energy"] += part * part
         sums["cross"] += part * field(Z0, c)
-        put(c, [jnp.where(even, field(Z0, c), total)] * 2)
+        put(c, [field(Z0, c), total])
 
     put(COLS, right0)
     put(COLS + 1, apply(Z0, Z1, orthogonal, compare))
@@ -199,25 +198,67 @@
     last = jnp.broadcast_to(last, (LANES, LANES))
     ours = lax.broadcasted_iota(jnp.int32, (LANES, LANES), 1) % ROWS >= COLS + 2
     for block in range(BLOCKS):
-        piece = slice(block * LANES, (block + 1) * LANES)
-        out_ref[piece, :] = jnp.where(ours, last, rows_ref[piece, :].T)
-
-
-def prepare(place, in_ref, ensemble_ref, decay_ref, innovation_ref, weight_ref,
-            add_ref, scale_ref, add_control_ref, scale_control_ref, rate_ref, amplitude_ref, carry_ref, own_ref):
-    for block in range(BLOCKS):
-        piece = in_ref[block * LANES : (block + 1) * LANES, :].T
+        piece = rows_ref[block * LANES : (block + 1) * LANES, :].T
+        to = pl.ds((block % 2) * 2 * LANES + block // 2, LANES, stride=2)
+        out_ref[to, :] = jnp.where(ours, last, piece)
+
+
+def one_half(at, first, in_ref, ensemble_ref, decay_ref, innovation_ref, weight_ref,
+             field0_ref, field1_ref, vector0_ref, vector1_ref, scalars_ref, rate_ref, amplitude_ref):
+    rows = []
+    for j in range(2):
+        pieces = [in_ref[pl.ds(2 * j * LANES + h, LANES, stride=2), :].T for h in range(2)]
+        state = jnp.where(first, pieces[0], pieces[1])
         for line in range(LINES):
-            own_ref[:, lane_block(line, block)] = piece[line * ROWS : (line + 1) * ROWS]
-
-    def scalar(at):
-        line, row = at // ROWS, at % ROWS
-        return own_ref[row : row + 1, line * DEVICES : (line + 1) * DEVICES]
+            start = line * CHIPS + j * LANES
+            here = pl.ds(pl.multiple_of(at + start, LANES), LANES)
+            part = slice(start, start + LANES)
+            group = pl.ds(2 * line + j, COLS, stride=8)
+            root = jnp.sqrt(weight_ref[:, here])
+            inverse = 1.0 / root
+            z0, z1 = (piece[line * ROWS : line * ROWS + COLS] for piece in pieces)
+            field0_ref[:, part] = inverse * z0
+            field1_ref[:, part] = inverse * z1
+            factor = ensemble_ref[0, :, here].astype(jnp.float32) * root
+            vector0_ref[group, :] = factor * (root * innovation_ref[:, here])
+            vector1_ref[group, :] = factor * z0
+            rate = decay_ref[:, here]
+            rate_ref[group, :] = rate
+            amplitude_ref[group, :] = jnp.sqrt((1.0 - rate) * (1.0 + rate))
+            rows.append((2 * line + j, state[line * ROWS + COLS : line * ROWS + COLS + 2]))
+        for i, place in enumerate(SCALARS):
+            scalars_ref[i : i + 1, j * LANES : (j + 1) * LANES] = pieces[0][place : place + 1]
+    rows = [row for _, row in sorted(rows, key=lambda pair: pair[0])]
+    refs = (vector0_ref, vector1_ref)
+    carry = [jnp.concatenate([row[i : i + 1] for row in rows], axis=0) for i in range(2)]
+    for c in reversed(range(COLS)):
+        part = slice(8 * c, 8 * c + 8)
+        rate, amplitude = rate_ref[part, :], amplitude_ref[part, :]
+        for i, ref in enumerate(refs):
+            summed = ref[part, :] + carry[i]
+            carry[i] = rate * summed
+            ref[part, :] = amplitude * summed
+
+
+def prepare(core, *refs):
+    one_half(core * HALF, core == 0, *refs)
+
+
+def finish(core, in_ref, ensemble_ref, decay_ref, innovation_ref, weight_ref, *refs):
+    own = refs[:5]
+    control_hbm, increment_hbm = refs[5:7]
+    other = refs[7:12]
+    rate_ref, amplitude_ref, control_ref, increment_ref, sems = refs[12:]
+    inputs = (in_ref, ensemble_ref, decay_ref, innovation_ref, weight_ref)
+    one_half((1 - core) * HALF, core == 0, *inputs, *other, rate_ref, amplitude_ref)
 
     def whole(value):
         return jnp.sum(value, axis=1, keepdims=True)
 
-    alphas, betas, kappas, energies, crosses = (scalar(at) for at in SCALARS)
+    def both(i):
+        return jnp.concatenate([ref[i : i + 1, :] for ref in (own[4], other[4])], axis=1)
+
+    alphas, betas, kappas, energies, crosses = (both(i) for i in range(5))
     alpha, beta = whole(alphas), whole(betas)
     ratio = beta / alpha
     shift = jnp.where(alphas > 0.0, betas / jnp.where(alphas > 0.0, alphas, 1.0), 0.0) - ratio
@@ -228,47 +269,24 @@
     back = jnp.where(curvature > 0.0, step * kappa / jnp.where(curvature > 0.0, curvature, 1.0), 0.0)
     ahead = step + back * (ratio + step * (kappa / alpha))
 
-    even = lax.rem(place, 2) == 0
-    to_own, to_other = jnp.where(even, ahead, -back), jnp.where(even, -back, ahead)
-    z0_own, z0_other = jnp.where(even, -back, 0.0), jnp.where(even, 0.0, -back)
-    for g in range(GROUPS):
-        part = slice(g * LANES, (g + 1) * LANES)
-        rows = pl.ds(g, COLS, stride=GROUPS)
-        root = jnp.sqrt(weight_ref[:, part])
-        own, inverse = own_ref[:COLS, part], 1.0 / root
-        add_ref[:, part] = to_own * inverse * own
-        scale_ref[:, part] = to_other * inverse
-        factor = ensemble_ref[0, :, part].astype(jnp.float32) * root
-        add_control_ref[rows, :] = factor * (ahead * (root * innovation_ref[:, part]) + z0_own * own)
-        scale_control_ref[rows, :] = z0_other * factor
-        rate = decay_ref[:, part]
-        rate_ref[rows, :] = rate
-        amplitude_ref[rows, :] = jnp.sqrt((1.0 - rate) * (1.0 + rate))
-        carry_ref[g : g + 1, :] = ahead * own_ref[COLS : COLS + 1, part] - back * own_ref[COLS + 1 : COLS + 2, part]
-
-
-def finish(in_ref, add_ref, scale_ref, add_control_ref, scale_control_ref, rate_ref, amplitude_ref, carry_ref,
-           control_hbm, increment_hbm, control_ref, increment_ref, sems):
-    for block in range(BLOCKS):
-        piece = in_ref[block * LANES : (block + 1) * LANES, :].T
-        for line in range(LINES):
-            part, other = lane_block(line, block), piece[line * ROWS : line * ROWS + COLS]
-            increment_ref[:, part] = add_ref[:, part] + scale_ref[:, part] * other
-            control_ref[pl.ds(line * BLOCKS + block, COLS, stride=GROUPS), :] = other
-    copies = [pltpu.make_async_copy(increment_ref, increment_hbm, sems.at[0])]
-    copies[0].start()
-    carry = carry_ref[...]
-    for c in reversed(range(COLS)):
-        part = slice(c * GROUPS, (c + 1) * GROUPS)
-        summed = add_control_ref[part, :] + scale_control_ref[part, :] * control_ref[part, :] + carry
-        carry = rate_ref[part, :] * summed
-        control_ref[part, :] = amplitude_ref[part, :] * summed
-        if c % 7 == 0:
-            part = slice(c * GROUPS, (c + 7) * GROUPS)
-            copies.append(
-                pltpu.make_async_copy(control_ref.at[part, :], control_hbm.at[part, :], sems.at[len(copies)])
-            )
-            copies[-1].start()
+    copies = []
+
+    def send(source, target):
+        copies.append(pltpu.make_async_copy(source, target, sems.at[len(copies)]))
+        copies[-1].start()
+
+    for at, (field0_ref, field1_ref, *_) in ((core, own), (1 - core, other)):
+        here = pl.ds(pl.multiple_of(at * HALF, HALF), HALF)
+        increment_ref[:, here] = ahead * field0_ref[...] - back * field1_ref[...]
+    send(increment_ref, increment_hbm)
+    for quarter in range(4):
+        for c in range(7 * quarter, 7 * quarter + 7):
+            for at, (_, _, vector0_ref, vector1_ref, _) in ((core, own), (1 - core, other)):
+                part = slice(8 * c, 8 * c + 8)
+                here = pl.ds(pl.multiple_of(c * GROUPS + 8 * at, 8), 8)
+                control_ref[here, :] = ahead * vector0_ref[part, :] - back * vector1_ref[part, :]
+        part = slice(7 * quarter * GROUPS, (7 * quarter + 7) * GROUPS)
+        send(control_ref.at[part, :], control_hbm.at[part, :])
     for copy in copies:
         copy.wait()
 
@@ -320,42 +338,47 @@
     )(received)
 
 
-def prepare_call(place, returned, *args):
-    plain, by_column = shape(COLS, WIDTH), shape(COLS * GROUPS, LANES)
+HALVES = ((COLS, HALF), (COLS, HALF), (COLS * 8, LANES), (COLS * 8, LANES), (8, CHIPS))
+
+
+def prepare_call(core, returned, *args):
     return call(
-        lambda *refs: prepare(place(), *refs),
-        (plain, plain, by_column, by_column, by_column, by_column, shape(GROUPS, LANES)),
-        [scratch(ROWS, WIDTH)],
+        lambda *refs: prepare(core(), *refs),
+        tuple(shape(*dims) for dims in HALVES),
+        [scratch(COLS * 8, LANES)] * 2,
         [VMEM] * 5,
-        (VMEM,) * 7,
+        (VMEM,) * 5,
     )(returned, *args)
 
 
-def finish_call(other, *prepared):
+def finish_call(core, other, args, prepared):
     return call(
-        finish,
+        lambda *refs: finish(core(), *refs),
         (shape(COLS * GROUPS, LANES), shape(COLS, WIDTH)),
-        [scratch(COLS * GROUPS, LANES), scratch(COLS, WIDTH), pltpu.SemaphoreType.DMA((5,))],
-        [VMEM] * 8,
+        [scratch(*dims) for dims in HALVES]
+        + [scratch(COLS * 8, LANES)] * 2
+        + [scratch(COLS * GROUPS, LANES), scratch(COLS, WIDTH), pltpu.SemaphoreType.DMA((5,))],
+        [VMEM] * 10,
         (HBM, HBM),
-    )(other, *prepared)
+    )(other, *args, *prepared)
 
 
 def on_device(ensemble, decay_rate, innovation, obs_weight):
     args = (ensemble, decay_rate, innovation, obs_weight)
-    axes = ("mem", "space")
-    place = lambda: lax.axis_index("mem")
-    sent = pack_call(place, *args)
-    received = lax.all_to_all(sent, axes, 0, 0, tiled=True)
-    returned = lax.all_to_all(own_call(received), axes, 0, 0, tiled=True)
-    other = lax.ppermute(returned, "mem", [(k, k ^ 1) for k in range(MEMBERS)])
-    control, increment = finish_call(other, *prepare_call(place, returned, *args))
+    core = lambda: lax.axis_index("core")
+    sent = pack_call(lambda: 8 * lax.axis_index("core") + lax.axis_index("y"), *args)
+    received = lax.all_to_all(sent, ("core", "y", "space"), 0, 0, tiled=True)
+    results = own_call(received).reshape(CHIPS, 2, LANES)
+    returned = lax.all_to_all(results, ("y", "space"), 0, 0, tiled=True).reshape(DEVICES, LANES)
+    other = lax.ppermute(returned, "core", [(0, 1), (1, 0)])
+    control, increment = finish_call(core, other, args, prepare_call(core, returned, *args))
     return control.reshape(1, COLS, WIDTH), increment
 
 
 def solution(mesh):
-    in_specs = (P("mem", "space", None), P("space", None), P("space", None), P("space", None))
-    out_specs = (P("mem", "space", None), P("space", None))
+    chips = jax.sharding.Mesh(mesh.devices.reshape(MEMBERS // 2, 2, TILES), ("y", "core", "space"))
+    split = P(("y", "core"), "space", None)
+    in_specs = (split, P("space", None), P("space", None), P("space", None))
     return jax.shard_map(
-        on_device, mesh=mesh, in_specs=in_specs, out_specs=out_specs, check_vma=False
+        on_device, mesh=chips, in_specs=in_specs, out_specs=(split, P("space", None)), check_vma=False
     )

time: 74 us -> 72.4 us (0.978)
  blocking collectives: 65.4 us -> 61.2 us
  starting transfers between devices: 1.91 us -> 4.76 us
    all_to_all x2, blocking collectives: 65.4 us -> 61.2 us  [the longest x1 38.7 us: on_device(): received = lax.all_to_all(sent, ('core', 'y', 'space'), 0, 0, tiled=True)]
    ppermute x1, starting transfers between devices: 1.91 us -> 4.76 us  [on_device(): other = lax.ppermute(returned, 'core', [(0, 1), (1, 0)])]
  transfers between devices with their start and end apart: 1 -> 1, of which waited for: 1 -> 1; matrix products, arithmetic and copies ran while one was open for 0% -> 0% of each run, Pallas kernels for 1% -> 0%
where the time goes in v4:
time: 72.4 us; the launch traced here: 72.2 us
  blocking collectives  61.2 us (85%)
  starting transfers between devices  4.76 us (7%)
  Pallas kernels  4.57 us (6%)
  waiting for transfers between devices  0.88 us (1%)
    all_to_all x1, blocking collectives, on_device(): received = lax.all_to_all(sent, ('core', 'y', 'space'), 0, 0, tiled=True)  38.7 us
    all_to_all x1, blocking collectives, on_device(): lax.all_to_all(results, ('y', 'space'), 0, 0, tiled=True)  22.6 us
    ppermute x1, starting transfers between devices, on_device(): other = lax.ppermute(returned, 'core', [(0, 1), (1, 0)])  4.76 us
    pallas_call x1, Pallas kernels, own_call(): call(own_lines, shape(DEVICES, LANES), [scratch(DEVICES, LANES), scratch(...  1.76 us
  transfers between devices with their start and end apart: 1, of which 1 were waited for; matrix products, arithmetic and copies ran while one was open for 0% of the time, Pallas kernels for 0%

profile of v4, /device:TPU:1, one launch (start us, length us, event | category | flops | bytes accessed | tf_op | source)
XLA Modules:
  0.0 72.2 jit_solution(18043437824302008778)
XLA Ops:
  0.6 1.4 %shard_map.59 = f32[512,128]{1,0:T(8,128)S(1)} custom-call(bf16[1,28,2048]{2,1,0:T(8,128)(2,1)} %refs_1_.5, f32[28,2048]{1,0:T(8,128)} %refs_2_.5, f32[28,2048]{1,0:T(8,128)} %refs_3_.5, f32[28,2048]{1,0:T(8,128)} %refs_4_.3), custom_call_target="tpu_custom_call" | custom-call | tf_op jit(solution)/shard_map/pallas_call | solution.py:314
  2.1 38.7 %all_to_all.16 = f32[512,1,128]{2,1,0:T(1,128)S(1)} all-to-all(f32[512,1,128]{2,1,0:T(1,128)S(1)} %bitcast.11), channel_id=1, replica_groups=mesh['y'=8,'core'=2,'space'=32] {'core','y','space'}, dimensions={0} | all-to-all | bytes 524288 | tf_op jit(solution)/shard_map/all_to_all | solution.py:370
  40.7 0.0 copy-start.2
  40.8 0.0 copy-start.3
  40.8 1.8 %shard_map.60 = f32[512,128]{1,0:T(8,128)S(1)} custom-call(f32[512,128]{1,0:T(8,128)S(1)} %bitcast.7), custom_call_target="tpu_custom_call" | custom-call | tf_op jit(solution)/shard_map/pallas_call | solution.py:326
  42.5 0.0 copy-start
  42.5 0.0 copy-start.1
  42.5 22.6 %all_to_all.17 = f32[256,2,128]{2,1,0:T(2,128)S(1)} all-to-all(f32[256,2,128]{2,1,0:T(2,128)S(1)} %bitcast.8), channel_id=1, replica_groups=mesh['y'=8,'core'=2,'space'=32] {'y','space'}, dimensions={0} | all-to-all | bytes 524288 | tf_op jit(solution)/shard_map/all_to_all | solution.py:372
  65.1 4.8 %collective-permute-start = (f32[512,128]{1,0:T(8,128)S(1)}, f32[512,128]{1,0:T(8,128)S(1)}, u32[]{:S(2)}, u32[]{:S(2)}) collective-permute-start(f32[512,128]{1,0:T(8,128)S(1)} %bitcast.9), channel_id=1, source_target_pairs={{0,32},{32,0},{1,33},{33,1},{2,34},{34,2},{3,35},{35,3},{4,36},{36... | collective-permute-start | bytes 786440 | tf_op jit(solution)/shard_map/ppermute | solution.py:373
  69.9 0.0 copy-done.2
  69.9 0.0 copy-done.3
  69.9 0.0 copy-done
  69.9 0.0 copy-done.1
  69.9 0.2 shard_map.61
  70.1 0.9 %collective-permute-done.refs_0_ = f32[512,128]{1,0:T(8,128)S(1)} collective-permute-done((f32[512,128]{1,0:T(8,128)S(1)}, f32[512,128]{1,0:T(8,128)S(1)}, u32[]{:S(2)}, u32[]{:S(2)}) %collective-permute-start) | collective-permute-done | bytes 262176 | tf_op jit(solution)/shard_map/ppermute | solution.py:373
  71.0 1.1 %shard_map.62 = (f32[448,128]{1,0:T(8,128)}, f32[28,2048]{1,0:T(8,128)}) custom-call(f32[512,128]{1,0:T(8,128)S(1)} %collective-permute-done.refs_0_, bf16[1,28,2048]{2,1,0:T(8,128)(2,1)S(1)} %copy-done.3, f32[28,2048]{1,0:T(8,128)S(1)} %copy-done, f32[28,2048]{1,0:T(8,128)S(1)} %copy-done.1, f32[28,2048]{1,0:T(8,128)S(1)} %copy-done.2, ...), custom_call_target="tpu_custom_call" | custom-call | tf_op jit(solution)/shard_map/pallas_call | solution.py:355
Async XLA Ops:
  40.7 29.1 %copy-start.2 = (f32[28,2048]{1,0:T(8,128)S(1)}, f32[28,2048]{1,0:T(8,128)}, u32[]{:S(2)}) copy-start(f32[28,2048]{1,0:T(8,128)} %refs_4_.3) | copy-start | bytes 688132
  40.8 29.1 %copy-start.3 = (bf16[1,28,2048]{2,1,0:T(8,128)(2,1)S(1)}, bf16[1,28,2048]{2,1,0:T(8,128)(2,1)}, u32[]{:S(2)}) copy-start(bf16[1,28,2048]{2,1,0:T(8,128)(2,1)} %refs_1_.5) | copy-start | bytes 344068
  42.5 27.4 %copy-start = (f32[28,2048]{1,0:T(8,128)S(1)}, f32[28,2048]{1,0:T(8,128)}, u32[]{:S(2)}) copy-start(f32[28,2048]{1,0:T(8,128)} %refs_2_.5) | copy-start | bytes 688132
  42.5 27.4 %copy-start.1 = (f32[28,2048]{1,0:T(8,128)S(1)}, f32[28,2048]{1,0:T(8,128)}, u32[]{:S(2)}) copy-start(f32[28,2048]{1,0:T(8,128)} %refs_3_.5) | copy-start | bytes 688132
  65.1 5.9 %collective-permute-start = (f32[512,128]{1,0:T(8,128)S(1)}, f32[512,128]{1,0:T(8,128)S(1)}, u32[]{:S(2)}, u32[]{:S(2)}) collective-permute-start(f32[512,128]{1,0:T(8,128)S(1)} %bitcast.9), channel_id=1, source_target_pairs={{0,32},{32,0},{1,33},{33,1},{2,34},{34,2},{3,35},{35,3},{4,36},{36... | collective-permute-start | bytes 786440 | tf_op jit(solution)/shard_map/ppermute | solution.py:373

commit v5 on v4

v5 whole, which is shorter than its diff:
```python
import jax
import jax.numpy as jnp
from jax import lax
from jax.experimental import pallas as pl
from jax.experimental.pallas import tpu as pltpu
from jax.sharding import PartitionSpec as P

MEMBERS, TILES, COLS, LINES = 16, 32, 28, 4
DEVICES = MEMBERS * TILES
ROWS = 32
LANES = 128
BLOCKS = DEVICES // LANES
GROUPS = LINES * BLOCKS
WIDTH = LINES * DEVICES
CHIPS, HALF = DEVICES // 2, WIDTH // 2
NEAR = 8
SCALARS = tuple(line * ROWS + COLS + 2 for line in range(LINES)) + (COLS + 3,)
VMEM = pl.BlockSpec(memory_space=pltpu.VMEM)
HBM = pl.BlockSpec(memory_space=pltpu.HBM)


def lane_block(line, block):
    start = (block // 2) * HALF + line * CHIPS + (block % 2) * LANES
    return slice(start, start + LANES)


def pack(core, y, ensemble_hbm, decay_hbm, innovation_hbm, weight_hbm, out_ref,
         ensemble_ref, decay_ref, innovation_ref, weight_ref, rows_ref, sems):
    pairs = (
        (ensemble_hbm, ensemble_ref), (weight_hbm, weight_ref), (decay_hbm, decay_ref), (innovation_hbm, innovation_ref)
    )
    copies = [pltpu.make_async_copy(*pair, sems.at[i]) for i, pair in enumerate(pairs)]
    for copy in copies:
        copy.start()
    for copy in copies:
        copy.wait()
    rows_ref[:COLS, :] = ensemble_ref[0].astype(jnp.float32) * jnp.sqrt(weight_ref[...])
    start = pl.multiple_of(8 * jnp.minimum(lax.div(y, 2), 2), 8)

    def four(ref):
        eight = ref[pl.ds(start, 8), :]
        inner = jnp.where(lax.rem(y, 2) == 0, eight[:4], eight[4:])
        return jnp.where(y >= 6, ref[COLS - 4 :, :], inner)

    scaled = jnp.sqrt(four(weight_ref)) * four(innovation_ref)
    rates = four(decay_ref)
    for owner in range(2):
        part = slice(owner * HALF, (owner + 1) * HALF)
        rows_ref[COLS:, part] = jnp.where(core == owner, rates[:, part], scaled[:, part])
    for block in range(BLOCKS):
        piece = jnp.concatenate([rows_ref[:, lane_block(line, block)] for line in range(LINES)], axis=0)
        to = pl.ds((block % 2) * 2 * LANES + block // 2, LANES, stride=2)
        out_ref[to, :] = piece.T


def spread(piece, lane_group):
    turned = [piece] + [pltpu.roll(piece, 32 * k, 1) for k in (1, 2, 3)]
    out = []
    for source in range(4):
        value = turned[(3 - source) % 4]
        for group in (2, 1, 0):
            value = jnp.where(lane_group == group, turned[(group - source) % 4], value)
        out.append(value)
    return out


RATE, SQUARED, AFTER, UPTO, INNOV, Z0, Z1 = range(7)
FAR = TILES // NEAR - 1


def places():
    lane = lax.broadcasted_iota(jnp.int32, (8, LANES), 1)
    sub = lax.broadcasted_iota(jnp.int32, (8, LANES), 0)
    return lane % TILES, lane // TILES, sub < 4


def arrived(core, in_ref, rows_ref, members_ref, keep_field):
    for j in range(2):
        pieces = [in_ref[pl.ds(2 * j * LANES + owner, LANES, stride=2), :] for owner in range(2)]
        rows_ref[j * LANES : (j + 1) * LANES, :] = jnp.where(core == 0, *pieces).T
    for c in range(COLS):
        members_ref[c] = rows_ref[pl.ds(c, 8, stride=ROWS), :]
    _, lane_group, low = places()
    for j in range(4):
        value = rows_ref[pl.ds(COLS + j, 8, stride=ROWS), :]
        other = pltpu.roll(value, 4, 0)
        for half, both in enumerate((jnp.where(low, value, other), jnp.where(low, other, value))):
            for source, copied in enumerate(spread(both, lane_group)):
                c = 16 * half + 4 * source + j
                if c < COLS:
                    keep_field(c, copied)


def turn(value, k, backward):
    return pltpu.roll(value, LANES - k if backward else k, 1)


def own_first(core, in_ref, members_ref, rates_ref, factors_ref, rows_ref):
    def keep_rate(c, value):
        rates_ref[RATE, c] = value

    arrived(core, in_ref, rows_ref, members_ref, keep_rate)
    tile, _, _ = places()
    one = jnp.ones((8, LANES), jnp.float32)
    upto, after = one, one
    for c in range(COLS):
        rate = rates_ref[RATE, c]
        rates_ref[SQUARED, c] = (1.0 - rate) * (1.0 + rate)
        upto = upto * rate
        rates_ref[UPTO, c] = upto
        rates_ref[AFTER, COLS - 1 - c] = after
        after = after * rates_ref[RATE, COLS - 1 - c]

    for backward in (True, False):

        def inside(k):
            return tile < TILES - k if backward else tile >= k

        product = one
        for k in range(1, NEAR + 1):
            factors_ref[int(backward), k - 1] = jnp.where(inside(k), product, 0.0)
            product = product * turn(upto, k, backward)
        stride = jnp.where(inside(NEAR), product, 0.0)
        product = stride
        for i in range(FAR):
            factors_ref[int(backward), NEAR + i] = jnp.where(inside(NEAR * (i + 1)), product, 0.0)
            product = stride * turn(product, NEAR, backward)


def own_lines(core, in_ref, own_members_ref, rates_ref, factors_ref, out_ref,
              rows_ref, other_members_ref, fields_ref, state_ref, first_ref):
    def keep_innovation(c, value):
        fields_ref[INNOV - INNOV, c] = value

    arrived(core, in_ref, rows_ref, other_members_ref, keep_innovation)
    members = (own_members_ref, other_members_ref)
    zero = jnp.zeros((8, LANES), jnp.float32)

    def field(kind, c):
        return rates_ref[kind, c] if kind < INNOV else fields_ref[kind - INNOV, c]

    def entering(values, backward):
        out = []
        for value in values:
            for steps in (range(1, NEAR + 1), range(NEAR, TILES, NEAR)):
                at = 0 if steps.step == 1 else NEAR
                terms = [factors_ref[int(backward), at + i] * turn(value, k, backward) for i, k in enumerate(steps)]
                if steps.step > 1:
                    terms.append(value)
                while len(terms) > 1:
                    terms = [sum(terms[i : i + 2]) for i in range(0, len(terms), 2)]
                value = terms[0]
            out.append(value)
        return out

    def apply(source, target, on_state, on_field):
        carry = [zero, zero]
        for c in reversed(range(COLS)):
            rate, weight = field(RATE, c), field(source, c)
            for i in range(2):
                summed = members[i][c] * weight + carry[i]
                state_ref[c, i] = summed
                carry[i] = rate * summed
        from_right = entering(carry, True)
        state = [zero, zero]
        for c in range(COLS):
            rate, squared, after = field(RATE, c), field(SQUARED, c), field(AFTER, c)
            for i in range(2):
                summed = state_ref[c, i] + after * from_right[i]
                driven = squared * summed
                on_state(c, i, summed, driven)
                state[i] = rate * state[i] + driven
                state_ref[c, i] = state[i]
        from_left = entering(state, False)
        for c in reversed(range(COLS)):
            upto = field(UPTO, c)
            total = sum(members[i][c] * (state_ref[c, i] + upto * from_left[i]) for i in range(2))
            total = total + pltpu.roll(total, 4, 0)
            total = total + pltpu.roll(total, 64, 1)
            total = total + pltpu.roll(total, 32, 1)
            fields_ref[target - INNOV, c] = total
            on_field(c, total)
        return from_right

    def whole(value):
        return jnp.sum(jnp.sum(value, axis=0, keepdims=True), axis=1, keepdims=True)

    sums = {name: zero for name in ("alpha", "beta", "kappa", "energy", "cross")}

    def keep(c, i, summed, driven):
        first_ref[c, i] = summed
        sums["alpha"] += summed * driven

    def square(c, total):
        sums["beta"] += total * total

    right0 = apply(INNOV, Z0, keep, square)
    alpha = whole(sums["alpha"])
    beta = 0.125 * whole(sums["beta"])
    ratio = jnp.where(alpha > 0.0, beta / jnp.where(alpha > 0.0, alpha, 1.0), 0.0)
    ratio = jnp.broadcast_to(ratio, (8, LANES))

    def orthogonal(c, i, summed, driven):
        part = summed - ratio * first_ref[c, i]
        sums["kappa"] += field(SQUARED, c) * part * part

    def put(row, values):
        rows_ref[pl.ds(row, 16, stride=ROWS), :] = jnp.concatenate(values, axis=0)

    def compare(c, total):
        part = total - ratio * field(Z0, c)
        sums["energy"] += part * part
        sums["cross"] += part * field(Z0, c)
        put(c, [field(Z0, c), total])

    put(COLS, right0)
    put(COLS + 1, apply(Z0, Z1, orthogonal, compare))
    scalars = (alpha, beta, whole(sums["kappa"]), 0.125 * whole(sums["energy"]), 0.125 * whole(sums["cross"]))
    row = lax.broadcasted_iota(jnp.int32, (1, LANES), 1)
    last = jnp.zeros((1, LANES), jnp.float32)
    for place, value in zip(SCALARS, scalars):
        last = jnp.where(row == place, value, last)
    last = jnp.broadcast_to(last, (LANES, LANES))
    ours = lax.broadcasted_iota(jnp.int32, (LANES, LANES), 1) % ROWS >= COLS + 2
    for block in range(BLOCKS):
        piece = rows_ref[block * LANES : (block + 1) * LANES, :].T
        to = pl.ds((block % 2) * 2 * LANES + block // 2, LANES, stride=2)
        out_ref[to, :] = jnp.where(ours, last, piece)


def factors_of(at, ensemble_ref, decay_ref, innovation_ref, weight_ref, refs):
    inverse_ref, vector_ref, factor_ref, rate_ref, amplitude_ref = refs
    for g in range(8):
        here = pl.ds(pl.multiple_of(at + g * LANES, LANES), LANES)
        group = pl.ds(g, COLS, stride=8)
        root = jnp.sqrt(weight_ref[:, here])
        inverse_ref[:, g * LANES : (g + 1) * LANES] = 1.0 / root
        factor = ensemble_ref[0, :, here].astype(jnp.float32) * root
        vector_ref[group, :] = factor * (root * innovation_ref[:, here])
        factor_ref[group, :] = factor
        rate = decay_ref[:, here]
        rate_ref[group, :] = rate
        amplitude_ref[group, :] = jnp.sqrt((1.0 - rate) * (1.0 + rate))


def one_half(mine, in_ref, field0_ref, field1_ref, vector0_ref, vector1_ref, scalars_ref,
             inverse_ref, vector_ref, factor_ref, rate_ref, amplitude_ref):
    rows = [None] * 8
    for j in range(2):
        pieces = [in_ref[pl.ds(2 * j * LANES + h, LANES, stride=2), :].T for h in range(2)]
        for line in range(LINES):
            g = 2 * line + j
            part = slice(g * LANES, (g + 1) * LANES)
            z0, z1 = (piece[line * ROWS : line * ROWS + COLS] for piece in pieces)
            inverse = inverse_ref[:, part]
            field0_ref[:, part] = inverse * z0
            field1_ref[:, part] = inverse * z1
            vector1_ref[pl.ds(g, COLS, stride=8), :] = z0
            rows[g] = pieces[mine][line * ROWS + COLS : line * ROWS + COLS + 2]
        for i, place in enumerate(SCALARS):
            scalars_ref[i : i + 1, j * LANES : (j + 1) * LANES] = pieces[0][place : place + 1]
    carry = [jnp.concatenate([row[i : i + 1] for row in rows], axis=0) for i in range(2)]
    for c in reversed(range(COLS)):
        part = slice(8 * c, 8 * c + 8)
        rate, amplitude = rate_ref[part, :], amplitude_ref[part, :]
        for i, value in enumerate((vector_ref[part, :], factor_ref[part, :] * vector1_ref[part, :])):
            summed = value + carry[i]
            carry[i] = rate * summed
            (vector0_ref, vector1_ref)[i][part, :] = amplitude * summed


def prepare(core, in_ref, *refs):
    args, half, other, own = refs[:4], refs[4:9], refs[9:14], refs[14:]
    factors_of(core * HALF, *args, own)
    one_half(0, in_ref, *half, *own)
    factors_of((1 - core) * HALF, *args, other)


def finish(core, in_ref, *refs):
    own, factors = refs[:5], refs[5:10]
    control_hbm, increment_hbm = refs[10:12]
    other = refs[12:17]
    control_ref, increment_ref, sems = refs[17:]
    one_half(1, in_ref, *other, *factors)

    def whole(value):
        return jnp.sum(value, axis=1, keepdims=True)

    def both(i):
        return jnp.concatenate([ref[i : i + 1, :] for ref in (own[4], other[4])], axis=1)

    alphas, betas, kappas, energies, crosses = (both(i) for i in range(5))
    alpha, beta = whole(alphas), whole(betas)
    ratio = beta / alpha
    shift = jnp.where(alphas > 0.0, betas / jnp.where(alphas > 0.0, alphas, 1.0), 0.0) - ratio
    kappa = whole(kappas + alphas * shift * shift)
    energy = whole(energies + shift * (2.0 * crosses + shift * betas))
    step = alpha / (alpha + beta)
    curvature = kappa + energy - step * kappa * (kappa / alpha)
    back = jnp.where(curvature > 0.0, step * kappa / jnp.where(curvature > 0.0, curvature, 1.0), 0.0)
    ahead = step + back * (ratio + step * (kappa / alpha))

    copies = []

    def send(source, target):
        copies.append(pltpu.make_async_copy(source, target, sems.at[len(copies)]))
        copies[-1].start()

    for at, (field0_ref, field1_ref, *_) in ((core, own), (1 - core, other)):
        here = pl.ds(pl.multiple_of(at * HALF, HALF), HALF)
        increment_ref[:, here] = ahead * field0_ref[...] - back * field1_ref[...]
    send(increment_ref, increment_hbm)
    for quarter in range(4):
        for c in range(7 * quarter, 7 * quarter + 7):
            for at, (_, _, vector0_ref, vector1_ref, _) in ((core, own), (1 - core, other)):
                part = slice(8 * c, 8 * c + 8)
                here = pl.ds(pl.multiple_of(c * GROUPS + 8 * at, 8), 8)
                control_ref[here, :] = ahead * vector0_ref[part, :] - back * vector1_ref[part, :]
        part = slice(7 * quarter * GROUPS, (7 * quarter + 7) * GROUPS)
        send(control_ref.at[part, :], control_hbm.at[part, :])
    for copy in copies:
        copy.wait()


def shape(*dims):
    return jax.ShapeDtypeStruct(dims, jnp.float32)


def scratch(*dims):
    return pltpu.VMEM(dims, jnp.float32)


def call(kernel, out_shape, scratch_shapes, in_specs, out_specs):
    return pl.pallas_call(
        kernel,
        out_shape=out_shape,
        in_specs=in_specs,
        out_specs=out_specs,
        scratch_shapes=scratch_shapes,
        compiler_params=pltpu.CompilerParams(vmem_limit_bytes=32 * 1024 * 1024),
    )


def columns(count):
    return (count, COLS, 8, LANES)


def pack_call(core, y, *args):
    return call(
        lambda *refs: pack(core(), y(), *refs),
        shape(DEVICES, LANES),
        [pltpu.VMEM((1, COLS, WIDTH), jnp.bfloat16)]
        + [scratch(COLS, WIDTH)] * 3
        + [scratch(ROWS, WIDTH), pltpu.SemaphoreType.DMA((4,))],
        [HBM] * 4,
        VMEM,
    )(*(pltpu.with_memory_space_constraint(value, pltpu.HBM) for value in args))


def own_call(core, received, other):
    first = call(
        lambda *refs: own_first(core(), *refs),
        (shape(COLS, 8, LANES), shape(*columns(4)), shape(2, NEAR + FAR, 8, LANES)),
        [scratch(2 * LANES, LANES)],
        [VMEM],
        (VMEM,) * 3,
    )(received)
    return call(
        lambda *refs: own_lines(core(), *refs),
        shape(DEVICES, LANES),
        [
            scratch(DEVICES, LANES),
            scratch(COLS, 8, LANES),
            scratch(*columns(3)),
            scratch(COLS, 2, 8, LANES),
            scratch(COLS, 2, 8, LANES),
        ],
        [VMEM] * 4,
        VMEM,
    )(other, *first)


BY_COLUMN = (COLS * 8, LANES)
RESULTS = ((COLS, HALF), (COLS, HALF), BY_COLUMN, BY_COLUMN, (8, CHIPS))
FACTORS = ((COLS, HALF), BY_COLUMN, BY_COLUMN, BY_COLUMN, BY_COLUMN)


def prepare_call(core, returned, *args):
    return call(
        lambda *refs: prepare(core(), *refs),
        tuple(shape(*dims) for dims in RESULTS + FACTORS),
        [scratch(*dims) for dims in FACTORS],
        [VMEM] * 5,
        (VMEM,) * 10,
    )(returned, *args)


def finish_call(core, other, prepared):
    return call(
        lambda *refs: finish(core(), *refs),
        (shape(COLS * GROUPS, LANES), shape(COLS, WIDTH)),
        [scratch(*dims) for dims in RESULTS]
        + [scratch(COLS * GROUPS, LANES), scratch(COLS, WIDTH), pltpu.SemaphoreType.DMA((5,))],
        [VMEM] * 11,
        (HBM, HBM),
    )(other, *prepared)


def on_device(ensemble, decay_rate, innovation, obs_weight):
    args = (ensemble, decay_rate, innovation, obs_weight)
    core, y = (lambda: lax.axis_index("core")), (lambda: lax.axis_index("y"))

    def among_chips(value):
        pieces = value.reshape(CHIPS, 2, LANES)
        return lax.all_to_all(pieces, ("y", "space"), 0, 0, tiled=True).reshape(DEVICES, LANES)

    def swap(value):
        return lax.ppermute(value, "core", [(0, 1), (1, 0)])

    received = among_chips(pack_call(core, y, *args))
    returned = among_chips(own_call(core, received, swap(received)))
    control, increment = finish_call(core, swap(returned), prepare_call(core, returned, *args))
    return control.reshape(1, COLS, WIDTH), increment


def solution(mesh):
    chips = jax.sharding.Mesh(mesh.devices.reshape(MEMBERS // 2, 2, TILES), ("y", "core", "space"))
    split = P(("y", "core"), "space", None)
    in_specs = (split, P("space", None), P("space", None), P("space", None))
    return jax.shard_map(
        on_device, mesh=chips, in_specs=in_specs, out_specs=(split, P("space", None)), check_vma=False
    )
```

time: 72.4 us -> 75.6 us (1.044)
  starting transfers between devices: 4.76 us -> 8.83 us
  blocking collectives: 61.2 us -> 59.3 us
    ppermute x1 -> x2, starting transfers between devices: 4.76 us -> 8.83 us  [swap(): return lax.ppermute(value, 'core', [(0, 1), (1, 0)])]
    all_to_all x2, blocking collectives: 61.2 us -> 59.3 us  [among_chips(): lax.all_to_all(pieces, ('y', 'space'), 0, 0, tiled=True)]
    pallas_call x2 -> x3, Pallas kernels: 3.2 us -> 3.63 us  [the longest x1 1.69 us: own_call(): call(lambda *refs: own_lines(core(), *refs), shape(DEVICES, LANES), [scra...]
  transfers between devices with their start and end apart: 1 -> 2, of which waited for: 1 -> 2; matrix products, arithmetic and copies ran while one was open for 0% -> 0% of each run, Pallas kernels for 0% -> 1%
where the time goes in v5:
time: 75.6 us; the launch traced here: 75.3 us
  blocking collectives  59.3 us (78%)
  starting transfers between devices  8.83 us (12%)
  Pallas kernels  5.13 us (7%)
  waiting for transfers between devices  1.37 us (2%)
    all_to_all x2, blocking collectives, among_chips(): lax.all_to_all(pieces, ('y', 'space'), 0, 0, tiled=True)  59.3 us
    ppermute x2, starting transfers between devices, swap(): return lax.ppermute(value, 'core', [(0, 1), (1, 0)])  8.83 us
    pallas_call x1, Pallas kernels, own_call(): call(lambda *refs: own_lines(core(), *refs), shape(DEVICES, LANES), [scra...  1.69 us
  transfers between devices with their start and end apart: 2, of which 2 were waited for; matrix products, arithmetic and copies ran while one was open for 0% of the time, Pallas kernels for 1%

profile of v5, /device:TPU:1, one launch (start us, length us, event | category | flops | bytes accessed | tf_op | source)
XLA Modules:
  0.0 75.3 jit_solution(11927761102915635936)
XLA Ops:
  0.6 1.4 %shard_map.59 = f32[512,128]{1,0:T(8,128)S(1)} custom-call(bf16[1,28,2048]{2,1,0:T(8,128)(2,1)} %refs_1_.3, f32[28,2048]{1,0:T(8,128)} %refs_2_.3, f32[28,2048]{1,0:T(8,128)} %refs_3_.3, f32[28,2048]{1,0:T(8,128)} %refs_4_.1), custom_call_target="tpu_custom_call" | custom-call | tf_op jit(solution)/shard_map/pallas_call | solution.py:349
  2.1 36.6 %all_to_all.10 = f32[256,2,128]{2,1,0:T(2,128)S(1)} all-to-all(f32[256,2,128]{2,1,0:T(2,128)S(1)} %bitcast.10), channel_id=1, replica_groups=mesh['y'=8,'core'=2,'space'=32] {'y','space'}, dimensions={0} | all-to-all | bytes 524288 | tf_op jit(solution)/shard_map/all_to_all | solution.py:415
  38.6 4.5 %collective-permute-start = (f32[512,128]{1,0:T(8,128)S(1)}, f32[512,128]{1,0:T(8,128)S(1)}, u32[]{:S(2)}, u32[]{:S(2)}) collective-permute-start(f32[512,128]{1,0:T(8,128)S(1)} %bitcast.5), channel_id=1, source_target_pairs={{0,32},{32,0},{1,33},{33,1},{2,34},{34,2},{3,35},{35,3},{4,36},{36... | collective-permute-start | bytes 786440 | tf_op jit(solution)/shard_map/ppermute | solution.py:418
  43.2 0.5 shard_map.60
  43.7 0.6 collective-permute-done.refs_0_
  44.3 0.0 copy-start.2
  44.3 0.0 copy-start.3
  44.3 1.7 %shard_map.61 = f32[512,128]{1,0:T(8,128)S(1)} custom-call(f32[512,128]{1,0:T(8,128)S(1)} %collective-permute-done.refs_0_, f32[28,8,128]{2,1,0:T(8,128)S(1)} %get-tuple-element.17.refs_1_, f32[4,28,8,128]{3,2,1,0:T(8,128)S(1)} %get-tuple-element.18.refs_2_, f32[2,11,8,128]{3,2,1,0:T(8,128)S(1)} %get-tuple-element.19.refs_3_), custom_call_target="tpu_custom_call" | custom-call | tf_op jit(solution)/shard_map/pallas_call | solution.py:368
  46.0 0.0 copy-start
  46.0 0.0 copy-start.1
  46.0 22.7 %all_to_all.11 = f32[256,2,128]{2,1,0:T(2,128)S(1)} all-to-all(f32[256,2,128]{2,1,0:T(2,128)S(1)} %bitcast.9), channel_id=1, replica_groups=mesh['y'=8,'core'=2,'space'=32] {'y','space'}, dimensions={0} | all-to-all | bytes 524288 | tf_op jit(solution)/shard_map/all_to_all | solution.py:415
  68.7 4.3 %collective-permute-start.1 = (f32[512,128]{1,0:T(8,128)S(1)}, f32[512,128]{1,0:T(8,128)S(1)}, u32[]{:S(2)}, u32[]{:S(2)}) collective-permute-start(f32[512,128]{1,0:T(8,128)S(1)} %bitcast.7), channel_id=1, source_target_pairs={{0,32},{32,0},{1,33},{33,1},{2,34},{34,2},{3,35},{35,3},{4,36},{36... | collective-permute-start | bytes 786440 | tf_op jit(solution)/shard_map/ppermute | solution.py:418
  73.1 0.0 copy-done.2
  73.1 0.0 copy-done.3
  73.1 0.0 copy-done
  73.1 0.0 copy-done.1
  73.1 0.4 shard_map.62
  73.5 0.7 collective-permute-done.1.refs_0_
  74.2 1.1 %shard_map.63 = (f32[448,128]{1,0:T(8,128)}, f32[28,2048]{1,0:T(8,128)}) custom-call(f32[512,128]{1,0:T(8,128)S(1)} %collective-permute-done.1.refs_0_, f32[28,1024]{1,0:T(8,128)S(1)} %get-tuple-element.20.refs_1_, f32[28,1024]{1,0:T(8,128)S(1)} %get-tuple-element.21.refs_2_, f32[224,128]{1,0:T(8,128)S(1)} %get-tuple-element.22.refs_3_, ...), custom_call_target="tpu_custom_call" | custom-call | tf_op jit(solution)/shard_map/pallas_call | solution.py:399
Async XLA Ops:
  38.6 5.7 %collective-permute-start = (f32[512,128]{1,0:T(8,128)S(1)}, f32[512,128]{1,0:T(8,128)S(1)}, u32[]{:S(2)}, u32[]{:S(2)}) collective-permute-start(f32[512,128]{1,0:T(8,128)S(1)} %bitcast.5), channel_id=1, source_target_pairs={{0,32},{32,0},{1,33},{33,1},{2,34},{34,2},{3,35},{35,3},{4,36},{36... | collective-permute-start | bytes 786440 | tf_op jit(solution)/shard_map/ppermute | solution.py:418
  44.3 28.8 %copy-start.2 = (f32[28,2048]{1,0:T(8,128)S(1)}, f32[28,2048]{1,0:T(8,128)}, u32[]{:S(2)}) copy-start(f32[28,2048]{1,0:T(8,128)} %refs_4_.1) | copy-start | bytes 688132
  44.3 28.8 %copy-start.3 = (bf16[1,28,2048]{2,1,0:T(8,128)(2,1)S(1)}, bf16[1,28,2048]{2,1,0:T(8,128)(2,1)}, u32[]{:S(2)}) copy-start(bf16[1,28,2048]{2,1,0:T(8,128)(2,1)} %refs_1_.3) | copy-start | bytes 344068
  46.0 27.1 %copy-start = (f32[28,2048]{1,0:T(8,128)S(1)}, f32[28,2048]{1,0:T(8,128)}, u32[]{:S(2)}) copy-start(f32[28,2048]{1,0:T(8,128)} %refs_2_.3) | copy-start | bytes 688132
  46.0 27.1 %copy-start.1 = (f32[28,2048]{1,0:T(8,128)S(1)}, f32[28,2048]{1,0:T(8,128)}, u32[]{:S(2)}) copy-start(f32[28,2048]{1,0:T(8,128)} %refs_3_.3) | copy-start | bytes 688132
  68.7 5.5 %collective-permute-start.1 = (f32[512,128]{1,0:T(8,128)S(1)}, f32[512,128]{1,0:T(8,128)S(1)}, u32[]{:S(2)}, u32[]{:S(2)}) collective-permute-start(f32[512,128]{1,0:T(8,128)S(1)} %bitcast.7), channel_id=1, source_target_pairs={{0,32},{32,0},{1,33},{33,1},{2,34},{34,2},{3,35},{35,3},{4,36},{36... | collective-permute-start | bytes 786440 | tf_op jit(solution)/shard_map/ppermute | solution.py:418

commit v6 on v4

--- a/solution.py
+++ b/solution.py
@@ -14,6 +14,8 @@
 WIDTH = LINES * DEVICES
 CHIPS, HALF = DEVICES // 2, WIDTH // 2
 NEAR = 8
+SEGMENT = 7
+SEGMENTS = [range(start, start + SEGMENT) for start in range(0, COLS, SEGMENT)]
 SCALARS = tuple(line * ROWS + COLS + 2 for line in range(LINES)) + (COLS + 3,)
 VMEM = pl.BlockSpec(memory_space=pltpu.VMEM)
 HBM = pl.BlockSpec(memory_space=pltpu.HBM)
@@ -26,6 +28,8 @@
 
 def pack(place, ensemble_hbm, decay_hbm, innovation_hbm, weight_hbm, out_ref,
          ensemble_ref, decay_ref, innovation_ref, weight_ref, rows_ref, sems):
+    quarter = lax.rem(place, 8)
+    start = pl.multiple_of(8 * jnp.minimum(lax.div(quarter, 2), 2), 8)
     pairs = (
         (ensemble_hbm, ensemble_ref), (weight_hbm, weight_ref), (decay_hbm, decay_ref), (innovation_hbm, innovation_ref)
     )
@@ -35,8 +39,6 @@
     for copy in copies:
         copy.wait()
     rows_ref[:COLS, :] = ensemble_ref[0].astype(jnp.float32) * jnp.sqrt(weight_ref[...])
-    quarter = lax.rem(place, 8)
-    start = pl.multiple_of(8 * jnp.minimum(lax.div(quarter, 2), 2), 8)
 
     def four(ref):
         eight = ref[pl.ds(start, 8), :]
@@ -48,6 +50,16 @@
     for block in range(BLOCKS):
         piece = jnp.concatenate([rows_ref[:, lane_block(line, block)] for line in range(LINES)], axis=0)
         out_ref[block * LANES : (block + 1) * LANES, :] = piece.T
+
+
+def balanced(join, terms):
+    while len(terms) > 1:
+        terms = [join(*terms[i : i + 2]) if i + 1 < len(terms) else terms[i] for i in range(0, len(terms), 2)]
+    return terms[0]
+
+
+def add(x, y):
+    return x + y
 
 
 def spread(piece, lane_group):
@@ -91,14 +103,20 @@
                     if c < COLS:
                         fields_ref[kind, c] = copied
 
-    upto, after = zero + 1.0, zero + 1.0
-    for c in range(COLS):
-        rate = field(RATE, c)
-        fields_ref[SQUARED, c] = (1.0 - rate) * (1.0 + rate)
-        upto = upto * rate
-        fields_ref[UPTO, c] = upto
-        fields_ref[AFTER, COLS - 1 - c] = after
-        after = after * field(RATE, COLS - 1 - c)
+    one = zero + 1.0
+    parts = []
+    for columns in SEGMENTS:
+        upto, after = one, one
+        for c in columns:
+            rate = field(RATE, c)
+            fields_ref[SQUARED, c] = (1.0 - rate) * (1.0 + rate)
+            upto = upto * rate
+            fields_ref[UPTO, c] = upto
+        for c in reversed(columns):
+            fields_ref[AFTER, c] = after
+            after = after * field(RATE, c)
+        parts.append(upto)
+    upto = balanced(lambda x, y: x * y, parts)
 
     def turn(value, k, backward):
         return pltpu.roll(value, LANES - k if backward else k, 1)
@@ -107,7 +125,7 @@
         return tile < TILES - k if backward else tile >= k
 
     def factors(backward):
-        near, product = [], zero + 1.0
+        near, product = [], one
         for k in range(1, NEAR + 1):
             near.append((k, jnp.where(inside(k, backward), product, 0.0)))
             product = product * turn(upto, k, backward)
@@ -124,37 +142,55 @@
         near, far = chains[backward]
         out = []
         for value in values:
-            value = sum(factor * turn(value, k, backward) for k, factor in near)
-            out.append(value + sum(factor * turn(value, k, backward) for k, factor in far))
+            value = balanced(add, [factor * turn(value, k, backward) for k, factor in near])
+            out.append(balanced(add, [value] + [factor * turn(value, k, backward) for k, factor in far]))
         return out
 
+    def through(ends, products, start):
+        states = [start]
+        for end, product in zip(ends, products):
+            states.append(end if states[-1] is None else end + product * states[-1])
+        return states
+
     def apply(source, target, on_state, on_field):
-        carry = [zero, zero]
-        for c in reversed(range(COLS)):
-            rate, weight = field(RATE, c), field(source, c)
+        ends = [[], []]
+        for columns in reversed(SEGMENTS):
+            carry = [None, None]
+            for c in reversed(columns):
+                rate, weight = field(RATE, c), field(source, c)
+                for i in range(2):
+                    summed = members_ref[c, i] * weight
+                    summed = summed if carry[i] is None else summed + carry[i]
+                    state_ref[c, i] = summed
+                    carry[i] = rate * summed
             for i in range(2):
-                summed = members_ref[c, i] * weight + carry[i]
-                state_ref[c, i] = summed
-                carry[i] = rate * summed
-        from_right = entering(carry, True)
-        state = [zero, zero]
-        for c in range(COLS):
-            rate, squared, after = field(RATE, c), field(SQUARED, c), field(AFTER, c)
+                ends[i].append(carry[i])
+        from_right = entering([through(ends[i], parts[::-1], None)[-1] for i in range(2)], True)
+        starts = [through(ends[i], parts[::-1], from_right[i])[:-1][::-1] for i in range(2)]
+        ends = [[], []]
+        for s, columns in enumerate(SEGMENTS):
+            state = [None, None]
+            for c in columns:
+                rate, squared, after = field(RATE, c), field(SQUARED, c), field(AFTER, c)
+                for i in range(2):
+                    summed = state_ref[c, i] + after * starts[i][s]
+                    driven = squared * summed
+                    on_state(c, i, summed, driven)
+                    state[i] = driven if state[i] is None else rate * state[i] + driven
+                    state_ref[c, i] = state[i]
             for i in range(2):
-                summed = state_ref[c, i] + after * from_right[i]
-                driven = squared * summed
-                on_state(c, i, summed, driven)
-                state[i] = rate * state[i] + driven
-                state_ref[c, i] = state[i]
-        from_left = entering(state, False)
-        for c in reversed(range(COLS)):
-            upto = field(UPTO, c)
-            total = sum(members_ref[c, i] * (state_ref[c, i] + upto * from_left[i]) for i in range(2))
-            total = total + pltpu.roll(total, 4, 0)
-            total = total + pltpu.roll(total, 64, 1)
-            total = total + pltpu.roll(total, 32, 1)
-            fields_ref[target, c] = total
-            on_field(c, total)
+                ends[i].append(state[i])
+        from_left = entering([through(ends[i], parts, None)[-1] for i in range(2)], False)
+        starts = [through(ends[i], parts, from_left[i])[:-1] for i in range(2)]
+        for s, columns in reversed(list(enumerate(SEGMENTS))):
+            for c in reversed(columns):
+                upto = field(UPTO, c)
+                total = add(*(members_ref[c, i] * (state_ref[c, i] + upto * starts[i][s]) for i in range(2)))
+                total = total + pltpu.roll(total, 4, 0)
+                total = total + pltpu.roll(total, 64, 1)
+                total = total + pltpu.roll(total, 32, 1)
+                fields_ref[target, c] = total
+                on_field(c, total)
         return from_right
 
     def whole(value):
@@ -203,54 +239,75 @@
         out_ref[to, :] = jnp.where(ours, last, piece)
 
 
-def one_half(at, first, in_ref, ensemble_ref, decay_ref, innovation_ref, weight_ref,
-             field0_ref, field1_ref, vector0_ref, vector1_ref, scalars_ref, rate_ref, amplitude_ref):
-    rows = []
+def factors_of(at, ensemble_ref, decay_ref, innovation_ref, weight_ref, refs):
+    inverse_ref, vector_ref, factor_ref, rate_ref, amplitude_ref, after_ref = refs
+    for g in range(8):
+        here = pl.ds(pl.multiple_of(at + g * LANES, LANES), LANES)
+        group = pl.ds(g, COLS, stride=8)
+        root = jnp.sqrt(weight_ref[:, here])
+        inverse_ref[:, g * LANES : (g + 1) * LANES] = 1.0 / root
+        factor = ensemble_ref[0, :, here].astype(jnp.float32) * root
+        vector_ref[group, :] = factor * (root * innovation_ref[:, here])
+        factor_ref[group, :] = factor
+        rate = decay_ref[:, here]
+        rate_ref[group, :] = rate
+        amplitude_ref[group, :] = jnp.sqrt((1.0 - rate) * (1.0 + rate))
+    for columns in SEGMENTS:
+        after = jnp.ones((8, LANES), jnp.float32)
+        for c in reversed(columns):
+            part = slice(8 * c, 8 * c + 8)
+            after_ref[part, :] = after
+            after = after * rate_ref[part, :]
+
+
+def one_half(core, in_ref, field0_ref, field1_ref, vector0_ref, vector1_ref, scalars_ref,
+             inverse_ref, vector_ref, factor_ref, rate_ref, amplitude_ref, after_ref):
+    rows = [None] * 8
     for j in range(2):
         pieces = [in_ref[pl.ds(2 * j * LANES + h, LANES, stride=2), :].T for h in range(2)]
-        state = jnp.where(first, pieces[0], pieces[1])
         for line in range(LINES):
-            start = line * CHIPS + j * LANES
-            here = pl.ds(pl.multiple_of(at + start, LANES), LANES)
-            part = slice(start, start + LANES)
-            group = pl.ds(2 * line + j, COLS, stride=8)
-            root = jnp.sqrt(weight_ref[:, here])
-            inverse = 1.0 / root
+            g = 2 * line + j
+            part = slice(g * LANES, (g + 1) * LANES)
             z0, z1 = (piece[line * ROWS : line * ROWS + COLS] for piece in pieces)
+            inverse = inverse_ref[:, part]
             field0_ref[:, part] = inverse * z0
             field1_ref[:, part] = inverse * z1
-            factor = ensemble_ref[0, :, here].astype(jnp.float32) * root
-            vector0_ref[group, :] = factor * (root * innovation_ref[:, here])
-            vector1_ref[group, :] = factor * z0
-            rate = decay_ref[:, here]
-            rate_ref[group, :] = rate
-            amplitude_ref[group, :] = jnp.sqrt((1.0 - rate) * (1.0 + rate))
-            rows.append((2 * line + j, state[line * ROWS + COLS : line * ROWS + COLS + 2]))
+            vector1_ref[pl.ds(g, COLS, stride=8), :] = z0
+            states = [piece[line * ROWS + COLS : line * ROWS + COLS + 2] for piece in pieces]
+            rows[g] = jnp.where(core == 0, *states)
         for i, place in enumerate(SCALARS):
             scalars_ref[i : i + 1, j * LANES : (j + 1) * LANES] = pieces[0][place : place + 1]
-    rows = [row for _, row in sorted(rows, key=lambda pair: pair[0])]
-    refs = (vector0_ref, vector1_ref)
-    carry = [jnp.concatenate([row[i : i + 1] for row in rows], axis=0) for i in range(2)]
-    for c in reversed(range(COLS)):
-        part = slice(8 * c, 8 * c + 8)
-        rate, amplitude = rate_ref[part, :], amplitude_ref[part, :]
-        for i, ref in enumerate(refs):
-            summed = ref[part, :] + carry[i]
-            carry[i] = rate * summed
-            ref[part, :] = amplitude * summed
-
-
-def prepare(core, *refs):
-    one_half(core * HALF, core == 0, *refs)
-
-
-def finish(core, in_ref, ensemble_ref, decay_ref, innovation_ref, weight_ref, *refs):
-    own = refs[:5]
-    control_hbm, increment_hbm = refs[5:7]
-    other = refs[7:12]
-    rate_ref, amplitude_ref, control_ref, increment_ref, sems = refs[12:]
-    inputs = (in_ref, ensemble_ref, decay_ref, innovation_ref, weight_ref)
-    one_half((1 - core) * HALF, core == 0, *inputs, *other, rate_ref, amplitude_ref)
+    entering = [jnp.concatenate([row[i : i + 1] for row in rows], axis=0) for i in range(2)]
+    for columns in reversed(SEGMENTS):
+        carry = [None, None]
+        for c in reversed(columns):
+            part = slice(8 * c, 8 * c + 8)
+            for i, value in enumerate((vector_ref[part, :], factor_ref[part, :] * vector1_ref[part, :])):
+                summed = value if carry[i] is None else value + carry[i]
+                carry[i] = rate_ref[part, :] * summed
+                (vector0_ref, vector1_ref)[i][part, :] = summed
+        for c in columns:
+            part = slice(8 * c, 8 * c + 8)
+            for ref, state in zip((vector0_ref, vector1_ref), entering):
+                ref[part, :] = amplitude_ref[part, :] * (ref[part, :] + after_ref[part, :] * state)
+        first = slice(8 * columns[0], 8 * columns[0] + 8)
+        product = rate_ref[first, :] * after_ref[first, :]
+        entering = [end + product * state for end, state in zip(carry, entering)]
+
+
+def prepare(core, in_ref, *refs):
+    args, half, other, own = refs[:4], refs[4:9], refs[9:15], refs[15:]
+    factors_of(core * HALF, *args, own)
+    one_half(core, in_ref, *half, *own)
+    factors_of((1 - core) * HALF, *args, other)
+
+
+def finish(core, in_ref, *refs):
+    own, factors = refs[:5], refs[5:11]
+    control_hbm, increment_hbm = refs[11:13]
+    other = refs[13:18]
+    control_ref, increment_ref, sems = refs[18:]
+    one_half(core, in_ref, *other, *factors)
 
     def whole(value):
         return jnp.sum(value, axis=1, keepdims=True)
@@ -313,12 +370,10 @@
 def pack_call(place, *args):
     return call(
         lambda *refs: pack(place(), *refs),
-        shape(DEVICES, LANES),
-        [pltpu.VMEM((1, COLS, WIDTH), jnp.bfloat16)]
-        + [scratch(COLS, WIDTH)] * 3
-        + [scratch(ROWS, WIDTH), pltpu.SemaphoreType.DMA((4,))],
+        (shape(DEVICES, LANES),) + tuple(jax.ShapeDtypeStruct(value.shape, value.dtype) for value in args),
+        [scratch(ROWS, WIDTH), pltpu.SemaphoreType.DMA((4,))],
         [HBM] * 4,
-        VMEM,
+        (VMEM,) * 5,
     )(*(pltpu.with_memory_space_constraint(value, pltpu.HBM) for value in args))
 
 
@@ -338,40 +393,41 @@
     )(received)
 
 
-HALVES = ((COLS, HALF), (COLS, HALF), (COLS * 8, LANES), (COLS * 8, LANES), (8, CHIPS))
+BY_COLUMN = (COLS * 8, LANES)
+RESULTS = ((COLS, HALF), (COLS, HALF), BY_COLUMN, BY_COLUMN, (8, CHIPS))
+FACTORS = ((COLS, HALF), BY_COLUMN, BY_COLUMN, BY_COLUMN, BY_COLUMN, BY_COLUMN)
 
 
 def prepare_call(core, returned, *args):
     return call(
         lambda *refs: prepare(core(), *refs),
-        tuple(shape(*dims) for dims in HALVES),
-        [scratch(COLS * 8, LANES)] * 2,
+        tuple(shape(*dims) for dims in RESULTS + FACTORS),
+        [scratch(*dims) for dims in FACTORS],
         [VMEM] * 5,
-        (VMEM,) * 5,
+        (VMEM,) * 11,
     )(returned, *args)
 
 
-def finish_call(core, other, args, prepared):
+def finish_call(core, other, prepared):
     return call(
         lambda *refs: finish(core(), *refs),
         (shape(COLS * GROUPS, LANES), shape(COLS, WIDTH)),
-        [scratch(*dims) for dims in HALVES]
-        + [scratch(COLS * 8, LANES)] * 2
+        [scratch(*dims) for dims in RESULTS]
         + [scratch(COLS * GROUPS, LANES), scratch(COLS, WIDTH), pltpu.SemaphoreType.DMA((5,))],
-        [VMEM] * 10,
+        [VMEM] * 12,
         (HBM, HBM),
-    )(other, *args, *prepared)
+    )(other, *prepared)
 
 
 def on_device(ensemble, decay_rate, innovation, obs_weight):
     args = (ensemble, decay_rate, innovation, obs_weight)
     core = lambda: lax.axis_index("core")
-    sent = pack_call(lambda: 8 * lax.axis_index("core") + lax.axis_index("y"), *args)
+    sent, *args = pack_call(lambda: 8 * lax.axis_index("core") + lax.axis_index("y"), *args)
     received = lax.all_to_all(sent, ("core", "y", "space"), 0, 0, tiled=True)
     results = own_call(received).reshape(CHIPS, 2, LANES)
     returned = lax.all_to_all(results, ("y", "space"), 0, 0, tiled=True).reshape(DEVICES, LANES)
     other = lax.ppermute(returned, "core", [(0, 1), (1, 0)])
-    control, increment = finish_call(core, other, args, prepare_call(core, returned, *args))
+    control, increment = finish_call(core, other, prepare_call(core, returned, *args))
     return control.reshape(1, COLS, WIDTH), increment
 
 

time: 72.4 us -> 72.2 us (level)
  transfers between devices with their start and end apart: 1 -> 1, of which waited for: 1 -> 1; matrix products, arithmetic and copies ran while one was open for 0% -> 0% of each run, Pallas kernels for 0% -> 1%
where the time goes in v6:
time: 72.2 us; the launch traced here: 71.9 us
  blocking collectives  61.1 us (85%)
  starting transfers between devices  4.76 us (7%)
  Pallas kernels  4.69 us (6%)
    all_to_all x1, blocking collectives, on_device(): received = lax.all_to_all(sent, ('core', 'y', 'space'), 0, 0, tiled=True)  38.7 us
    all_to_all x1, blocking collectives, on_device(): lax.all_to_all(results, ('y', 'space'), 0, 0, tiled=True)  22.4 us
    ppermute x1, starting transfers between devices, on_device(): other = lax.ppermute(returned, 'core', [(0, 1), (1, 0)])  4.76 us
    pallas_call x1, Pallas kernels, own_call(): call(own_lines, shape(DEVICES, LANES), [scratch(DEVICES, LANES), scratch(...  1.67 us
    pallas_call x1, Pallas kernels, pack_call(): call(lambda *refs: pack(place(), *refs), (shape(DEVICES, LANES),) + tuple...  1.45 us
  transfers between devices with their start and end apart: 1, of which 1 were waited for; matrix products, arithmetic and copies ran while one was open for 0% of the time, Pallas kernels for 1%

profile of v6, /device:TPU:1, one launch (start us, length us, event | category | flops | bytes accessed | tf_op | source)
XLA Modules:
  0.0 71.9 jit_solution(6748747324122478099)
XLA Ops:
  0.6 1.4 %shard_map.59 = (f32[512,128]{1,0:T(8,128)S(1)}, bf16[1,28,2048]{2,1,0:T(8,128)(2,1)S(1)}, f32[28,2048]{1,0:T(8,128)S(1)}, f32[28,2048]{1,0:T(8,128)S(1)}, f32[28,2048]{1,0:T(8,128)S(1)}) custom-call(bf16[1,28,2048]{2,1,0:T(8,128)(2,1)} %refs_0_.1, f32[28,2048]{1,0:T(8,128)} %refs_1_.1, f32[28,2048]{1,0:T(8,128)} %refs_2_.1, f32[28,2048]{1,0:T(8,128)} %refs_3_.1), custom_call_target="tpu_custom_call" | custom-call | tf_op jit(solution)/shard_map/pallas_call | solution.py:371
  2.1 38.7 %all_to_all.16 = f32[512,1,128]{2,1,0:T(1,128)S(1)} all-to-all(f32[512,1,128]{2,1,0:T(1,128)S(1)} %bitcast.11), channel_id=1, replica_groups=mesh['y'=8,'core'=2,'space'=32] {'core','y','space'}, dimensions={0} | all-to-all | bytes 524288 | tf_op jit(solution)/shard_map/all_to_all | solution.py:426
  40.8 1.7 %shard_map.60 = f32[512,128]{1,0:T(8,128)S(1)} custom-call(f32[512,128]{1,0:T(8,128)S(1)} %bitcast.7), custom_call_target="tpu_custom_call" | custom-call | tf_op jit(solution)/shard_map/pallas_call | solution.py:381
  42.4 22.4 %all_to_all.17 = f32[256,2,128]{2,1,0:T(2,128)S(1)} all-to-all(f32[256,2,128]{2,1,0:T(2,128)S(1)} %bitcast.8), channel_id=1, replica_groups=mesh['y'=8,'core'=2,'space'=32] {'y','space'}, dimensions={0} | all-to-all | bytes 524288 | tf_op jit(solution)/shard_map/all_to_all | solution.py:428
  64.9 4.8 %collective-permute-start = (f32[512,128]{1,0:T(8,128)S(1)}, f32[512,128]{1,0:T(8,128)S(1)}, u32[]{:S(2)}, u32[]{:S(2)}) collective-permute-start(f32[512,128]{1,0:T(8,128)S(1)} %bitcast.9), channel_id=1, source_target_pairs={{0,32},{32,0},{1,33},{33,1},{2,34},{34,2},{3,35},{35,3},{4,36},{36... | collective-permute-start | bytes 786440 | tf_op jit(solution)/shard_map/ppermute | solution.py:429
  69.6 0.4 shard_map.61
  70.1 0.7 %collective-permute-done.refs_0_ = f32[512,128]{1,0:T(8,128)S(1)} collective-permute-done((f32[512,128]{1,0:T(8,128)S(1)}, f32[512,128]{1,0:T(8,128)S(1)}, u32[]{:S(2)}, u32[]{:S(2)}) %collective-permute-start) | collective-permute-done | bytes 262176 | tf_op jit(solution)/shard_map/ppermute | solution.py:429
  70.8 1.2 %shard_map.62 = (f32[448,128]{1,0:T(8,128)}, f32[28,2048]{1,0:T(8,128)}) custom-call(f32[512,128]{1,0:T(8,128)S(1)} %collective-permute-done.refs_0_, f32[28,1024]{1,0:T(8,128)S(1)} %get-tuple-element.25.refs_1_, f32[28,1024]{1,0:T(8,128)S(1)} %get-tuple-element.26.refs_2_, f32[224,128]{1,0:T(8,128)S(1)} %get-tuple-element.27.refs_3_, ...), custom_call_target="tpu_custom_call" | custom-call | tf_op jit(solution)/shard_map/pallas_call | solution.py:412
Async XLA Ops:
  64.9 5.9 %collective-permute-start = (f32[512,128]{1,0:T(8,128)S(1)}, f32[512,128]{1,0:T(8,128)S(1)}, u32[]{:S(2)}, u32[]{:S(2)}) collective-permute-start(f32[512,128]{1,0:T(8,128)S(1)} %bitcast.9), channel_id=1, source_target_pairs={{0,32},{32,0},{1,33},{33,1},{2,34},{34,2},{3,35},{35,3},{4,36},{36... | collective-permute-start | bytes 786440 | tf_op jit(solution)/shard_map/ppermute | solution.py:429

commit v7 on v6

--- a/solution.py
+++ b/solution.py
@@ -13,7 +13,6 @@
 GROUPS = LINES * BLOCKS
 WIDTH = LINES * DEVICES
 CHIPS, HALF = DEVICES // 2, WIDTH // 2
-NEAR = 8
 SEGMENT = 7
 SEGMENTS = [range(start, start + SEGMENT) for start in range(0, COLS, SEGMENT)]
 SCALARS = tuple(line * ROWS + COLS + 2 for line in range(LINES)) + (COLS + 3,)
@@ -27,12 +26,13 @@
 
 
 def pack(place, ensemble_hbm, decay_hbm, innovation_hbm, weight_hbm, out_ref,
-         ensemble_ref, decay_ref, innovation_ref, weight_ref, rows_ref, sems):
+         ensemble_ref, weight_ref, eight_ref, last_ref, rows_ref, sems):
     quarter = lax.rem(place, 8)
     start = pl.multiple_of(8 * jnp.minimum(lax.div(quarter, 2), 2), 8)
-    pairs = (
-        (ensemble_hbm, ensemble_ref), (weight_hbm, weight_ref), (decay_hbm, decay_ref), (innovation_hbm, innovation_ref)
-    )
+    pairs = [(ensemble_hbm, ensemble_ref), (weight_hbm, weight_ref)]
+    for i, hbm in enumerate((decay_hbm, innovation_hbm)):
+        pairs.append((hbm.at[pl.ds(start, 8), :], eight_ref.at[i]))
+        pairs.append((hbm.at[COLS - 4 : COLS, :], last_ref.at[i]))
     copies = [pltpu.make_async_copy(*pair, sems.at[i]) for i, pair in enumerate(pairs)]
     for copy in copies:
         copy.start()
@@ -40,13 +40,12 @@
         copy.wait()
     rows_ref[:COLS, :] = ensemble_ref[0].astype(jnp.float32) * jnp.sqrt(weight_ref[...])
 
-    def four(ref):
-        eight = ref[pl.ds(start, 8), :]
+    def four(eight, last):
         inner = jnp.where(lax.rem(quarter, 2) == 0, eight[:4], eight[4:])
-        return jnp.where(quarter >= 6, ref[COLS - 4 :, :], inner)
-
-    scaled = jnp.sqrt(four(weight_ref)) * four(innovation_ref)
-    rows_ref[COLS:, :] = jnp.where(place < 8, four(decay_ref), scaled)
+        return jnp.where(quarter >= 6, last, inner)
+
+    scaled = jnp.sqrt(four(weight_ref[pl.ds(start, 8), :], weight_ref[COLS - 4 :, :])) * four(eight_ref[1], last_ref[1])
+    rows_ref[COLS:, :] = jnp.where(place < 8, four(eight_ref[0], last_ref[0]), scaled)
     for block in range(BLOCKS):
         piece = jnp.concatenate([rows_ref[:, lane_block(line, block)] for line in range(LINES)], axis=0)
         out_ref[block * LANES : (block + 1) * LANES, :] = piece.T
@@ -125,26 +124,18 @@
         return tile < TILES - k if backward else tile >= k
 
     def factors(backward):
-        near, product = [], one
-        for k in range(1, NEAR + 1):
-            near.append((k, jnp.where(inside(k, backward), product, 0.0)))
+        out, product = [], one
+        for k in range(1, TILES):
+            out.append((k, jnp.where(inside(k, backward), product, 0.0)))
             product = product * turn(upto, k, backward)
-        stride = jnp.where(inside(NEAR, backward), product, 0.0)
-        far, product = [(NEAR, stride)], stride
-        for k in range(2 * NEAR, TILES, NEAR):
-            product = stride * turn(product, NEAR, backward)
-            far.append((k, jnp.where(inside(k, backward), product, 0.0)))
-        return near, far
+        return out
 
     chains = {backward: factors(backward) for backward in (True, False)}
 
     def entering(values, backward):
-        near, far = chains[backward]
-        out = []
-        for value in values:
-            value = balanced(add, [factor * turn(value, k, backward) for k, factor in near])
-            out.append(balanced(add, [value] + [factor * turn(value, k, backward) for k, factor in far]))
-        return out
+        return [
+            balanced(add, [factor * turn(value, k, backward) for k, factor in chains[backward]]) for value in values
+        ]
 
     def through(ends, products, start):
         states = [start]
@@ -370,10 +361,12 @@
 def pack_call(place, *args):
     return call(
         lambda *refs: pack(place(), *refs),
-        (shape(DEVICES, LANES),) + tuple(jax.ShapeDtypeStruct(value.shape, value.dtype) for value in args),
-        [scratch(ROWS, WIDTH), pltpu.SemaphoreType.DMA((4,))],
+        shape(DEVICES, LANES),
+        [pltpu.VMEM((1, COLS, WIDTH), jnp.bfloat16)]
+        + [scratch(COLS, WIDTH), scratch(2, 8, WIDTH), scratch(2, 4, WIDTH)]
+        + [scratch(ROWS, WIDTH), pltpu.SemaphoreType.DMA((6,))],
         [HBM] * 4,
-        (VMEM,) * 5,
+        VMEM,
     )(*(pltpu.with_memory_space_constraint(value, pltpu.HBM) for value in args))
 
 
@@ -422,9 +415,9 @@
 def on_device(ensemble, decay_rate, innovation, obs_weight):
     args = (ensemble, decay_rate, innovation, obs_weight)
     core = lambda: lax.axis_index("core")
-    sent, *args = pack_call(lambda: 8 * lax.axis_index("core") + lax.axis_index("y"), *args)
+    sent = pack_call(lambda: 8 * lax.axis_index("core") + lax.axis_index("y"), *args)
     received = lax.all_to_all(sent, ("core", "y", "space"), 0, 0, tiled=True)
-    results = own_call(received).reshape(CHIPS, 2, LANES)
+    results = own_call(received).reshape(CHIPS, 2 * LANES)
     returned = lax.all_to_all(results, ("y", "space"), 0, 0, tiled=True).reshape(DEVICES, LANES)
     other = lax.ppermute(returned, "core", [(0, 1), (1, 0)])
     control, increment = finish_call(core, other, prepare_call(core, returned, *args))

time: 72.2 us -> 72.1 us (level)
  no operation moved by 1% of the time
where the time goes in v7:
time: 72.1 us; the launch traced here: 71.9 us
  blocking collectives  61.2 us (85%)
  starting transfers between devices  4.76 us (7%)
  Pallas kernels  4.47 us (6%)
    all_to_all x1, blocking collectives, on_device(): received = lax.all_to_all(sent, ('core', 'y', 'space'), 0, 0, tiled=True)  38.7 us
    all_to_all x1, blocking collectives, on_device(): lax.all_to_all(results, ('y', 'space'), 0, 0, tiled=True)  22.6 us
    ppermute x1, starting transfers between devices, on_device(): other = lax.ppermute(returned, 'core', [(0, 1), (1, 0)])  4.76 us
    pallas_call x1, Pallas kernels, own_call(): call(own_lines, shape(DEVICES, LANES), [scratch(DEVICES, LANES), scratch(...  1.59 us
  transfers between devices with their start and end apart: 1, of which 1 were waited for; matrix products, arithmetic and copies ran while one was open for 0% of the time, Pallas kernels for 1%

profile of v7, /device:TPU:1, one launch (start us, length us, event | category | flops | bytes accessed | tf_op | source)
XLA Modules:
  0.0 71.9 jit_solution(3534221187575550897)
XLA Ops:
  0.6 1.3 %shard_map.59 = f32[512,128]{1,0:T(8,128)S(1)} custom-call(bf16[1,28,2048]{2,1,0:T(8,128)(2,1)} %refs_1_.3, f32[28,2048]{1,0:T(8,128)} %refs_2_.3, f32[28,2048]{1,0:T(8,128)} %refs_3_.3, f32[28,2048]{1,0:T(8,128)} %refs_4_.1), custom_call_target="tpu_custom_call" | custom-call | tf_op jit(solution)/shard_map/pallas_call | solution.py:362
  1.9 38.7 %all_to_all.20 = f32[512,1,128]{2,1,0:T(1,128)S(1)} all-to-all(f32[512,1,128]{2,1,0:T(1,128)S(1)} %bitcast.11), channel_id=1, replica_groups=mesh['y'=8,'core'=2,'space'=32] {'core','y','space'}, dimensions={0} | all-to-all | bytes 524288 | tf_op jit(solution)/shard_map/all_to_all | solution.py:419
  40.6 0.0 copy-start.2
  40.6 0.0 copy-start.3
  40.6 1.6 %shard_map.60 = f32[512,128]{1,0:T(8,128)S(1)} custom-call(f32[512,128]{1,0:T(8,128)S(1)} %bitcast.7), custom_call_target="tpu_custom_call" | custom-call | tf_op jit(solution)/shard_map/pallas_call | solution.py:374
  42.2 0.0 copy-start
  42.2 0.0 copy-start.1
  42.2 22.6 %all_to_all.21 = f32[256,1,256]{2,1,0:T(1,128)S(1)} all-to-all(f32[256,1,256]{2,1,0:T(1,128)S(1)} %bitcast.8), channel_id=1, replica_groups=mesh['y'=8,'core'=2,'space'=32] {'y','space'}, dimensions={0} | all-to-all | bytes 524288 | tf_op jit(solution)/shard_map/all_to_all | solution.py:421
  64.8 4.8 %collective-permute-start = (f32[512,128]{1,0:T(8,128)S(1)}, f32[512,128]{1,0:T(8,128)S(1)}, u32[]{:S(2)}, u32[]{:S(2)}) collective-permute-start(f32[512,128]{1,0:T(8,128)S(1)} %bitcast.9), channel_id=1, source_target_pairs={{0,32},{32,0},{1,33},{33,1},{2,34},{34,2},{3,35},{35,3},{4,36},{36... | collective-permute-start | bytes 786440 | tf_op jit(solution)/shard_map/ppermute | solution.py:422
  69.6 0.0 copy-done.2
  69.6 0.0 copy-done.3
  69.6 0.0 copy-done
  69.6 0.0 copy-done.1
  69.6 0.4 shard_map.61
  70.0 0.7 collective-permute-done.refs_0_
  70.7 1.2 %shard_map.62 = (f32[448,128]{1,0:T(8,128)}, f32[28,2048]{1,0:T(8,128)}) custom-call(f32[512,128]{1,0:T(8,128)S(1)} %collective-permute-done.refs_0_, f32[28,1024]{1,0:T(8,128)S(1)} %get-tuple-element.15.refs_1_, f32[28,1024]{1,0:T(8,128)S(1)} %get-tuple-element.16.refs_2_, f32[224,128]{1,0:T(8,128)S(1)} %get-tuple-element.17.refs_3_, ...), custom_call_target="tpu_custom_call" | custom-call | tf_op jit(solution)/shard_map/pallas_call | solution.py:405
Async XLA Ops:
  40.6 29.0 %copy-start.2 = (f32[28,2048]{1,0:T(8,128)S(1)}, f32[28,2048]{1,0:T(8,128)}, u32[]{:S(2)}) copy-start(f32[28,2048]{1,0:T(8,128)} %refs_4_.1) | copy-start | bytes 688132
  40.6 29.0 %copy-start.3 = (bf16[1,28,2048]{2,1,0:T(8,128)(2,1)S(1)}, bf16[1,28,2048]{2,1,0:T(8,128)(2,1)}, u32[]{:S(2)}) copy-start(bf16[1,28,2048]{2,1,0:T(8,128)(2,1)} %refs_1_.3) | copy-start | bytes 344068
  42.2 27.4 %copy-start = (f32[28,2048]{1,0:T(8,128)S(1)}, f32[28,2048]{1,0:T(8,128)}, u32[]{:S(2)}) copy-start(f32[28,2048]{1,0:T(8,128)} %refs_2_.3) | copy-start | bytes 688132
  42.2 27.4 %copy-start.1 = (f32[28,2048]{1,0:T(8,128)S(1)}, f32[28,2048]{1,0:T(8,128)}, u32[]{:S(2)}) copy-start(f32[28,2048]{1,0:T(8,128)} %refs_3_.3) | copy-start | bytes 688132
  64.8 5.9 %collective-permute-start = (f32[512,128]{1,0:T(8,128)S(1)}, f32[512,128]{1,0:T(8,128)S(1)}, u32[]{:S(2)}, u32[]{:S(2)}) collective-permute-start(f32[512,128]{1,0:T(8,128)S(1)} %bitcast.9), channel_id=1, source_target_pairs={{0,32},{32,0},{1,33},{33,1},{2,34},{34,2},{3,35},{35,3},{4,36},{36... | collective-permute-start | bytes 786440 | tf_op jit(solution)/shard_map/ppermute | solution.py:422

commit v8 on v7

--- a/solution.py
+++ b/solution.py
@@ -236,7 +236,7 @@
         here = pl.ds(pl.multiple_of(at + g * LANES, LANES), LANES)
         group = pl.ds(g, COLS, stride=8)
         root = jnp.sqrt(weight_ref[:, here])
-        inverse_ref[:, g * LANES : (g + 1) * LANES] = 1.0 / root
+        inverse_ref[:COLS, g * LANES : (g + 1) * LANES] = 1.0 / root
         factor = ensemble_ref[0, :, here].astype(jnp.float32) * root
         vector_ref[group, :] = factor * (root * innovation_ref[:, here])
         factor_ref[group, :] = factor
@@ -260,9 +260,9 @@
             g = 2 * line + j
             part = slice(g * LANES, (g + 1) * LANES)
             z0, z1 = (piece[line * ROWS : line * ROWS + COLS] for piece in pieces)
-            inverse = inverse_ref[:, part]
-            field0_ref[:, part] = inverse * z0
-            field1_ref[:, part] = inverse * z1
+            inverse = inverse_ref[:COLS, part]
+            field0_ref[:COLS, part] = inverse * z0
+            field1_ref[:COLS, part] = inverse * z1
             vector1_ref[pl.ds(g, COLS, stride=8), :] = z0
             states = [piece[line * ROWS + COLS : line * ROWS + COLS + 2] for piece in pieces]
             rows[g] = jnp.where(core == 0, *states)
@@ -325,7 +325,7 @@
 
     for at, (field0_ref, field1_ref, *_) in ((core, own), (1 - core, other)):
         here = pl.ds(pl.multiple_of(at * HALF, HALF), HALF)
-        increment_ref[:, here] = ahead * field0_ref[...] - back * field1_ref[...]
+        increment_ref[:, here] = ahead * field0_ref[:COLS, :] - back * field1_ref[:COLS, :]
     send(increment_ref, increment_hbm)
     for quarter in range(4):
         for c in range(7 * quarter, 7 * quarter + 7):
@@ -386,9 +386,9 @@
     )(received)
 
 
-BY_COLUMN = (COLS * 8, LANES)
-RESULTS = ((COLS, HALF), (COLS, HALF), BY_COLUMN, BY_COLUMN, (8, CHIPS))
-FACTORS = ((COLS, HALF), BY_COLUMN, BY_COLUMN, BY_COLUMN, BY_COLUMN, BY_COLUMN)
+BY_COLUMN = (ROWS * 8, LANES)
+RESULTS = ((ROWS, HALF), (ROWS, HALF), BY_COLUMN, BY_COLUMN, (8, CHIPS))
+FACTORS = ((ROWS, HALF), BY_COLUMN, BY_COLUMN, BY_COLUMN, BY_COLUMN, BY_COLUMN)
 
 
 def prepare_call(core, returned, *args):

time: 72.1 us -> 72.1 us (level)
  no operation moved by 1% of the time
where the time goes in v8:
time: 72.1 us; the launch traced here: 71.9 us
  blocking collectives  61.2 us (85%)
  starting transfers between devices  4.76 us (7%)
  Pallas kernels  4.47 us (6%)
    all_to_all x1, blocking collectives, on_device(): received = lax.all_to_all(sent, ('core', 'y', 'space'), 0, 0, tiled=True)  38.7 us
    all_to_all x1, blocking collectives, on_device(): lax.all_to_all(results, ('y', 'space'), 0, 0, tiled=True)  22.6 us
    ppermute x1, starting transfers between devices, on_device(): other = lax.ppermute(returned, 'core', [(0, 1), (1, 0)])  4.76 us
    pallas_call x1, Pallas kernels, own_call(): call(own_lines, shape(DEVICES, LANES), [scratch(DEVICES, LANES), scratch(...  1.59 us
  transfers between devices with their start and end apart: 1, of which 1 were waited for; matrix products, arithmetic and copies ran while one was open for 0% of the time, Pallas kernels for 1%

profile of v8, /device:TPU:1, one launch (start us, length us, event | category | flops | bytes accessed | tf_op | source)
XLA Modules:
  0.0 71.9 jit_solution(12699524001035500209)
XLA Ops:
  0.6 1.3 %shard_map.59 = f32[512,128]{1,0:T(8,128)S(1)} custom-call(bf16[1,28,2048]{2,1,0:T(8,128)(2,1)} %refs_1_.3, f32[28,2048]{1,0:T(8,128)} %refs_2_.3, f32[28,2048]{1,0:T(8,128)} %refs_3_.3, f32[28,2048]{1,0:T(8,128)} %refs_4_.1), custom_call_target="tpu_custom_call" | custom-call | tf_op jit(solution)/shard_map/pallas_call | solution.py:362
  1.9 38.7 %all_to_all.20 = f32[512,1,128]{2,1,0:T(1,128)S(1)} all-to-all(f32[512,1,128]{2,1,0:T(1,128)S(1)} %bitcast.11), channel_id=1, replica_groups=mesh['y'=8,'core'=2,'space'=32] {'core','y','space'}, dimensions={0} | all-to-all | bytes 524288 | tf_op jit(solution)/shard_map/all_to_all | solution.py:419
  40.6 0.0 copy-start.2
  40.6 0.0 copy-start.3
  40.6 1.6 %shard_map.60 = f32[512,128]{1,0:T(8,128)S(1)} custom-call(f32[512,128]{1,0:T(8,128)S(1)} %bitcast.7), custom_call_target="tpu_custom_call" | custom-call | tf_op jit(solution)/shard_map/pallas_call | solution.py:374
  42.2 0.0 copy-start
  42.2 0.0 copy-start.1
  42.2 22.6 %all_to_all.21 = f32[256,1,256]{2,1,0:T(1,128)S(1)} all-to-all(f32[256,1,256]{2,1,0:T(1,128)S(1)} %bitcast.8), channel_id=1, replica_groups=mesh['y'=8,'core'=2,'space'=32] {'y','space'}, dimensions={0} | all-to-all | bytes 524288 | tf_op jit(solution)/shard_map/all_to_all | solution.py:421
  64.8 4.8 %collective-permute-start = (f32[512,128]{1,0:T(8,128)S(1)}, f32[512,128]{1,0:T(8,128)S(1)}, u32[]{:S(2)}, u32[]{:S(2)}) collective-permute-start(f32[512,128]{1,0:T(8,128)S(1)} %bitcast.9), channel_id=1, source_target_pairs={{0,32},{32,0},{1,33},{33,1},{2,34},{34,2},{3,35},{35,3},{4,36},{36... | collective-permute-start | bytes 786440 | tf_op jit(solution)/shard_map/ppermute | solution.py:422
  69.6 0.0 copy-done.2
  69.6 0.0 copy-done.3
  69.6 0.0 copy-done
  69.6 0.0 copy-done.1
  69.6 0.4 shard_map.61
  70.0 0.7 collective-permute-done.refs_0_
  70.7 1.2 %shard_map.62 = (f32[448,128]{1,0:T(8,128)}, f32[28,2048]{1,0:T(8,128)}) custom-call(f32[512,128]{1,0:T(8,128)S(1)} %collective-permute-done.refs_0_, f32[32,1024]{1,0:T(8,128)S(1)} %get-tuple-element.15.refs_1_, f32[32,1024]{1,0:T(8,128)S(1)} %get-tuple-element.16.refs_2_, f32[256,128]{1,0:T(8,128)S(1)} %get-tuple-element.17.refs_3_, ...), custom_call_target="tpu_custom_call" | custom-call | tf_op jit(solution)/shard_map/pallas_call | solution.py:405
Async XLA Ops:
  40.6 29.0 %copy-start.2 = (f32[28,2048]{1,0:T(8,128)S(1)}, f32[28,2048]{1,0:T(8,128)}, u32[]{:S(2)}) copy-start(f32[28,2048]{1,0:T(8,128)} %refs_4_.1) | copy-start | bytes 688132
  40.6 29.0 %copy-start.3 = (bf16[1,28,2048]{2,1,0:T(8,128)(2,1)S(1)}, bf16[1,28,2048]{2,1,0:T(8,128)(2,1)}, u32[]{:S(2)}) copy-start(bf16[1,28,2048]{2,1,0:T(8,128)(2,1)} %refs_1_.3) | copy-start | bytes 344068
  42.2 27.4 %copy-start = (f32[28,2048]{1,0:T(8,128)S(1)}, f32[28,2048]{1,0:T(8,128)}, u32[]{:S(2)}) copy-start(f32[28,2048]{1,0:T(8,128)} %refs_2_.3) | copy-start | bytes 688132
  42.2 27.4 %copy-start.1 = (f32[28,2048]{1,0:T(8,128)S(1)}, f32[28,2048]{1,0:T(8,128)}, u32[]{:S(2)}) copy-start(f32[28,2048]{1,0:T(8,128)} %refs_3_.3) | copy-start | bytes 688132
  64.8 5.9 %collective-permute-start = (f32[512,128]{1,0:T(8,128)S(1)}, f32[512,128]{1,0:T(8,128)S(1)}, u32[]{:S(2)}, u32[]{:S(2)}) collective-permute-start(f32[512,128]{1,0:T(8,128)S(1)} %bitcast.9), channel_id=1, source_target_pairs={{0,32},{32,0},{1,33},{33,1},{2,34},{34,2},{3,35},{35,3},{4,36},{36... | collective-permute-start | bytes 786440 | tf_op jit(solution)/shard_map/ppermute | solution.py:422

commit v9 on v8

--- a/solution.py
+++ b/solution.py
@@ -6,6 +6,7 @@
 from jax.sharding import PartitionSpec as P
 
 MEMBERS, TILES, COLS, LINES = 16, 32, 28, 4
+XS, ZS = 4, 8
 DEVICES = MEMBERS * TILES
 ROWS = 32
 LANES = 128
@@ -47,8 +48,11 @@
     scaled = jnp.sqrt(four(weight_ref[pl.ds(start, 8), :], weight_ref[COLS - 4 :, :])) * four(eight_ref[1], last_ref[1])
     rows_ref[COLS:, :] = jnp.where(place < 8, four(eight_ref[0], last_ref[0]), scaled)
     for block in range(BLOCKS):
-        piece = jnp.concatenate([rows_ref[:, lane_block(line, block)] for line in range(LINES)], axis=0)
-        out_ref[block * LANES : (block + 1) * LANES, :] = piece.T
+        piece = jnp.concatenate([rows_ref[:, lane_block(line, block)] for line in range(LINES)], axis=0).T
+        for half in range(2):
+            x = 2 * (block % 2) + half
+            to = pl.ds((block // 2) * CHIPS + x, CHIPS // XS, stride=XS)
+            out_ref[to, :] = piece[half * CHIPS // XS : (half + 1) * CHIPS // XS]
 
 
 def balanced(join, terms):
@@ -226,8 +230,12 @@
     ours = lax.broadcasted_iota(jnp.int32, (LANES, LANES), 1) % ROWS >= COLS + 2
     for block in range(BLOCKS):
         piece = rows_ref[block * LANES : (block + 1) * LANES, :].T
-        to = pl.ds((block % 2) * 2 * LANES + block // 2, LANES, stride=2)
-        out_ref[to, :] = jnp.where(ours, last, piece)
+        here = slice(block * LANES, (block + 1) * LANES)
+        rows_ref[here, :] = jnp.where(ours, last, piece)
+        for x in range(XS):
+            from_x = rows_ref[pl.ds(block * LANES + x, LANES // XS, stride=XS), :]
+            to = pl.ds(2 * (x * CHIPS // XS + (block % 2) * LANES // XS) + block // 2, LANES // XS, stride=2)
+            out_ref[to, :] = from_x
 
 
 def factors_of(at, ensemble_ref, decay_ref, innovation_ref, weight_ref, refs):
@@ -416,18 +424,17 @@
     args = (ensemble, decay_rate, innovation, obs_weight)
     core = lambda: lax.axis_index("core")
     sent = pack_call(lambda: 8 * lax.axis_index("core") + lax.axis_index("y"), *args)
-    received = lax.all_to_all(sent, ("core", "y", "space"), 0, 0, tiled=True)
+    received = lax.all_to_all(sent, ("core", "y", "z", "x"), 0, 0, tiled=True)
     results = own_call(received).reshape(CHIPS, 2 * LANES)
-    returned = lax.all_to_all(results, ("y", "space"), 0, 0, tiled=True).reshape(DEVICES, LANES)
+    returned = lax.all_to_all(results, ("x", "y", "z"), 0, 0, tiled=True).reshape(DEVICES, LANES)
     other = lax.ppermute(returned, "core", [(0, 1), (1, 0)])
     control, increment = finish_call(core, other, prepare_call(core, returned, *args))
     return control.reshape(1, COLS, WIDTH), increment
 
 
 def solution(mesh):
-    chips = jax.sharding.Mesh(mesh.devices.reshape(MEMBERS // 2, 2, TILES), ("y", "core", "space"))
-    split = P(("y", "core"), "space", None)
-    in_specs = (split, P("space", None), P("space", None), P("space", None))
+    chips = jax.sharding.Mesh(mesh.devices.reshape(MEMBERS // 2, 2, ZS, XS), ("y", "core", "z", "x"))
+    whole, field = P(("y", "core"), ("z", "x"), None), P(("z", "x"), None)
     return jax.shard_map(
-        on_device, mesh=chips, in_specs=in_specs, out_specs=(split, P("space", None)), check_vma=False
+        on_device, mesh=chips, in_specs=(whole, field, field, field), out_specs=(whole, field), check_vma=False
     )

time: 72.1 us -> 71.9 us (level)
  no operation moved by 1% of the time
where the time goes in v9:
time: 71.9 us; the launch traced here: 71.7 us
  blocking collectives  60.9 us (85%)
  starting transfers between devices  4.91 us (7%)
  Pallas kernels  4.47 us (6%)
    all_to_all x1, blocking collectives, on_device(): received = lax.all_to_all(sent, ('core', 'y', 'z', 'x'), 0, 0, tiled=True)  38.7 us
    all_to_all x1, blocking collectives, on_device(): lax.all_to_all(results, ('x', 'y', 'z'), 0, 0, tiled=True)  22.3 us
    ppermute x1, starting transfers between devices, on_device(): other = lax.ppermute(returned, 'core', [(0, 1), (1, 0)])  4.91 us
    pallas_call x1, Pallas kernels, own_call(): call(own_lines, shape(DEVICES, LANES), [scratch(DEVICES, LANES), scratch(...  1.6 us
  transfers between devices with their start and end apart: 1, of which 1 were waited for; matrix products, arithmetic and copies ran while one was open for 0% of the time, Pallas kernels for 1%

profile of v9, /device:TPU:1, one launch (start us, length us, event | category | flops | bytes accessed | tf_op | source)
XLA Modules:
  0.0 71.7 jit_solution(3705190358658078783)
XLA Ops:
  0.6 1.3 %shard_map.59 = f32[512,128]{1,0:T(8,128)S(1)} custom-call(bf16[1,28,2048]{2,1,0:T(8,128)(2,1)} %refs_1_.3, f32[28,2048]{1,0:T(8,128)} %refs_2_.3, f32[28,2048]{1,0:T(8,128)} %refs_3_.3, f32[28,2048]{1,0:T(8,128)} %refs_4_.1), custom_call_target="tpu_custom_call" | custom-call | tf_op jit(solution)/shard_map/pallas_call | solution.py:370
  1.9 38.7 %all_to_all.20 = f32[512,1,128]{2,1,0:T(1,128)S(1)} all-to-all(f32[512,1,128]{2,1,0:T(1,128)S(1)} %bitcast.11), channel_id=1, replica_groups=mesh['y'=8,'core'=2,'z'=8,'x'=4] {'core','y','z','x'}, dimensions={0} | all-to-all | bytes 524288 | tf_op jit(solution)/shard_map/all_to_all | solution.py:427
  40.6 0.0 copy-start.2
  40.6 0.0 copy-start.3
  40.6 1.6 %shard_map.60 = f32[512,128]{1,0:T(8,128)S(1)} custom-call(f32[512,128]{1,0:T(8,128)S(1)} %bitcast.7), custom_call_target="tpu_custom_call" | custom-call | tf_op jit(solution)/shard_map/pallas_call | solution.py:382
  42.2 0.0 copy-start
  42.2 0.0 copy-start.1
  42.2 22.3 %all_to_all.21 = f32[256,1,256]{2,1,0:T(1,128)S(1)} all-to-all(f32[256,1,256]{2,1,0:T(1,128)S(1)} %bitcast.8), channel_id=1, replica_groups=mesh['y'=8,'core'=2,'z'=8,'x'=4] {'x','y','z'}, dimensions={0} | all-to-all | bytes 524288 | tf_op jit(solution)/shard_map/all_to_all | solution.py:429
  64.5 4.9 %collective-permute-start = (f32[512,128]{1,0:T(8,128)S(1)}, f32[512,128]{1,0:T(8,128)S(1)}, u32[]{:S(2)}, u32[]{:S(2)}) collective-permute-start(f32[512,128]{1,0:T(8,128)S(1)} %bitcast.9), channel_id=1, source_target_pairs={{0,32},{32,0},{1,33},{33,1},{2,34},{34,2},{3,35},{35,3},{4,36},{36... | collective-permute-start | bytes 786440 | tf_op jit(solution)/shard_map/ppermute | solution.py:430
  69.4 0.0 copy-done.2
  69.4 0.0 copy-done.3
  69.4 0.0 copy-done
  69.4 0.0 copy-done.1
  69.4 0.4 shard_map.61
  69.9 0.7 collective-permute-done.refs_0_
  70.5 1.2 %shard_map.62 = (f32[448,128]{1,0:T(8,128)}, f32[28,2048]{1,0:T(8,128)}) custom-call(f32[512,128]{1,0:T(8,128)S(1)} %collective-permute-done.refs_0_, f32[32,1024]{1,0:T(8,128)S(1)} %get-tuple-element.15.refs_1_, f32[32,1024]{1,0:T(8,128)S(1)} %get-tuple-element.16.refs_2_, f32[256,128]{1,0:T(8,128)S(1)} %get-tuple-element.17.refs_3_, ...), custom_call_target="tpu_custom_call" | custom-call | tf_op jit(solution)/shard_map/pallas_call | solution.py:413
Async XLA Ops:
  40.6 28.8 %copy-start.2 = (f32[28,2048]{1,0:T(8,128)S(1)}, f32[28,2048]{1,0:T(8,128)}, u32[]{:S(2)}) copy-start(f32[28,2048]{1,0:T(8,128)} %refs_4_.1) | copy-start | bytes 688132
  40.6 28.8 %copy-start.3 = (bf16[1,28,2048]{2,1,0:T(8,128)(2,1)S(1)}, bf16[1,28,2048]{2,1,0:T(8,128)(2,1)}, u32[]{:S(2)}) copy-start(bf16[1,28,2048]{2,1,0:T(8,128)(2,1)} %refs_1_.3) | copy-start | bytes 344068
  42.2 27.2 %copy-start = (f32[28,2048]{1,0:T(8,128)S(1)}, f32[28,2048]{1,0:T(8,128)}, u32[]{:S(2)}) copy-start(f32[28,2048]{1,0:T(8,128)} %refs_2_.3) | copy-start | bytes 688132
  42.2 27.2 %copy-start.1 = (f32[28,2048]{1,0:T(8,128)S(1)}, f32[28,2048]{1,0:T(8,128)}, u32[]{:S(2)}) copy-start(f32[28,2048]{1,0:T(8,128)} %refs_3_.3) | copy-start | bytes 688132
  64.5 6.1 %collective-permute-start = (f32[512,128]{1,0:T(8,128)S(1)}, f32[512,128]{1,0:T(8,128)S(1)}, u32[]{:S(2)}, u32[]{:S(2)}) collective-permute-start(f32[512,128]{1,0:T(8,128)S(1)} %bitcast.9), channel_id=1, source_target_pairs={{0,32},{32,0},{1,33},{33,1},{2,34},{34,2},{3,35},{35,3},{4,36},{36... | collective-permute-start | bytes 786440 | tf_op jit(solution)/shard_map/ppermute | solution.py:430

commit v10 on v9

--- a/solution.py
+++ b/solution.py
@@ -6,7 +6,7 @@
 from jax.sharding import PartitionSpec as P
 
 MEMBERS, TILES, COLS, LINES = 16, 32, 28, 4
-XS, ZS = 4, 8
+XS, YS, ZS = 4, 8, 8
 DEVICES = MEMBERS * TILES
 ROWS = 32
 LANES = 128
@@ -51,8 +51,10 @@
         piece = jnp.concatenate([rows_ref[:, lane_block(line, block)] for line in range(LINES)], axis=0).T
         for half in range(2):
             x = 2 * (block % 2) + half
-            to = pl.ds((block // 2) * CHIPS + x, CHIPS // XS, stride=XS)
-            out_ref[to, :] = piece[half * CHIPS // XS : (half + 1) * CHIPS // XS]
+            for y in range(YS):
+                to = pl.ds(x * LANES + 2 * y + block // 2, ZS, stride=2 * YS)
+                start = half * YS * ZS + y * ZS
+                out_ref[to, :] = piece[start : start + ZS]
 
 
 def balanced(join, terms):
@@ -78,8 +80,12 @@
 
 def own_lines(in_ref, out_ref, rows_ref, members_ref, fields_ref, state_ref, first_ref):
     for block in range(BLOCKS):
+        for i in range(YS // 2):
+            for x in range(XS):
+                given = in_ref[pl.ds(x * LANES + (block % 2) * YS + 2 * i + block // 2, ZS, stride=2 * YS), :]
+                rows_ref[pl.ds(block * LANES + i * TILES + x, ZS, stride=XS), :] = given
         piece = slice(block * LANES, (block + 1) * LANES)
-        rows_ref[piece, :] = in_ref[piece, :].T
+        rows_ref[piece, :] = rows_ref[piece, :].T
 
     lane = lax.broadcasted_iota(jnp.int32, (8, LANES), 1)
     sub = lax.broadcasted_iota(jnp.int32, (8, LANES), 0)
@@ -424,7 +430,7 @@
     args = (ensemble, decay_rate, innovation, obs_weight)
     core = lambda: lax.axis_index("core")
     sent = pack_call(lambda: 8 * lax.axis_index("core") + lax.axis_index("y"), *args)
-    received = lax.all_to_all(sent, ("core", "y", "z", "x"), 0, 0, tiled=True)
+    received = lax.all_to_all(sent, ("x", "z", "y", "core"), 0, 0, tiled=True)
     results = own_call(received).reshape(CHIPS, 2 * LANES)
     returned = lax.all_to_all(results, ("x", "y", "z"), 0, 0, tiled=True).reshape(DEVICES, LANES)
     other = lax.ppermute(returned, "core", [(0, 1), (1, 0)])

time: 71.9 us -> 72.2 us (level)
  blocking collectives: 60.9 us -> 61.7 us
where the time goes in v10:
time: 72.2 us; the launch traced here: 72 us
  blocking collectives  61.7 us (85%)
  Pallas kernels  4.55 us (6%)
  starting transfers between devices  4.35 us (6%)
    all_to_all x1, blocking collectives, on_device(): received = lax.all_to_all(sent, ('x', 'z', 'y', 'core'), 0, 0, tiled=True)  38.8 us
    all_to_all x1, blocking collectives, on_device(): lax.all_to_all(results, ('x', 'y', 'z'), 0, 0, tiled=True)  22.9 us
    ppermute x1, starting transfers between devices, on_device(): other = lax.ppermute(returned, 'core', [(0, 1), (1, 0)])  4.35 us
    pallas_call x1, Pallas kernels, own_call(): call(own_lines, shape(DEVICES, LANES), [scratch(DEVICES, LANES), scratch(...  1.67 us
  transfers between devices with their start and end apart: 1, of which 1 were waited for; matrix products, arithmetic and copies ran while one was open for 0% of the time, Pallas kernels for 1%

profile of v10, /device:TPU:1, one launch (start us, length us, event | category | flops | bytes accessed | tf_op | source)
XLA Modules:
  0.0 72.0 jit_solution(10939170065463685519)
XLA Ops:
  0.6 1.3 %shard_map.59 = f32[512,128]{1,0:T(8,128)S(1)} custom-call(bf16[1,28,2048]{2,1,0:T(8,128)(2,1)} %refs_1_.3, f32[28,2048]{1,0:T(8,128)} %refs_2_.3, f32[28,2048]{1,0:T(8,128)} %refs_3_.3, f32[28,2048]{1,0:T(8,128)} %refs_4_.1), custom_call_target="tpu_custom_call" | custom-call | tf_op jit(solution)/shard_map/pallas_call | solution.py:376
  1.9 38.8 %all_to_all.20 = f32[512,1,128]{2,1,0:T(1,128)S(1)} all-to-all(f32[512,1,128]{2,1,0:T(1,128)S(1)} %bitcast.11), channel_id=1, replica_groups=mesh['y'=8,'core'=2,'z'=8,'x'=4] {'x','z','y','core'}, dimensions={0} | all-to-all | bytes 524288 | tf_op jit(solution)/shard_map/all_to_all | solution.py:433
  40.7 0.0 copy-start.2
  40.7 0.0 copy-start.3
  40.7 1.7 %shard_map.60 = f32[512,128]{1,0:T(8,128)S(1)} custom-call(f32[512,128]{1,0:T(8,128)S(1)} %bitcast.7), custom_call_target="tpu_custom_call" | custom-call | tf_op jit(solution)/shard_map/pallas_call | solution.py:388
  42.4 0.0 copy-start
  42.4 0.0 copy-start.1
  42.4 22.9 %all_to_all.21 = f32[256,1,256]{2,1,0:T(1,128)S(1)} all-to-all(f32[256,1,256]{2,1,0:T(1,128)S(1)} %bitcast.8), channel_id=1, replica_groups=mesh['y'=8,'core'=2,'z'=8,'x'=4] {'x','y','z'}, dimensions={0} | all-to-all | bytes 524288 | tf_op jit(solution)/shard_map/all_to_all | solution.py:435
  65.3 4.3 %collective-permute-start = (f32[512,128]{1,0:T(8,128)S(1)}, f32[512,128]{1,0:T(8,128)S(1)}, u32[]{:S(2)}, u32[]{:S(2)}) collective-permute-start(f32[512,128]{1,0:T(8,128)S(1)} %bitcast.9), channel_id=1, source_target_pairs={{0,32},{32,0},{1,33},{33,1},{2,34},{34,2},{3,35},{35,3},{4,36},{36... | collective-permute-start | bytes 786440 | tf_op jit(solution)/shard_map/ppermute | solution.py:436
  69.7 0.0 copy-done.2
  69.7 0.0 copy-done.3
  69.7 0.0 copy-done
  69.7 0.0 copy-done.1
  69.7 0.4 shard_map.61
  70.2 0.7 collective-permute-done.refs_0_
  70.8 1.2 %shard_map.62 = (f32[448,128]{1,0:T(8,128)}, f32[28,2048]{1,0:T(8,128)}) custom-call(f32[512,128]{1,0:T(8,128)S(1)} %collective-permute-done.refs_0_, f32[32,1024]{1,0:T(8,128)S(1)} %get-tuple-element.15.refs_1_, f32[32,1024]{1,0:T(8,128)S(1)} %get-tuple-element.16.refs_2_, f32[256,128]{1,0:T(8,128)S(1)} %get-tuple-element.17.refs_3_, ...), custom_call_target="tpu_custom_call" | custom-call | tf_op jit(solution)/shard_map/pallas_call | solution.py:419
Async XLA Ops:
  40.7 29.0 %copy-start.2 = (f32[28,2048]{1,0:T(8,128)S(1)}, f32[28,2048]{1,0:T(8,128)}, u32[]{:S(2)}) copy-start(f32[28,2048]{1,0:T(8,128)} %refs_4_.1) | copy-start | bytes 688132
  40.7 29.0 %copy-start.3 = (bf16[1,28,2048]{2,1,0:T(8,128)(2,1)S(1)}, bf16[1,28,2048]{2,1,0:T(8,128)(2,1)}, u32[]{:S(2)}) copy-start(bf16[1,28,2048]{2,1,0:T(8,128)(2,1)} %refs_1_.3) | copy-start | bytes 344068
  42.4 27.3 %copy-start = (f32[28,2048]{1,0:T(8,128)S(1)}, f32[28,2048]{1,0:T(8,128)}, u32[]{:S(2)}) copy-start(f32[28,2048]{1,0:T(8,128)} %refs_2_.3) | copy-start | bytes 688132
  42.4 27.3 %copy-start.1 = (f32[28,2048]{1,0:T(8,128)S(1)}, f32[28,2048]{1,0:T(8,128)}, u32[]{:S(2)}) copy-start(f32[28,2048]{1,0:T(8,128)} %refs_3_.3) | copy-start | bytes 688132
  65.3 5.5 %collective-permute-start = (f32[512,128]{1,0:T(8,128)S(1)}, f32[512,128]{1,0:T(8,128)S(1)}, u32[]{:S(2)}, u32[]{:S(2)}) collective-permute-start(f32[512,128]{1,0:T(8,128)S(1)} %bitcast.9), channel_id=1, source_target_pairs={{0,32},{32,0},{1,33},{33,1},{2,34},{34,2},{3,35},{35,3},{4,36},{36... | collective-permute-start | bytes 786440 | tf_op jit(solution)/shard_map/ppermute | solution.py:436

commit v11 on v9

--- a/solution.py
+++ b/solution.py
@@ -14,7 +14,7 @@
 GROUPS = LINES * BLOCKS
 WIDTH = LINES * DEVICES
 CHIPS, HALF = DEVICES // 2, WIDTH // 2
-SEGMENT = 7
+SEGMENT = 4
 SEGMENTS = [range(start, start + SEGMENT) for start in range(0, COLS, SEGMENT)]
 SCALARS = tuple(line * ROWS + COLS + 2 for line in range(LINES)) + (COLS + 3,)
 VMEM = pl.BlockSpec(memory_space=pltpu.VMEM)
@@ -221,7 +221,7 @@
 
     put(COLS, right0)
     put(COLS + 1, apply(Z0, Z1, orthogonal, compare))
-    scalars = (alpha, beta, whole(sums["kappa"]), 0.125 * whole(sums["energy"]), 0.125 * whole(sums["cross"]))
+    scalars = (alpha, ratio[:1, :1], whole(sums["kappa"]), 0.125 * whole(sums["energy"]), 0.125 * whole(sums["cross"]))
     row = lax.broadcasted_iota(jnp.int32, (1, LANES), 1)
     last = jnp.zeros((1, LANES), jnp.float32)
     for place, value in zip(SCALARS, scalars):
@@ -314,16 +314,18 @@
     def both(i):
         return jnp.concatenate([ref[i : i + 1, :] for ref in (own[4], other[4])], axis=1)
 
-    alphas, betas, kappas, energies, crosses = (both(i) for i in range(5))
+    alphas, ratios, kappas, energies, crosses = (both(i) for i in range(5))
+    betas = alphas * ratios
     alpha, beta = whole(alphas), whole(betas)
     ratio = beta / alpha
-    shift = jnp.where(alphas > 0.0, betas / jnp.where(alphas > 0.0, alphas, 1.0), 0.0) - ratio
+    shift = ratios - ratio
     kappa = whole(kappas + alphas * shift * shift)
     energy = whole(energies + shift * (2.0 * crosses + shift * betas))
     step = alpha / (alpha + beta)
-    curvature = kappa + energy - step * kappa * (kappa / alpha)
+    turned = step * (kappa / alpha)
+    curvature = kappa + energy - turned * kappa
     back = jnp.where(curvature > 0.0, step * kappa / jnp.where(curvature > 0.0, curvature, 1.0), 0.0)
-    ahead = step + back * (ratio + step * (kappa / alpha))
+    ahead = step + back * (ratio + turned)
 
     copies = []
 

time: 71.9 us -> 71.9 us (level)
  no operation moved by 1% of the time
where the time goes in v11:
time: 71.9 us; the launch traced here: 71.6 us
  blocking collectives  60.9 us (85%)
  starting transfers between devices  4.91 us (7%)
  Pallas kernels  4.37 us (6%)
    all_to_all x1, blocking collectives, on_device(): received = lax.all_to_all(sent, ('core', 'y', 'z', 'x'), 0, 0, tiled=True)  38.7 us
    all_to_all x1, blocking collectives, on_device(): lax.all_to_all(results, ('x', 'y', 'z'), 0, 0, tiled=True)  22.3 us
    ppermute x1, starting transfers between devices, on_device(): other = lax.ppermute(returned, 'core', [(0, 1), (1, 0)])  4.91 us
    pallas_call x1, Pallas kernels, own_call(): call(own_lines, shape(DEVICES, LANES), [scratch(DEVICES, LANES), scratch(...  1.55 us
  transfers between devices with their start and end apart: 1, of which 1 were waited for; matrix products, arithmetic and copies ran while one was open for 0% of the time, Pallas kernels for 1%

profile of v11, /device:TPU:1, one launch (start us, length us, event | category | flops | bytes accessed | tf_op | source)
XLA Modules:
  0.0 71.6 jit_solution(9837765807967774379)
XLA Ops:
  0.6 1.3 %shard_map.59 = f32[512,128]{1,0:T(8,128)S(1)} custom-call(bf16[1,28,2048]{2,1,0:T(8,128)(2,1)} %refs_1_.3, f32[28,2048]{1,0:T(8,128)} %refs_2_.3, f32[28,2048]{1,0:T(8,128)} %refs_3_.3, f32[28,2048]{1,0:T(8,128)} %refs_4_.1), custom_call_target="tpu_custom_call" | custom-call | tf_op jit(solution)/shard_map/pallas_call | solution.py:372
  1.9 38.7 %all_to_all.20 = f32[512,1,128]{2,1,0:T(1,128)S(1)} all-to-all(f32[512,1,128]{2,1,0:T(1,128)S(1)} %bitcast.11), channel_id=1, replica_groups=mesh['y'=8,'core'=2,'z'=8,'x'=4] {'core','y','z','x'}, dimensions={0} | all-to-all | bytes 524288 | tf_op jit(solution)/shard_map/all_to_all | solution.py:429
  40.6 0.0 copy-start.2
  40.6 0.0 copy-start.3
  40.6 1.5 %shard_map.60 = f32[512,128]{1,0:T(8,128)S(1)} custom-call(f32[512,128]{1,0:T(8,128)S(1)} %bitcast.7), custom_call_target="tpu_custom_call" | custom-call | tf_op jit(solution)/shard_map/pallas_call | solution.py:384
  42.2 0.0 copy-start
  42.2 0.0 copy-start.1
  42.2 22.3 %all_to_all.21 = f32[256,1,256]{2,1,0:T(1,128)S(1)} all-to-all(f32[256,1,256]{2,1,0:T(1,128)S(1)} %bitcast.8), channel_id=1, replica_groups=mesh['y'=8,'core'=2,'z'=8,'x'=4] {'x','y','z'}, dimensions={0} | all-to-all | bytes 524288 | tf_op jit(solution)/shard_map/all_to_all | solution.py:431
  64.4 4.9 %collective-permute-start = (f32[512,128]{1,0:T(8,128)S(1)}, f32[512,128]{1,0:T(8,128)S(1)}, u32[]{:S(2)}, u32[]{:S(2)}) collective-permute-start(f32[512,128]{1,0:T(8,128)S(1)} %bitcast.9), channel_id=1, source_target_pairs={{0,32},{32,0},{1,33},{33,1},{2,34},{34,2},{3,35},{35,3},{4,36},{36... | collective-permute-start | bytes 786440 | tf_op jit(solution)/shard_map/ppermute | solution.py:432
  69.3 0.0 copy-done.2
  69.4 0.0 copy-done.3
  69.4 0.0 copy-done
  69.4 0.0 copy-done.1
  69.4 0.4 shard_map.61
  69.8 0.7 collective-permute-done.refs_0_
  70.5 1.1 %shard_map.62 = (f32[448,128]{1,0:T(8,128)}, f32[28,2048]{1,0:T(8,128)}) custom-call(f32[512,128]{1,0:T(8,128)S(1)} %collective-permute-done.refs_0_, f32[32,1024]{1,0:T(8,128)S(1)} %get-tuple-element.15.refs_1_, f32[32,1024]{1,0:T(8,128)S(1)} %get-tuple-element.16.refs_2_, f32[256,128]{1,0:T(8,128)S(1)} %get-tuple-element.17.refs_3_, ...), custom_call_target="tpu_custom_call" | custom-call | tf_op jit(solution)/shard_map/pallas_call | solution.py:415
Async XLA Ops:
  40.6 28.7 %copy-start.2 = (f32[28,2048]{1,0:T(8,128)S(1)}, f32[28,2048]{1,0:T(8,128)}, u32[]{:S(2)}) copy-start(f32[28,2048]{1,0:T(8,128)} %refs_4_.1) | copy-start | bytes 688132
  40.6 28.8 %copy-start.3 = (bf16[1,28,2048]{2,1,0:T(8,128)(2,1)S(1)}, bf16[1,28,2048]{2,1,0:T(8,128)(2,1)}, u32[]{:S(2)}) copy-start(bf16[1,28,2048]{2,1,0:T(8,128)(2,1)} %refs_1_.3) | copy-start | bytes 344068
  42.2 27.2 %copy-start = (f32[28,2048]{1,0:T(8,128)S(1)}, f32[28,2048]{1,0:T(8,128)}, u32[]{:S(2)}) copy-start(f32[28,2048]{1,0:T(8,128)} %refs_2_.3) | copy-start | bytes 688132
  42.2 27.2 %copy-start.1 = (f32[28,2048]{1,0:T(8,128)S(1)}, f32[28,2048]{1,0:T(8,128)}, u32[]{:S(2)}) copy-start(f32[28,2048]{1,0:T(8,128)} %refs_3_.3) | copy-start | bytes 688132
  64.4 6.1 %collective-permute-start = (f32[512,128]{1,0:T(8,128)S(1)}, f32[512,128]{1,0:T(8,128)S(1)}, u32[]{:S(2)}, u32[]{:S(2)}) collective-permute-start(f32[512,128]{1,0:T(8,128)S(1)} %bitcast.9), channel_id=1, source_target_pairs={{0,32},{32,0},{1,33},{33,1},{2,34},{34,2},{3,35},{35,3},{4,36},{36... | collective-permute-start | bytes 786440 | tf_op jit(solution)/shard_map/ppermute | solution.py:432

commit v12 on v9

--- a/solution.py
+++ b/solution.py
@@ -331,10 +331,6 @@
         copies.append(pltpu.make_async_copy(source, target, sems.at[len(copies)]))
         copies[-1].start()
 
-    for at, (field0_ref, field1_ref, *_) in ((core, own), (1 - core, other)):
-        here = pl.ds(pl.multiple_of(at * HALF, HALF), HALF)
-        increment_ref[:, here] = ahead * field0_ref[:COLS, :] - back * field1_ref[:COLS, :]
-    send(increment_ref, increment_hbm)
     for quarter in range(4):
         for c in range(7 * quarter, 7 * quarter + 7):
             for at, (_, _, vector0_ref, vector1_ref, _) in ((core, own), (1 - core, other)):
@@ -343,6 +339,10 @@
                 control_ref[here, :] = ahead * vector0_ref[part, :] - back * vector1_ref[part, :]
         part = slice(7 * quarter * GROUPS, (7 * quarter + 7) * GROUPS)
         send(control_ref.at[part, :], control_hbm.at[part, :])
+    for at, (field0_ref, field1_ref, *_) in ((core, own), (1 - core, other)):
+        here = pl.ds(pl.multiple_of(at * HALF, HALF), HALF)
+        increment_ref[:, here] = ahead * field0_ref[:COLS, :] - back * field1_ref[:COLS, :]
+    send(increment_ref, increment_hbm)
     for copy in copies:
         copy.wait()
 

time: 71.9 us -> 72 us (level)
  no operation moved by 1% of the time
where the time goes in v12:
time: 72 us; the launch traced here: 71.7 us
  blocking collectives  60.9 us (85%)
  starting transfers between devices  4.91 us (7%)
  Pallas kernels  4.51 us (6%)
    all_to_all x1, blocking collectives, on_device(): received = lax.all_to_all(sent, ('core', 'y', 'z', 'x'), 0, 0, tiled=True)  38.7 us
    all_to_all x1, blocking collectives, on_device(): lax.all_to_all(results, ('x', 'y', 'z'), 0, 0, tiled=True)  22.3 us
    ppermute x1, starting transfers between devices, on_device(): other = lax.ppermute(returned, 'core', [(0, 1), (1, 0)])  4.91 us
    pallas_call x1, Pallas kernels, own_call(): call(own_lines, shape(DEVICES, LANES), [scratch(DEVICES, LANES), scratch(...  1.6 us
  transfers between devices with their start and end apart: 1, of which 1 were waited for; matrix products, arithmetic and copies ran while one was open for 0% of the time, Pallas kernels for 1%

profile of v12, /device:TPU:1, one launch (start us, length us, event | category | flops | bytes accessed | tf_op | source)
XLA Modules:
  0.0 71.7 jit_solution(18335972447730324123)
XLA Ops:
  0.6 1.3 %shard_map.59 = f32[512,128]{1,0:T(8,128)S(1)} custom-call(bf16[1,28,2048]{2,1,0:T(8,128)(2,1)} %refs_1_.3, f32[28,2048]{1,0:T(8,128)} %refs_2_.3, f32[28,2048]{1,0:T(8,128)} %refs_3_.3, f32[28,2048]{1,0:T(8,128)} %refs_4_.1), custom_call_target="tpu_custom_call" | custom-call | tf_op jit(solution)/shard_map/pallas_call | solution.py:370
  1.9 38.7 %all_to_all.20 = f32[512,1,128]{2,1,0:T(1,128)S(1)} all-to-all(f32[512,1,128]{2,1,0:T(1,128)S(1)} %bitcast.11), channel_id=1, replica_groups=mesh['y'=8,'core'=2,'z'=8,'x'=4] {'core','y','z','x'}, dimensions={0} | all-to-all | bytes 524288 | tf_op jit(solution)/shard_map/all_to_all | solution.py:427
  40.6 0.0 copy-start.2
  40.6 0.0 copy-start.3
  40.6 1.6 %shard_map.60 = f32[512,128]{1,0:T(8,128)S(1)} custom-call(f32[512,128]{1,0:T(8,128)S(1)} %bitcast.7), custom_call_target="tpu_custom_call" | custom-call | tf_op jit(solution)/shard_map/pallas_call | solution.py:382
  42.2 0.0 copy-start
  42.2 0.0 copy-start.1
  42.2 22.3 %all_to_all.21 = f32[256,1,256]{2,1,0:T(1,128)S(1)} all-to-all(f32[256,1,256]{2,1,0:T(1,128)S(1)} %bitcast.8), channel_id=1, replica_groups=mesh['y'=8,'core'=2,'z'=8,'x'=4] {'x','y','z'}, dimensions={0} | all-to-all | bytes 524288 | tf_op jit(solution)/shard_map/all_to_all | solution.py:429
  64.5 4.9 %collective-permute-start = (f32[512,128]{1,0:T(8,128)S(1)}, f32[512,128]{1,0:T(8,128)S(1)}, u32[]{:S(2)}, u32[]{:S(2)}) collective-permute-start(f32[512,128]{1,0:T(8,128)S(1)} %bitcast.9), channel_id=1, source_target_pairs={{0,32},{32,0},{1,33},{33,1},{2,34},{34,2},{3,35},{35,3},{4,36},{36... | collective-permute-start | bytes 786440 | tf_op jit(solution)/shard_map/ppermute | solution.py:430
  69.4 0.0 copy-done.2
  69.4 0.0 copy-done.3
  69.4 0.0 copy-done
  69.4 0.0 copy-done.1
  69.4 0.4 shard_map.61
  69.9 0.7 collective-permute-done.refs_0_
  70.5 1.2 %shard_map.62 = (f32[448,128]{1,0:T(8,128)}, f32[28,2048]{1,0:T(8,128)}) custom-call(f32[512,128]{1,0:T(8,128)S(1)} %collective-permute-done.refs_0_, f32[32,1024]{1,0:T(8,128)S(1)} %get-tuple-element.15.refs_1_, f32[32,1024]{1,0:T(8,128)S(1)} %get-tuple-element.16.refs_2_, f32[256,128]{1,0:T(8,128)S(1)} %get-tuple-element.17.refs_3_, ...), custom_call_target="tpu_custom_call" | custom-call | tf_op jit(solution)/shard_map/pallas_call | solution.py:413
Async XLA Ops:
  40.6 28.8 %copy-start.2 = (f32[28,2048]{1,0:T(8,128)S(1)}, f32[28,2048]{1,0:T(8,128)}, u32[]{:S(2)}) copy-start(f32[28,2048]{1,0:T(8,128)} %refs_4_.1) | copy-start | bytes 688132
  40.6 28.8 %copy-start.3 = (bf16[1,28,2048]{2,1,0:T(8,128)(2,1)S(1)}, bf16[1,28,2048]{2,1,0:T(8,128)(2,1)}, u32[]{:S(2)}) copy-start(bf16[1,28,2048]{2,1,0:T(8,128)(2,1)} %refs_1_.3) | copy-start | bytes 344068
  42.2 27.2 %copy-start = (f32[28,2048]{1,0:T(8,128)S(1)}, f32[28,2048]{1,0:T(8,128)}, u32[]{:S(2)}) copy-start(f32[28,2048]{1,0:T(8,128)} %refs_2_.3) | copy-start | bytes 688132
  42.2 27.2 %copy-start.1 = (f32[28,2048]{1,0:T(8,128)S(1)}, f32[28,2048]{1,0:T(8,128)}, u32[]{:S(2)}) copy-start(f32[28,2048]{1,0:T(8,128)} %refs_3_.3) | copy-start | bytes 688132
  64.5 6.1 %collective-permute-start = (f32[512,128]{1,0:T(8,128)S(1)}, f32[512,128]{1,0:T(8,128)S(1)}, u32[]{:S(2)}, u32[]{:S(2)}) collective-permute-start(f32[512,128]{1,0:T(8,128)S(1)} %bitcast.9), channel_id=1, source_target_pairs={{0,32},{32,0},{1,33},{33,1},{2,34},{34,2},{3,35},{35,3},{4,36},{36... | collective-permute-start | bytes 786440 | tf_op jit(solution)/shard_map/ppermute | solution.py:430
